TPU v7x, 32 devices: a whole 2x2x4 slice. The times are simulated.
32 devices in a mesh: mu: 8 (over y, x, core), aux: 4 (over z).
Axes of the slice: x: 2, y: 2, z: 4, core: 2. Of those that a mesh axis runs over, the one named last changes fastest.
Arguments:
- b_tensor: bfloat16 [64, 512, 512], P('aux', 'mu'), as said below
- density: bfloat16 [512, 512], P('mu'), may hold values from -0.25 to 0.25
- pair_mask: int32 [8, 8], replicated, may hold values from 0 to 1, as said below
- dens_mask: int32 [8, 8], replicated, may hold values from 0 to 1, as said below
Outputs:
- exchange_k: float32 [512, 512], P(('mu', 'aux'))
Inputs may be any that keep to these rules, and one draw needn't show every extreme that they name: `pair_mask`: symmetric, with ones on the diagonal. `dens_mask`: symmetric, with ones on the diagonal. `b_tensor`: symmetric in its last two dimensions.
All inputs are finite; a program needn't handle non-finite values.
Results may differ from a plain program's by a relative error of at most 0.0029.
Values may be sent and summed in bfloat16 or wider, within the bound.
No kernel may reach another device: no remote copies, remote signals or barrier semaphores. Data moves between devices by JAX's collectives and lax.ppermute only.
A program may use at most 128 MiB of HBM per device.

v0:
```python
import jax
import jax.numpy as jnp
from jax import lax
from jax.sharding import PartitionSpec as P


def per_device(b_tensor, density, pair_mask, dens_mask):
    depth = b_tensor.shape[0]
    width = b_tensor.shape[1]
    nbas = b_tensor.shape[2]
    owner = lax.axis_index("mu")
    pair_row = lax.dynamic_slice_in_dim(pair_mask, owner, 1, 0)[0]
    dens_row = lax.dynamic_slice_in_dim(dens_mask, owner, 1, 0)[0]
    pair_cols = jnp.repeat(pair_row, width).astype(jnp.bfloat16)
    dens_cols = jnp.repeat(dens_row, width).astype(jnp.bfloat16)
    kept = b_tensor * pair_cols[None, None, :]
    dens_kept = density * dens_cols[None, :]
    flat_kept = kept.reshape(depth * width, nbas)
    summed = jnp.dot(
        flat_kept,
        lax.all_gather(dens_kept, "mu", axis=0, tiled=True),
        preferred_element_type=jnp.float32,
    )
    half_x = summed.astype(jnp.bfloat16).reshape(depth, width, nbas)
    x_cols = lax.all_to_all(half_x, "mu", split_axis=2, concat_axis=1, tiled=True)
    partner = lax.all_to_all(kept, "mu", split_axis=2, concat_axis=1, tiled=True)
    return lax.psum_scatter(
        jnp.einsum("pms,pns->mn", x_cols, partner, preferred_element_type=jnp.float32),
        ("mu", "aux"),
        scatter_dimension=0,
        tiled=True,
    )


def solution(mesh):
    in_specs = (P("aux", "mu", None), P("mu", None), P(), P())
    out_specs = P(("mu", "aux"), None)
    return jax.shard_map(
        per_device, mesh=mesh, in_specs=in_specs, out_specs=out_specs, check_vma=False
    )
```

profile of v0, /device:TPU:0, one launch (start us, length us, event | category | flops | bytes accessed | tf_op | source)
XLA Modules:
  0.0 217.7 jit_solution(13145009972696608522)
XLA Ops:
  6.5 0.7 convert_bitcast_fusion
  7.2 0.1 broadcast_in_dim.9
  7.3 0.1 convert_element_type.36
  7.4 0.1 broadcast_in_dim.8
  7.5 0.1 convert_element_type.33
  7.6 0.8 broadcast_multiply_fusion.1
  8.4 11.3 %all_gather.3 = bf16[512,512]{1,0:T(8,128)(2,1)S(1)} all-gather(bf16[64,512]{1,0:T(8,128)(2,1)S(1)} %broadcast_multiply_fusion.1), channel_id=1, replica_groups=mesh['mu'=8,'aux'=4] {'mu'}, dimensions={0}, use_global_device_ids=true | all-gather | bytes 589824 | tf_op jit(solution)/shard_map/all_gather | solution.py:21
  19.7 1.3 broadcast_multiply_fusion
  21.0 0.0 copy-start
  21.0 0.7 convolution_convert_fusion
  21.7 0.3 copy-done
  22.0 2.0 copy.11
  24.1 2.7 %reshape.25 = bf16[8,2,32768]{2,1,0:T(2,128)(2,1)} reshape(bf16[512,16,64]{2,1,0:T(8,128)(2,1)S(1)} %bitcast.32) | data formatting | bytes 2097152
  26.7 3.6 %all-to-all-start = ((bf16[8,2,32768]{2,1,0:T(2,128)(2,1)}), bf16[8,2,32768]{2,1,0:T(2,128)(2,1)S(1)}, u32[]{:S(2)}, u32[]{:S(2)}) async-start(bf16[8,2,32768]{2,1,0:T(2,128)(2,1)} %reshape.25), calls=%async_computation | async-start | bytes 2097152 | tf_op jit(solution)/shard_map/all_to_all | solution.py:25
  30.3 3.0 %copy.13 = bf16[16,64,512]{1,0,2:T(8,128)(2,1)S(1)} copy(bf16[16,64,512]{2,1,0:T(8,128)(2,1)} %copy-done) | data formatting | bytes 2097152 | tf_op jit(solution)/shard_map/mul | solution.py:16
  33.3 2.7 %reshape.27 = bf16[8,2,32768]{2,1,0:T(2,128)(2,1)} reshape(bf16[512,16,64]{2,1,0:T(8,128)(2,1)S(1)} %bitcast.33) | data formatting | bytes 2097152
  36.0 9.7 %all-to-all-done = bf16[8,2,32768]{2,1,0:T(2,128)(2,1)S(1)} async-done(((bf16[8,2,32768]{2,1,0:T(2,128)(2,1)}), bf16[8,2,32768]{2,1,0:T(2,128)(2,1)S(1)}, u32[]{:S(2)}, u32[]{:S(2)}) %all-to-all-start) | async-done | bytes 1048608 | tf_op jit(solution)/shard_map/all_to_all | solution.py:25
  45.6 4.2 %all-to-all-start.1 = ((bf16[8,2,32768]{2,1,0:T(2,128)(2,1)}), bf16[8,2,32768]{2,1,0:T(2,128)(2,1)}, u32[]{:S(2)}, u32[]{:S(2)}) async-start(bf16[8,2,32768]{2,1,0:T(2,128)(2,1)} %reshape.27), calls=%async_computation.1 | async-start | bytes 2097152 | tf_op jit(solution)/shard_map/all_to_all | solution.py:26
  49.9 0.0 reduce-scatter.2.cloned.1.call-start
  49.9 1.4 reshape.26
  51.4 2.7 %copy.18 = bf16[16,64,8,64]{1,2,3,0:T(8,128)(2,1)} copy(bf16[16,64,8,64]{1,0,3,2:T(8,128)(2,1)S(1)} %bitcast.34) | data formatting | bytes 2097152 | tf_op jit(solution)/shard_map/all_to_all | solution.py:25
  54.1 3.2 %all_to_all.29 = bf16[16,512,64]{1,2,0:T(8,128)(2,1)S(1)} reshape(bf16[16,8,64,64]{2,1,3,0:T(8,128)(2,1)} %bitcast.35) | data formatting | bytes 2097152 | tf_op jit(solution)/shard_map/all_to_all | solution.py:25
  57.3 8.0 %all-to-all-done.1 = bf16[8,2,32768]{2,1,0:T(2,128)(2,1)} async-done(((bf16[8,2,32768]{2,1,0:T(2,128)(2,1)}), bf16[8,2,32768]{2,1,0:T(2,128)(2,1)}, u32[]{:S(2)}, u32[]{:S(2)}) %all-to-all-start.1) | async-done | bytes 1048608 | tf_op jit(solution)/shard_map/all_to_all | solution.py:26
  65.3 3.1 %reshape.28 = bf16[512,16,64]{2,1,0:T(8,128)(2,1)S(1)} reshape(bf16[8,2,32768]{2,1,0:T(2,128)(2,1)} %all-to-all-done.1) | data formatting | bytes 2097152
  68.4 2.7 %copy.17 = bf16[16,64,8,64]{1,2,3,0:T(8,128)(2,1)} copy(bf16[16,64,8,64]{1,0,3,2:T(8,128)(2,1)S(1)} %bitcast.36) | data formatting | bytes 2097152 | tf_op jit(solution)/shard_map/all_to_all | solution.py:26
  71.1 3.2 %all_to_all.33 = bf16[16,512,64]{1,2,0:T(8,128)(2,1)S(1)} reshape(bf16[16,8,64,64]{2,1,3,0:T(8,128)(2,1)} %bitcast.37) | data formatting | bytes 2097152 | tf_op jit(solution)/shard_map/all_to_all | solution.py:26
  74.3 1.7 convolution_bitcast_fusion
  76.0 0.0 reduce-scatter.2.cloned.1.call-update
  76.0 134.8 %reduce-scatter.2.cloned.1.call-done = f32[16,512]{1,0:T(8,128)} async-done(((f32[512,512]{1,0:T(8,128)}), f32[16,512]{1,0:T(8,128)}) %reduce-scatter.2.cloned.1.call-update) | async-done | bytes 32784 | tf_op jit(solution)/shard_map/reduce_scatter | solution.py:27
Async XLA Ops:
  21.0 1.0 copy-start
  26.7 18.9 %all-to-all-start = ((bf16[8,2,32768]{2,1,0:T(2,128)(2,1)}), bf16[8,2,32768]{2,1,0:T(2,128)(2,1)S(1)}, u32[]{:S(2)}, u32[]{:S(2)}) async-start(bf16[8,2,32768]{2,1,0:T(2,128)(2,1)} %reshape.25), calls=%async_computation | async-start | bytes 2097152 | tf_op jit(solution)/shard_map/all_to_all | solution.py:25
  45.6 19.7 %all-to-all-start.1 = ((bf16[8,2,32768]{2,1,0:T(2,128)(2,1)}), bf16[8,2,32768]{2,1,0:T(2,128)(2,1)}, u32[]{:S(2)}, u32[]{:S(2)}) async-start(bf16[8,2,32768]{2,1,0:T(2,128)(2,1)} %reshape.27), calls=%async_computation.1 | async-start | bytes 2097152 | tf_op jit(solution)/shard_map/all_to_all | solution.py:26
  49.9 161.0 %reduce-scatter.2.cloned.1.call-start = ((), (), s32[]{:S(2)}) async-start(), calls=%async_computation.3 | async-start | bytes 1081344 | tf_op jit(solution)/shard_map/reduce_scatter | solution.py:27
Sparse Core Ops, SparseCore 0:
  76.1 134.6 reduce-scatter.1
where the time goes:
time: 218 us
  waiting for transfers between devices  153 us (70%)
  local copies, waits for them, and re-layouts  27.3 us (13%)
  between operations  13.5 us (6%)
  blocking collectives  11.3 us (5%)
  starting transfers between devices  7.84 us (4%)
  other arithmetic  2.85 us (1%)
  matrix products  2.4 us (1%)
    reduce_scatter x1, waiting for transfers between devices, per_device(): lax.psum_scatter(jnp.einsum('pms,pns->mn', x_cols, partner, preferred_ele...  135 us
    all_gather x1, blocking collectives, per_device(): lax.all_gather(dens_kept, 'mu', axis=0, tiled=True)  11.3 us
    unnamed x6, local copies, waits for them, and re-layouts  10.2 us
    all_to_all x1, waiting for transfers between devices, per_device(): lax.all_to_all(half_x, 'mu', split_axis=2, concat_axis=1, tiled=True)  9.66 us
    all_to_all x1, waiting for transfers between devices, per_device(): lax.all_to_all(kept, 'mu', split_axis=2, concat_axis=1, tiled=True)  8.02 us
    all_to_all x2, local copies, waits for them, and re-layouts, per_device(): lax.all_to_all(half_x, 'mu', split_axis=2, concat_axis=1, tiled=True)  5.89 us
    all_to_all x2, local copies, waits for them, and re-layouts, per_device(): lax.all_to_all(kept, 'mu', split_axis=2, concat_axis=1, tiled=True)  5.89 us
  transfers between devices with their start and end apart: 3, of which 3 were waited for; matrix products, arithmetic and copies ran while one was open for 5% of the time, Pallas kernels for 0%

commit v1 on v0

v1 whole, which is shorter than its diff:
```python
import jax
import jax.numpy as jnp
from jax import lax
from jax.experimental import pallas as pl
from jax.experimental.pallas import tpu as pltpu
from jax.sharding import PartitionSpec as P

BF = jnp.bfloat16
F32 = jnp.float32
BLK = 64
TILE = 2 * BLK
CHIPS = 4
NEXT = {1: 2, 2: 3, 3: 1}


def expand_row(mask_ref, row, size):
    block = lax.broadcasted_iota(jnp.int32, (1, size), 1) // BLK
    line = jnp.zeros((1, size), F32)
    for j in range(size // BLK):
        line = jnp.where(block == j, mask_ref[row, j].astype(F32), line)
    return line.astype(BF)


def pack_kernel(group, b_ref, d_ref, pair_ref, dens_ref, own_ref, *send_refs):
    me = lax.axis_index("mu")
    c = me // 2
    size = b_ref.shape[2]
    pair_line = expand_row(pair_ref, me, size)
    dens = d_ref[...] * expand_row(dens_ref, me, size)
    for p in range(group):
        own_ref[p] = b_ref[c * group + p] * pair_line
    own_ref[group] = dens
    for d in (1, 2, 3):
        send = send_refs[d - 1]
        r = c ^ d
        n = c ^ d ^ NEXT[d]
        for slot, chip in enumerate((c, n)):
            cols = pl.ds(pl.multiple_of(chip * TILE, TILE), TILE)
            block = lax.broadcasted_iota(jnp.int32, (1, TILE), 1) // BLK
            line = jnp.where(block == 0, pair_ref[me, 2 * chip], pair_ref[me, 2 * chip + 1]).astype(F32).astype(BF)
            for p in range(group):
                send[p, :, slot * TILE : (slot + 1) * TILE] = b_ref[r * group + p, :, cols] * line
        half = size // 2
        send[group] = dens[:, :half]
        send[group + 1] = dens[:, half:]


def main_kernel(group, own_ref, mate_ref, r1, r2, r3, q1, q2, q3, e1, e2, e3, keep_ref, t_scr, d_scr, l_scr, x_scr, k_scr):
    me = lax.axis_index("mu")
    c = me // 2
    k = me % 2
    size = t_scr.shape[1]
    half = size // 2

    def rows(chip, core):
        return pl.multiple_of(chip * TILE + core * BLK, BLK)

    def cols(chip):
        return pl.ds(pl.multiple_of(chip * TILE, TILE), TILE)

    for core, own in ((k, own_ref), (1 - k, mate_ref)):
        d_scr[pl.ds(rows(c, core), BLK), :] = own[group]
        for p in range(group):
            t_scr[pl.ds(p * size + rows(c, core), BLK), :] = own[p]
    for d, mine, other in ((1, r1, q1), (2, r2, q2), (3, r3, q3)):
        r = c ^ d
        n = c ^ NEXT[d]
        for core, ref in ((k, mine), (1 - k, other)):
            d_scr[pl.ds(rows(r, core), BLK), :half] = ref[group]
            d_scr[pl.ds(rows(r, core), BLK), half:] = ref[group + 1]
            for p in range(group):
                at = pl.ds(p * size + rows(r, core), BLK)
                t_scr[at, cols(r)] = ref[p, :, :TILE]
                t_scr[at, cols(n)] = ref[p, :, TILE:]
    for d in (1, 2, 3):
        r = c ^ d
        n = c ^ NEXT[d]
        for p in range(group):
            for src, dst in ((c, r), (r, n)):
                block = t_scr[pl.ds(pl.multiple_of(p * size + src * TILE, TILE), TILE), cols(dst)]
                t_scr[pl.ds(pl.multiple_of(p * size + dst * TILE, TILE), TILE), cols(src)] = block.T
    for p in range(group):
        for r in range(CHIPS):
            l_scr[(p * CHIPS + r) * BLK : (p * CHIPS + r + 1) * BLK, :] = t_scr[pl.ds(p * size + rows(r, k), BLK), :]
    for p in range(group):
        x_scr[:, p * size : (p + 1) * size] = jnp.dot(
            l_scr[p * CHIPS * BLK : (p + 1) * CHIPS * BLK, :], d_scr[...], preferred_element_type=F32
        ).astype(BF)
    k_scr[...] = jnp.dot(x_scr[...], t_scr[...], preferred_element_type=F32)
    for d, out in ((1, e1), (2, e2), (3, e3)):
        out[...] = k_scr[pl.ds(pl.multiple_of((c ^ d) * BLK, BLK), BLK), :].astype(BF)
    keep_ref[...] = k_scr[pl.ds(pl.multiple_of(c * BLK, BLK), BLK), :]


def spread(b_tensor, density, pair_mask, dens_mask):
    depth, width, size = b_tensor.shape
    group = depth // CHIPS
    vmem = pl.BlockSpec(memory_space=pltpu.VMEM)
    smem = pl.BlockSpec(memory_space=pltpu.SMEM)

    def swap(x, step):
        return lax.ppermute(x, "mu", [(i, i ^ step) for i in range(2 * CHIPS)])

    piece = jax.ShapeDtypeStruct((group + 2, width, size // 2), BF)
    own, *sends = pl.pallas_call(
        lambda *refs: pack_kernel(group, *refs),
        out_shape=[jax.ShapeDtypeStruct((group + 1, width, size), BF), piece, piece, piece],
        in_specs=[vmem, vmem, smem, smem],
        out_specs=[vmem] * 4,
        compiler_params=pltpu.CompilerParams(vmem_limit_bytes=16 << 20),
        name="pack",
    )(b_tensor, density, pair_mask, dens_mask)
    got = [swap(send, 2 * d) for d, send in zip((1, 2, 3), sends)]
    mate = swap(own, 1)
    others = [swap(g, 1) for g in got]
    chunk = jax.ShapeDtypeStruct((width, size), BF)
    *parts, keep = pl.pallas_call(
        lambda *refs: main_kernel(group, *refs),
        out_shape=[chunk, chunk, chunk, jax.ShapeDtypeStruct((width, size), F32)],
        in_specs=[vmem] * 8,
        out_specs=[vmem] * 4,
        scratch_shapes=[
            pltpu.VMEM((group * size, size), BF),
            pltpu.VMEM((size, size), BF),
            pltpu.VMEM((group * size // 2, size), BF),
            pltpu.VMEM((size // 2, group * size), BF),
            pltpu.VMEM((size // 2, size), F32),
        ],
        compiler_params=pltpu.CompilerParams(vmem_limit_bytes=32 << 20),
        name="exchange",
    )(own, mate, *got, *others)
    plane = keep
    for d, part in zip((1, 2, 3), parts):
        plane = plane + swap(part, 2 * d).astype(F32)
    a = lax.axis_index("aux")
    strip = width // 4

    def strip_of(index):
        return lax.dynamic_slice_in_dim(plane, index * strip, strip, 0)

    total = strip_of(a)
    for d in (1, 2, 3):
        total = total + lax.ppermute(strip_of(a ^ d), "aux", [(i, i ^ d) for i in range(4)])
    return total


def gathered(b_tensor, density, pair_mask, dens_mask):
    depth, width, nbas = b_tensor.shape
    owner = lax.axis_index("mu")
    pair_row = lax.dynamic_slice_in_dim(pair_mask, owner, 1, 0)[0]
    dens_row = lax.dynamic_slice_in_dim(dens_mask, owner, 1, 0)[0]
    kept = b_tensor * jnp.repeat(pair_row, width).astype(BF)[None, None, :]
    dens_kept = density * jnp.repeat(dens_row, width).astype(BF)[None, :]
    summed = jnp.dot(
        kept.reshape(depth * width, nbas),
        lax.all_gather(dens_kept, "mu", axis=0, tiled=True),
        preferred_element_type=F32,
    )
    half_x = summed.astype(BF).reshape(depth, width, nbas)
    x_cols = lax.all_to_all(half_x, "mu", split_axis=2, concat_axis=1, tiled=True)
    partner = lax.all_to_all(kept, "mu", split_axis=2, concat_axis=1, tiled=True)
    return lax.psum_scatter(
        jnp.einsum("pms,pns->mn", x_cols, partner, preferred_element_type=F32),
        ("mu", "aux"),
        scatter_dimension=0,
        tiled=True,
    )


def solution(mesh):
    in_specs = (P("aux", "mu", None), P("mu", None), P(), P())
    out_specs = P(("mu", "aux"), None)

    def per_device(b_tensor, density, pair_mask, dens_mask):
        depth, width, size = b_tensor.shape
        fits = mesh.shape["mu"] == 2 * CHIPS and mesh.shape["aux"] == 4
        fits = fits and depth % CHIPS == 0 and width == BLK and size == 2 * CHIPS * BLK
        step = spread if fits else gathered
        return step(b_tensor, density, pair_mask, dens_mask)

    return jax.shard_map(per_device, mesh=mesh, in_specs=in_specs, out_specs=out_specs, check_vma=False)
```

time: 218 us -> 40.8 us (0.19)
  waiting for transfers between devices: 153 us -> 19.5 us
  local copies, waits for them, and re-layouts: 27.3 us -> 3.45 us
  between operations: 13.5 us -> 0.05 us
  blocking collectives: 11.3 us -> 0 us
  starting transfers between devices: 7.84 us -> 13.1 us
  Pallas kernels: 0 us -> 3.91 us
  matrix products: 2.4 us -> 0 us
  other arithmetic: 2.85 us -> 0.65 us
    reduce_scatter x1 -> x0, waiting for transfers between devices: 135 us -> none  [per_device(): lax.psum_scatter(jnp.einsum('pms,pns->mn', x_cols, partner, preferred_ele...]
    ppermute x0 -> x13, waiting for transfers between devices: none -> 19.5 us  [the longest x10 14 us: swap(): return lax.ppermute(x, 'mu', [(i, i ^ step) for i in range(2 * CHIPS)])]
    all_to_all x2 -> x0, waiting for transfers between devices: 17.7 us -> none  [the longest x1 9.66 us: per_device(): lax.all_to_all(half_x, 'mu', split_axis=2, concat_axis=1, tiled=True)]
    ppermute x0 -> x13, starting transfers between devices: none -> 13.1 us  [the longest x10 8.61 us: swap(): return lax.ppermute(x, 'mu', [(i, i ^ step) for i in range(2 * CHIPS)])]
    all_to_all x4 -> x0, local copies, waits for them, and re-layouts: 11.8 us -> none  [the longest x2 5.89 us: per_device(): lax.all_to_all(half_x, 'mu', split_axis=2, concat_axis=1, tiled=True)]
    all_gather x1 -> x0, blocking collectives: 11.3 us -> none  [per_device(): lax.all_gather(dens_kept, 'mu', axis=0, tiled=True)]
    all_to_all x2 -> x0, starting transfers between devices: 7.79 us -> none  [the longest x1 4.24 us: per_device(): lax.all_to_all(kept, 'mu', split_axis=2, concat_axis=1, tiled=True)]
    unnamed x6 -> x8, local copies, waits for them, and re-layouts: 10.2 us -> 3.44 us
  transfers between devices with their start and end apart: 3 -> 13, of which waited for: 3 -> 9; matrix products, arithmetic and copies ran while one was open for 5% -> 0% of each run, Pallas kernels for 0% -> 0%
where the time goes in v1:
time: 40.8 us; the launch traced here: 40.6 us
  waiting for transfers between devices  19.5 us (48%)
  starting transfers between devices  13.1 us (32%)
  Pallas kernels  3.91 us (10%)
  local copies, waits for them, and re-layouts  3.45 us (8%)
  other arithmetic  0.65 us (2%)
    ppermute x10, waiting for transfers between devices, swap(): return lax.ppermute(x, 'mu', [(i, i ^ step) for i in range(2 * CHIPS)])  14 us
    ppermute x10, starting transfers between devices, swap(): return lax.ppermute(x, 'mu', [(i, i ^ step) for i in range(2 * CHIPS)])  8.61 us
    ppermute x3, waiting for transfers between devices, spread(): lax.ppermute(strip_of(a ^ d), 'aux', [(i, i ^ d) for i in range(4)])  5.49 us
    ppermute x3, starting transfers between devices, spread(): lax.ppermute(strip_of(a ^ d), 'aux', [(i, i ^ d) for i in range(4)])  4.45 us
    unnamed x8, local copies, waits for them, and re-layouts  3.44 us
    pallas_call x1, Pallas kernels, spread(): pl.pallas_call(lambda *refs: main_kernel(group, *refs), out_shape=[chunk,...  3.13 us
  transfers between devices with their start and end apart: 13, of which 9 were waited for; matrix products, arithmetic and copies ran while one was open for 0% of the time, Pallas kernels for 0%

profile of v1, /device:TPU:0, one launch (start us, length us, event | category | flops | bytes accessed | tf_op | source)
XLA Modules:
  0.0 40.6 jit_solution(6948579579509256396)
XLA Ops:
  0.0 1.2 %copy-done = bf16[16,64,512]{2,1,0:T(8,128)(2,1)S(1)} copy-done((bf16[16,64,512]{2,1,0:T(8,128)(2,1)S(1)}, bf16[16,64,512]{2,1,0:T(8,128)(2,1)}, u32[]{:S(2)}) %copy-start) | copy-done | bytes 1048600
  1.2 0.8 %copy-done.1 = bf16[64,512]{1,0:T(8,128)(2,1)S(1)} copy-done((bf16[64,512]{1,0:T(8,128)(2,1)S(1)}, bf16[64,512]{1,0:T(8,128)(2,1)}, u32[]{:S(2)}) %copy-start.1) | copy-done | bytes 65560
  2.1 0.7 %copy-done.2 = s32[8,8]{1,0:T(8,128)S(1)} copy-done((s32[8,8]{1,0:T(8,128)S(1)}, s32[8,8]{1,0:T(8,128)}, u32[]{:S(2)}) %copy-start.2) | copy-done | bytes 280
  2.8 0.7 %copy-done.3 = s32[8,8]{1,0:T(8,128)S(1)} copy-done((s32[8,8]{1,0:T(8,128)S(1)}, s32[8,8]{1,0:T(8,128)}, u32[]{:S(2)}) %copy-start.3) | copy-done | bytes 280
  3.4 0.8 %pack.1 = (bf16[5,64,512]{2,1,0:T(8,128)(2,1)S(1)}, bf16[6,64,256]{2,1,0:T(8,128)(2,1)S(1)}, bf16[6,64,256]{2,1,0:T(8,128)(2,1)S(1)}, bf16[6,64,256]{2,1,0:T(8,128)(2,1)S(1)}) custom-call(bf16[16,64,512]{2,1,0:T(8,128)(2,1)S(1)} %copy-done, bf16[64,512]{1,0:T(8,128)(2,1)S(1)} %copy-done.1, s32[8,8]{1,0:T(8,128)S(1)} %copy-done.2, s32[8,8]{1,0:T(8,128)S(1)} %copy-done.3), custom_call_target="tpu_custom_call" | custom-call | tf_op jit(solution)/shard_map/pack/pallas_call | solution.py:105
  4.2 3.0 %collective-permute-start.1 = (bf16[6,64,256]{2,1,0:T(8,128)(2,1)S(1)}, bf16[6,64,256]{2,1,0:T(8,128)(2,1)S(1)}, u32[]{:S(2)}, u32[]{:S(2)}) collective-permute-start(bf16[6,64,256]{2,1,0:T(8,128)(2,1)S(1)} %get-tuple-element.14), channel_id=1, source_target_pairs={{0,8},{4,12},{8,0},{12,4},{16,24},{20,28},{24,16},{28,20},{1,9},{5... | collective-permute-start | bytes 589832 | tf_op jit(solution)/shard_map/ppermute | solution.py:102
  7.2 1.5 %collective-permute-start.2 = (bf16[6,64,256]{2,1,0:T(8,128)(2,1)S(1)}, bf16[6,64,256]{2,1,0:T(8,128)(2,1)S(1)}, u32[]{:S(2)}, u32[]{:S(2)}) collective-permute-start(bf16[6,64,256]{2,1,0:T(8,128)(2,1)S(1)} %get-tuple-element.15), channel_id=1, source_target_pairs={{0,16},{4,20},{8,24},{12,28},{16,0},{20,4},{24,8},{28,12},{1,17},{... | collective-permute-start | bytes 589832 | tf_op jit(solution)/shard_map/ppermute | solution.py:102
  8.8 0.0 collective-permute-start.3
  8.8 0.0 collective-permute-start
  8.8 4.2 %collective-permute-done.1.refs_2_ = bf16[6,64,256]{2,1,0:T(8,128)(2,1)S(1)} collective-permute-done((bf16[6,64,256]{2,1,0:T(8,128)(2,1)S(1)}, bf16[6,64,256]{2,1,0:T(8,128)(2,1)S(1)}, u32[]{:S(2)}, u32[]{:S(2)}) %collective-permute-start.1) | collective-permute-done | bytes 196640 | tf_op jit(solution)/shard_map/ppermute | solution.py:102
  13.0 0.0 collective-permute-start.4
  13.0 4.8 %collective-permute-done.2.refs_3_ = bf16[6,64,256]{2,1,0:T(8,128)(2,1)S(1)} collective-permute-done((bf16[6,64,256]{2,1,0:T(8,128)(2,1)S(1)}, bf16[6,64,256]{2,1,0:T(8,128)(2,1)S(1)}, u32[]{:S(2)}, u32[]{:S(2)}) %collective-permute-start.2) | collective-permute-done | bytes 196640 | tf_op jit(solution)/shard_map/ppermute | solution.py:102
  17.8 0.0 collective-permute-start.5
  17.8 0.0 collective-permute-done.3.refs_4_
  17.8 0.5 %collective-permute-start.6 = (bf16[6,64,256]{2,1,0:T(8,128)(2,1)S(1)}, bf16[6,64,256]{2,1,0:T(8,128)(2,1)S(1)}, u32[]{:S(2)}, u32[]{:S(2)}) collective-permute-start(bf16[6,64,256]{2,1,0:T(8,128)(2,1)S(1)} %collective-permute-done.3.refs_4_), channel_id=1, source_target_pairs={{0,4},{4,0},{8,12},{12,8},{16,20},{20,16},{24,28},{28,24},{1,5},{5... | collective-permute-start | bytes 589832 | tf_op jit(solution)/shard_map/ppermute | solution.py:102
  18.3 0.0 collective-permute-done.refs_1_
  18.3 0.0 collective-permute-done.4.refs_5_
  18.3 0.9 %collective-permute-done.5.refs_6_ = bf16[6,64,256]{2,1,0:T(8,128)(2,1)S(1)} collective-permute-done((bf16[6,64,256]{2,1,0:T(8,128)(2,1)S(1)}, bf16[6,64,256]{2,1,0:T(8,128)(2,1)S(1)}, u32[]{:S(2)}, u32[]{:S(2)}) %collective-permute-start.5) | collective-permute-done | bytes 196640 | tf_op jit(solution)/shard_map/ppermute | solution.py:102
  19.3 0.3 collective-permute-done.6.refs_7_
  19.5 3.1 %exchange.1 = (bf16[64,512]{1,0:T(8,128)(2,1)S(1)}, bf16[64,512]{1,0:T(8,128)(2,1)S(1)}, bf16[64,512]{1,0:T(8,128)(2,1)S(1)}, f32[64,512]{1,0:T(8,128)S(1)}) custom-call(bf16[5,64,512]{2,1,0:T(8,128)(2,1)S(1)} %get-tuple-element.13.refs_0_, bf16[5,64,512]{2,1,0:T(8,128)(2,1)S(1)} %collective-permute-done.refs_1_, ...), custom_call_target="tpu_custom_call" | custom-call | tf_op jit(solution)/shard_map/exchange/pallas_call | solution.py:117
  22.7 1.0 %collective-permute-start.7 = (bf16[64,512]{1,0:T(8,128)(2,1)S(1)}, bf16[64,512]{1,0:T(8,128)(2,1)S(1)}, u32[]{:S(2)}, u32[]{:S(2)}) collective-permute-start(bf16[64,512]{1,0:T(8,128)(2,1)S(1)} %get-tuple-element.18), channel_id=1, source_target_pairs={{0,8},{4,12},{8,0},{12,4},{16,24},{20,28},{24,16},{28,20},{1,9},{5... | collective-permute-start | bytes 196616 | tf_op jit(solution)/shard_map/ppermute | solution.py:102
  23.7 1.1 %collective-permute-start.8 = (bf16[64,512]{1,0:T(8,128)(2,1)S(1)}, bf16[64,512]{1,0:T(8,128)(2,1)S(1)}, u32[]{:S(2)}, u32[]{:S(2)}) collective-permute-start(bf16[64,512]{1,0:T(8,128)(2,1)S(1)} %get-tuple-element.19), channel_id=1, source_target_pairs={{0,16},{4,20},{8,24},{12,28},{16,0},{20,4},{24,8},{28,12},{1,17},{... | collective-permute-start | bytes 196616 | tf_op jit(solution)/shard_map/ppermute | solution.py:102
  24.8 1.4 %collective-permute-start.9 = (bf16[64,512]{1,0:T(8,128)(2,1)S(1)}, bf16[64,512]{1,0:T(8,128)(2,1)S(1)}, u32[]{:S(2)}, u32[]{:S(2)}) collective-permute-start(bf16[64,512]{1,0:T(8,128)(2,1)S(1)} %get-tuple-element.20), channel_id=1, source_target_pairs={{0,24},{4,28},{8,16},{12,20},{16,8},{20,12},{24,0},{28,4},{1,25},{... | collective-permute-start | bytes 196616 | tf_op jit(solution)/shard_map/ppermute | solution.py:102
  26.2 0.8 %collective-permute-done.7 = bf16[64,512]{1,0:T(8,128)(2,1)S(1)} collective-permute-done((bf16[64,512]{1,0:T(8,128)(2,1)S(1)}, bf16[64,512]{1,0:T(8,128)(2,1)S(1)}, u32[]{:S(2)}, u32[]{:S(2)}) %collective-permute-start.7) | collective-permute-done | bytes 65568 | tf_op jit(solution)/shard_map/ppermute | solution.py:102
  27.0 1.0 %collective-permute-done.8 = bf16[64,512]{1,0:T(8,128)(2,1)S(1)} collective-permute-done((bf16[64,512]{1,0:T(8,128)(2,1)S(1)}, bf16[64,512]{1,0:T(8,128)(2,1)S(1)}, u32[]{:S(2)}, u32[]{:S(2)}) %collective-permute-start.8) | collective-permute-done | bytes 65568 | tf_op jit(solution)/shard_map/ppermute | solution.py:102
  28.0 2.0 %collective-permute-done.9 = bf16[64,512]{1,0:T(8,128)(2,1)S(1)} collective-permute-done((bf16[64,512]{1,0:T(8,128)(2,1)S(1)}, bf16[64,512]{1,0:T(8,128)(2,1)S(1)}, u32[]{:S(2)}, u32[]{:S(2)}) %collective-permute-start.9) | collective-permute-done | bytes 65568 | tf_op jit(solution)/shard_map/ppermute | solution.py:102
  30.0 1.6 %collective-permute-start.10 = (f32[16,512]{1,0:T(8,128)S(1)}, f32[16,512]{1,0:T(8,128)S(1)}, u32[]{:S(2)}, u32[]{:S(2)}) collective-permute-start(f32[16,512]{1,0:T(8,128)S(1)} %get-tuple-element.21), channel_id=1, source_target_pairs={{0,1},{1,0},{2,3},{3,2},{4,5},{5,4},{6,7},{7,6},{8,9},{9,8},{10,11... | collective-permute-start | bytes 98312 | tf_op jit(solution)/shard_map/ppermute | solution.py:143
  31.7 2.6 %collective-permute-start.11 = (f32[16,512]{1,0:T(8,128)S(1)}, f32[16,512]{1,0:T(8,128)S(1)}, u32[]{:S(2)}, u32[]{:S(2)}) collective-permute-start(f32[16,512]{1,0:T(8,128)S(1)} %get-tuple-element.23), channel_id=1, source_target_pairs={{0,2},{1,3},{2,0},{3,1},{4,6},{5,7},{6,4},{7,5},{8,10},{9,11},{10,... | collective-permute-start | bytes 98312 | tf_op jit(solution)/shard_map/ppermute | solution.py:143
  34.2 0.2 collective-permute-start.12
  34.5 2.6 %collective-permute-done.11 = f32[16,512]{1,0:T(8,128)S(1)} collective-permute-done((f32[16,512]{1,0:T(8,128)S(1)}, f32[16,512]{1,0:T(8,128)S(1)}, u32[]{:S(2)}, u32[]{:S(2)}) %collective-permute-start.11) | collective-permute-done | bytes 32800 | tf_op jit(solution)/shard_map/ppermute | solution.py:143
  37.1 2.9 %collective-permute-done.12 = f32[16,512]{1,0:T(8,128)S(1)} collective-permute-done((f32[16,512]{1,0:T(8,128)S(1)}, f32[16,512]{1,0:T(8,128)S(1)}, u32[]{:S(2)}, u32[]{:S(2)}) %collective-permute-start.12) | collective-permute-done | bytes 32800 | tf_op jit(solution)/shard_map/ppermute | solution.py:143
  40.0 0.6 %add_add_fusion = f32[16,512]{1,0:T(8,128)} fusion(f32[16,512]{1,0:T(8,128)S(1)} %collective-permute-done.12, f32[16,512]{1,0:T(8,128)S(1)} %collective-permute-done.11, f32[16,512]{1,0:T(8,128)S(1)} %collective-permute-done.10, f32[64,512]{1,0:T(8,128)S(1)} %convert_add_fusion, s32[]{:T(128)S(6)} %select_n.12), kind=kLoop, calls=%fused_computation.1 | loop fusion | flops 24576 | bytes 163844 | tf_op jit(solution)/shard_map/add | solution.py:143
  (7 shorter events, 0.1 us)
Async XLA Ops:
  0.0 1.2 %copy-start = (bf16[16,64,512]{2,1,0:T(8,128)(2,1)S(1)}, bf16[16,64,512]{2,1,0:T(8,128)(2,1)}, u32[]{:S(2)}) copy-start(bf16[16,64,512]{2,1,0:T(8,128)(2,1)} %refs_0_.1) | copy-start | bytes 3145732
  1.2 0.8 %copy-start.1 = (bf16[64,512]{1,0:T(8,128)(2,1)S(1)}, bf16[64,512]{1,0:T(8,128)(2,1)}, u32[]{:S(2)}) copy-start(bf16[64,512]{1,0:T(8,128)(2,1)} %refs_1_.1) | copy-start | bytes 196612
  2.1 0.7 %copy-start.2 = (s32[8,8]{1,0:T(8,128)S(1)}, s32[8,8]{1,0:T(8,128)}, u32[]{:S(2)}) copy-start(s32[8,8]{1,0:T(8,128)} %refs_2_.1) | copy-start | bytes 772
  2.8 0.7 %copy-start.3 = (s32[8,8]{1,0:T(8,128)S(1)}, s32[8,8]{1,0:T(8,128)}, u32[]{:S(2)}) copy-start(s32[8,8]{1,0:T(8,128)} %refs_3_.1) | copy-start | bytes 772
  4.2 8.7 %collective-permute-start.1 = (bf16[6,64,256]{2,1,0:T(8,128)(2,1)S(1)}, bf16[6,64,256]{2,1,0:T(8,128)(2,1)S(1)}, u32[]{:S(2)}, u32[]{:S(2)}) collective-permute-start(bf16[6,64,256]{2,1,0:T(8,128)(2,1)S(1)} %get-tuple-element.14), channel_id=1, source_target_pairs={{0,8},{4,12},{8,0},{12,4},{16,24},{20,28},{24,16},{28,20},{1,9},{5... | collective-permute-start | bytes 589832 | tf_op jit(solution)/shard_map/ppermute | solution.py:102
  7.2 10.6 %collective-permute-start.2 = (bf16[6,64,256]{2,1,0:T(8,128)(2,1)S(1)}, bf16[6,64,256]{2,1,0:T(8,128)(2,1)S(1)}, u32[]{:S(2)}, u32[]{:S(2)}) collective-permute-start(bf16[6,64,256]{2,1,0:T(8,128)(2,1)S(1)} %get-tuple-element.15), channel_id=1, source_target_pairs={{0,16},{4,20},{8,24},{12,28},{16,0},{20,4},{24,8},{28,12},{1,17},{... | collective-permute-start | bytes 589832 | tf_op jit(solution)/shard_map/ppermute | solution.py:102
  8.8 9.1 %collective-permute-start.3 = (bf16[6,64,256]{2,1,0:T(8,128)(2,1)S(1)}, bf16[6,64,256]{2,1,0:T(8,128)(2,1)S(1)}, u32[]{:S(2)}, u32[]{:S(2)}) collective-permute-start(bf16[6,64,256]{2,1,0:T(8,128)(2,1)S(1)} %get-tuple-element.16), channel_id=1, source_target_pairs={{0,24},{4,28},{8,16},{12,20},{16,8},{20,12},{24,0},{28,4},{1,25},{... | collective-permute-start | bytes 589832 | tf_op jit(solution)/shard_map/ppermute | solution.py:102
  8.8 9.6 %collective-permute-start = (bf16[5,64,512]{2,1,0:T(8,128)(2,1)S(1)}, bf16[5,64,512]{2,1,0:T(8,128)(2,1)S(1)}, u32[]{:S(2)}, u32[]{:S(2)}) collective-permute-start(bf16[5,64,512]{2,1,0:T(8,128)(2,1)S(1)} %get-tuple-element.13.refs_0_), channel_id=1, source_target_pairs={{0,4},{4,0},{8,12},{12,8},{16,20},{20,16},{24,28},{28,24},{1,5},{5... | collective-permute-start | bytes 983048 | tf_op jit(solution)/shard_map/ppermute | solution.py:102
  13.0 5.4 %collective-permute-start.4 = (bf16[6,64,256]{2,1,0:T(8,128)(2,1)S(1)}, bf16[6,64,256]{2,1,0:T(8,128)(2,1)S(1)}, u32[]{:S(2)}, u32[]{:S(2)}) collective-permute-start(bf16[6,64,256]{2,1,0:T(8,128)(2,1)S(1)} %collective-permute-done.1.refs_2_), channel_id=1, source_target_pairs={{0,4},{4,0},{8,12},{12,8},{16,20},{20,16},{24,28},{28,24},{1,5},{5... | collective-permute-start | bytes 589832 | tf_op jit(solution)/shard_map/ppermute | solution.py:102
  17.8 1.4 %collective-permute-start.5 = (bf16[6,64,256]{2,1,0:T(8,128)(2,1)S(1)}, bf16[6,64,256]{2,1,0:T(8,128)(2,1)S(1)}, u32[]{:S(2)}, u32[]{:S(2)}) collective-permute-start(bf16[6,64,256]{2,1,0:T(8,128)(2,1)S(1)} %collective-permute-done.2.refs_3_), channel_id=1, source_target_pairs={{0,4},{4,0},{8,12},{12,8},{16,20},{20,16},{24,28},{28,24},{1,5},{5... | collective-permute-start | bytes 589832 | tf_op jit(solution)/shard_map/ppermute | solution.py:102
  17.8 1.7 %collective-permute-start.6 = (bf16[6,64,256]{2,1,0:T(8,128)(2,1)S(1)}, bf16[6,64,256]{2,1,0:T(8,128)(2,1)S(1)}, u32[]{:S(2)}, u32[]{:S(2)}) collective-permute-start(bf16[6,64,256]{2,1,0:T(8,128)(2,1)S(1)} %collective-permute-done.3.refs_4_), channel_id=1, source_target_pairs={{0,4},{4,0},{8,12},{12,8},{16,20},{20,16},{24,28},{28,24},{1,5},{5... | collective-permute-start | bytes 589832 | tf_op jit(solution)/shard_map/ppermute | solution.py:102
  22.7 4.3 %collective-permute-start.7 = (bf16[64,512]{1,0:T(8,128)(2,1)S(1)}, bf16[64,512]{1,0:T(8,128)(2,1)S(1)}, u32[]{:S(2)}, u32[]{:S(2)}) collective-permute-start(bf16[64,512]{1,0:T(8,128)(2,1)S(1)} %get-tuple-element.18), channel_id=1, source_target_pairs={{0,8},{4,12},{8,0},{12,4},{16,24},{20,28},{24,16},{28,20},{1,9},{5... | collective-permute-start | bytes 196616 | tf_op jit(solution)/shard_map/ppermute | solution.py:102
  23.7 4.3 %collective-permute-start.8 = (bf16[64,512]{1,0:T(8,128)(2,1)S(1)}, bf16[64,512]{1,0:T(8,128)(2,1)S(1)}, u32[]{:S(2)}, u32[]{:S(2)}) collective-permute-start(bf16[64,512]{1,0:T(8,128)(2,1)S(1)} %get-tuple-element.19), channel_id=1, source_target_pairs={{0,16},{4,20},{8,24},{12,28},{16,0},{20,4},{24,8},{28,12},{1,17},{... | collective-permute-start | bytes 196616 | tf_op jit(solution)/shard_map/ppermute | solution.py:102
  24.8 5.2 %collective-permute-start.9 = (bf16[64,512]{1,0:T(8,128)(2,1)S(1)}, bf16[64,512]{1,0:T(8,128)(2,1)S(1)}, u32[]{:S(2)}, u32[]{:S(2)}) collective-permute-start(bf16[64,512]{1,0:T(8,128)(2,1)S(1)} %get-tuple-element.20), channel_id=1, source_target_pairs={{0,24},{4,28},{8,16},{12,20},{16,8},{20,12},{24,0},{28,4},{1,25},{... | collective-permute-start | bytes 196616 | tf_op jit(solution)/shard_map/ppermute | solution.py:102
  30.0 4.5 %collective-permute-start.10 = (f32[16,512]{1,0:T(8,128)S(1)}, f32[16,512]{1,0:T(8,128)S(1)}, u32[]{:S(2)}, u32[]{:S(2)}) collective-permute-start(f32[16,512]{1,0:T(8,128)S(1)} %get-tuple-element.21), channel_id=1, source_target_pairs={{0,1},{1,0},{2,3},{3,2},{4,5},{5,4},{6,7},{7,6},{8,9},{9,8},{10,11... | collective-permute-start | bytes 98312 | tf_op jit(solution)/shard_map/ppermute | solution.py:143
  31.7 5.4 %collective-permute-start.11 = (f32[16,512]{1,0:T(8,128)S(1)}, f32[16,512]{1,0:T(8,128)S(1)}, u32[]{:S(2)}, u32[]{:S(2)}) collective-permute-start(f32[16,512]{1,0:T(8,128)S(1)} %get-tuple-element.23), channel_id=1, source_target_pairs={{0,2},{1,3},{2,0},{3,1},{4,6},{5,7},{6,4},{7,5},{8,10},{9,11},{10,... | collective-permute-start | bytes 98312 | tf_op jit(solution)/shard_map/ppermute | solution.py:143
  34.2 5.7 %collective-permute-start.12 = (f32[16,512]{1,0:T(8,128)S(1)}, f32[16,512]{1,0:T(8,128)S(1)}, u32[]{:S(2)}, u32[]{:S(2)}) collective-permute-start(f32[16,512]{1,0:T(8,128)S(1)} %get-tuple-element.22), channel_id=1, source_target_pairs={{0,3},{1,2},{2,1},{3,0},{4,7},{5,6},{6,5},{7,4},{8,11},{9,10},{10,... | collective-permute-start | bytes 98312 | tf_op jit(solution)/shard_map/ppermute | solution.py:143

commit v2 on v1

v2 whole, which is shorter than its diff:
```python
import jax
import jax.numpy as jnp
from jax import lax
from jax.experimental import pallas as pl
from jax.experimental.pallas import tpu as pltpu
from jax.sharding import PartitionSpec as P

BF = jnp.bfloat16
F32 = jnp.float32
BLK = 64
TILE = 2 * BLK
CHIPS = 4


def expand_row(mask_ref, row, size):
    block = lax.broadcasted_iota(jnp.int32, (1, size), 1) // BLK
    line = jnp.zeros((1, size), F32)
    for j in range(size // BLK):
        line = jnp.where(block == j, mask_ref[row, j].astype(F32), line)
    return line.astype(BF)


def column(chip):
    return pl.ds(pl.multiple_of(chip * TILE, TILE), TILE)


def pack_kernel(group, b_hbm, d_hbm, pair_hbm, dens_hbm, own_ref, s1, s2, s3, pair_ref, dens_ref, d_ref, line_ref, sems):
    me = lax.axis_index("mu")
    c = me // 2
    k = me % 2
    size = d_ref.shape[1]
    part = group // 2
    copies = [
        pltpu.make_async_copy(pair_hbm, pair_ref, sems.at[0]),
        pltpu.make_async_copy(dens_hbm, dens_ref, sems.at[1]),
        pltpu.make_async_copy(d_hbm, d_ref, sems.at[2]),
    ]
    pieces = []
    for send, d in ((s1, 1 + k), (s2, 2 - k), (s3, 3)):
        first = (c ^ d) * group
        pieces.append((send, 0, group, first, c))
        if send is not s3:
            pieces.append((send, group, group, first, c ^ (3 - d)))
            pieces.append((send, 2 * group, part, first + (d - 1) * part, c ^ 3))
    for i, (send, slot, count, first, chip) in enumerate(pieces):
        copies.append(
            pltpu.make_async_copy(
                b_hbm.at[pl.ds(first, count), :, column(chip)], send.at[pl.ds(slot, count)], sems.at[3 + i]
            )
        )
    copies.append(
        pltpu.make_async_copy(b_hbm.at[pl.ds(c * group, group)], own_ref.at[pl.ds(0, group)], sems.at[3 + len(pieces)])
    )
    for copy in copies:
        copy.start()
    copies[0].wait()
    pair_line = expand_row(pair_ref, me, size)
    for j in range(CHIPS):
        line_ref[j] = pair_line[:, j * TILE : (j + 1) * TILE].astype(F32)
    copies[1].wait()
    dens_line = expand_row(dens_ref, me, size)
    copies[2].wait()
    dens = d_ref[...] * dens_line
    own_dens = [dens[:, (2 * (j % CHIPS) + j // CHIPS) * BLK :][:, :BLK] for j in range(2 * CHIPS)]
    tiles = [jnp.concatenate(own_dens[2 * j : 2 * j + 2], axis=1) for j in range(CHIPS)]
    for j in range(CHIPS):
        own_ref[group, :, j * TILE : (j + 1) * TILE] = tiles[j]
        for send in (s1, s2, s3):
            send[send.shape[0] - CHIPS + j] = tiles[j]
    for copy, (send, slot, count, first, chip) in zip(copies[3:], pieces):
        copy.wait()
        line = line_ref[chip].astype(BF)
        for p in range(slot, slot + count):
            send[p] = send[p] * line
    copies[-1].wait()
    for p in range(group):
        own_ref[p] = own_ref[p] * pair_line


def main_kernel(group, own_ref, mate_ref, r1, r2, r3, q1, q2, q3, e1, e2, e3, keep_ref, t_scr, d_scr, x_scr, k_scr):
    me = lax.axis_index("mu")
    c = me // 2
    k = me % 2
    size = t_scr.shape[1]
    half = size // 2
    part = group // 2

    def rows(p, core, chip):
        return pl.ds(pl.multiple_of(p * size + core * half + chip * BLK, BLK), BLK)

    def fill(o0, o1, x0, y0, g0, x1, y1, g1):
        cx, cy, cg = c ^ 1, c ^ 2, c ^ 3
        for core, own, x, y, g in ((0, o0, x0, y0, g0), (1, o1, x1, y1, g1)):
            d_scr[pl.ds(pl.multiple_of(c * TILE + core * BLK, BLK), BLK), :] = own[group]
            for r, ref in ((cx, x), (cy, y), (cg, g)):
                at = pl.ds(pl.multiple_of(r * TILE + core * BLK, BLK), BLK)
                for j in range(CHIPS):
                    d_scr[at, j * TILE : (j + 1) * TILE] = ref[ref.shape[0] - CHIPS + j]
            for p in range(group):
                t_scr[rows(p, core, c), :] = own[p]
                t_scr[rows(p, core, cx), column(cx)] = x[p]
                t_scr[rows(p, core, cx), column(cg)] = x[group + p]
                t_scr[rows(p, core, cy), column(cy)] = y[p]
                t_scr[rows(p, core, cy), column(cg)] = y[group + p]
                t_scr[rows(p, core, cg), column(cg)] = g[p]
                if p < part:
                    t_scr[rows(p, core, cx), column(cy)] = x[2 * group + p]
                else:
                    t_scr[rows(p, core, cy), column(cx)] = y[2 * group + p - part]
        for p in range(group):
            tasks = [(c, dst, o0[p, :, column(dst)], o1[p, :, column(dst)]) for dst in (cx, cy, cg)]
            tasks.append((cx, cg, x0[group + p], x1[group + p]))
            tasks.append((cy, cg, y0[group + p], y1[group + p]))
            if p < part:
                tasks.append((cx, cy, x0[2 * group + p], x1[2 * group + p]))
            else:
                tasks.append((cy, cx, y0[2 * group + p - part], y1[2 * group + p - part]))
            for s, dst, top, low in tasks:
                block = jnp.concatenate([top, low], axis=0).T
                t_scr[rows(p, 0, dst), column(s)] = block[:BLK]
                t_scr[rows(p, 1, dst), column(s)] = block[BLK:]

    @pl.when(k == 0)
    def _():
        fill(own_ref, mate_ref, r1, r2, r3, q2, q1, q3)

    @pl.when(k == 1)
    def _():
        fill(mate_ref, own_ref, q1, q2, q3, r2, r1, r3)

    for p in range(group):
        mine = t_scr[pl.ds(pl.multiple_of(p * size + k * half, half), half), :]
        x_scr[:, p * size : (p + 1) * size] = jnp.dot(mine, d_scr[...], preferred_element_type=F32).astype(BF)
    k_scr[...] = jnp.dot(x_scr[...], t_scr[...], preferred_element_type=F32)
    for out, d in ((e1, 1 + k), (e2, 2 - k), (e3, 3)):
        out[...] = k_scr[pl.ds(pl.multiple_of((c ^ d) * BLK, BLK), BLK), :].astype(BF)
    keep_ref[...] = k_scr[pl.ds(pl.multiple_of(c * BLK, BLK), BLK), :]


def spread(b_tensor, density, pair_mask, dens_mask):
    depth, width, size = b_tensor.shape
    group = depth // CHIPS
    vmem = pl.BlockSpec(memory_space=pltpu.VMEM)
    hbm = pl.BlockSpec(memory_space=pl.ANY)

    def swap(x, step):
        return lax.ppermute(x, "mu", [(i, i ^ step) for i in range(2 * CHIPS)])

    def turn(x, first):
        return lax.ppermute(x, "mu", [(i, i ^ (2 if (i % 2 == 0) == first else 4)) for i in range(2 * CHIPS)])

    def around(x1, x2, x3):
        return turn(x1, True), turn(x2, False), swap(x3, 6)

    def slots(count):
        return jax.ShapeDtypeStruct((count, width, TILE), BF)

    near = 2 * group + group // 2 + CHIPS
    own, *sends = pl.pallas_call(
        lambda *refs: pack_kernel(group, *refs),
        out_shape=[jax.ShapeDtypeStruct((group + 1, width, size), BF), slots(near), slots(near), slots(group + CHIPS)],
        in_specs=[hbm] * 4,
        out_specs=[vmem] * 4,
        scratch_shapes=[
            pltpu.SMEM(pair_mask.shape, jnp.int32),
            pltpu.SMEM(dens_mask.shape, jnp.int32),
            pltpu.VMEM(density.shape, BF),
            pltpu.VMEM((CHIPS, 1, TILE), F32),
            pltpu.SemaphoreType.DMA((11,)),
        ],
        compiler_params=pltpu.CompilerParams(vmem_limit_bytes=16 << 20),
        name="pack",
    )(*(pltpu.with_memory_space_constraint(x, pltpu.HBM) for x in (b_tensor, density, pair_mask, dens_mask)))
    got = around(*sends)
    mate = swap(own, 1)
    others = [swap(g, 1) for g in got]
    chunk = jax.ShapeDtypeStruct((width, size), BF)
    *parts, keep = pl.pallas_call(
        lambda *refs: main_kernel(group, *refs),
        out_shape=[chunk, chunk, chunk, jax.ShapeDtypeStruct((width, size), F32)],
        in_specs=[vmem] * 8,
        out_specs=[vmem] * 4,
        scratch_shapes=[
            pltpu.VMEM((group * size, size), BF),
            pltpu.VMEM((size, size), BF),
            pltpu.VMEM((size // 2, group * size), BF),
            pltpu.VMEM((size // 2, size), F32),
        ],
        compiler_params=pltpu.CompilerParams(vmem_limit_bytes=32 << 20),
        name="exchange",
    )(own, mate, *got, *others)
    plane = keep
    for part in around(*parts):
        plane = plane + part.astype(F32)
    a = lax.axis_index("aux")
    strips = plane.reshape(2, 2, width // 4, size)

    def pick(x, index, axis):
        return lax.dynamic_index_in_dim(x, index, axis, keepdims=False)

    def along(x, step):
        return lax.ppermute(x, "aux", [(i, i ^ step) for i in range(4)])

    pair = pick(strips, a % 2, 1) + along(pick(strips, 1 - a % 2, 1), 1)
    return pick(pair, a // 2, 0) + along(pick(pair, 1 - a // 2, 0), 2)


def gathered(b_tensor, density, pair_mask, dens_mask):
    depth, width, nbas = b_tensor.shape
    owner = lax.axis_index("mu")
    pair_row = lax.dynamic_slice_in_dim(pair_mask, owner, 1, 0)[0]
    dens_row = lax.dynamic_slice_in_dim(dens_mask, owner, 1, 0)[0]
    kept = b_tensor * jnp.repeat(pair_row, width).astype(BF)[None, None, :]
    dens_kept = density * jnp.repeat(dens_row, width).astype(BF)[None, :]
    summed = jnp.dot(
        kept.reshape(depth * width, nbas),
        lax.all_gather(dens_kept, "mu", axis=0, tiled=True),
        preferred_element_type=F32,
    )
    half_x = summed.astype(BF).reshape(depth, width, nbas)
    x_cols = lax.all_to_all(half_x, "mu", split_axis=2, concat_axis=1, tiled=True)
    partner = lax.all_to_all(kept, "mu", split_axis=2, concat_axis=1, tiled=True)
    return lax.psum_scatter(
        jnp.einsum("pms,pns->mn", x_cols, partner, preferred_element_type=F32),
        ("mu", "aux"),
        scatter_dimension=0,
        tiled=True,
    )


def solution(mesh):
    in_specs = (P("aux", "mu", None), P("mu", None), P(), P())
    out_specs = P(("mu", "aux"), None)

    def per_device(b_tensor, density, pair_mask, dens_mask):
        depth, width, size = b_tensor.shape
        fits = mesh.shape["mu"] == 2 * CHIPS and mesh.shape["aux"] == 4
        fits = fits and depth % CHIPS == 0 and width == BLK and size == 2 * CHIPS * BLK
        step = spread if fits else gathered
        return step(b_tensor, density, pair_mask, dens_mask)

    return jax.shard_map(per_device, mesh=mesh, in_specs=in_specs, out_specs=out_specs, check_vma=False)
```

time: 40.8 us -> 35.5 us (0.87)
  local copies, waits for them, and re-layouts: 3.45 us -> 0.03 us
  waiting for transfers between devices: 19.5 us -> 18.2 us
  Pallas kernels: 3.91 us -> 3.14 us
    ppermute x10 -> x6, waiting for transfers between devices: 14 us -> 6.39 us  [swap(): return lax.ppermute(x, 'mu', [(i, i ^ step) for i in range(2 * CHIPS)])]
    ppermute x3 -> x6, starting transfers between devices: 4.45 us -> 12 us  [the longest x4 7.53 us: turn(): lax.ppermute(x, 'mu', [(i, i ^ (2 if (i % 2 == 0) == first else 4)) for i...]
    ppermute x10 -> x6, starting transfers between devices: 8.61 us -> 1.22 us  [swap(): return lax.ppermute(x, 'mu', [(i, i ^ step) for i in range(2 * CHIPS)])]
    ppermute x3 -> x6, waiting for transfers between devices: 5.49 us -> 11.8 us  [the longest x4 7.08 us: turn(): lax.ppermute(x, 'mu', [(i, i ^ (2 if (i % 2 == 0) == first else 4)) for i...]
    unnamed x8 -> x0, local copies, waits for them, and re-layouts: 3.44 us -> none
    pallas_call x1, Pallas kernels: 3.13 us -> 1.83 us  [spread(): pl.pallas_call(lambda *refs: main_kernel(group, *refs), out_shape=[chunk,...]
    pallas_call x1, Pallas kernels: 0.78 us -> 1.32 us  [spread(): pl.pallas_call(lambda *refs: pack_kernel(group, *refs), out_shape=[jax.Sh...]
  transfers between devices with their start and end apart: 13 -> 12, of which waited for: 9 -> 9; matrix products, arithmetic and copies ran while one was open for 0% -> 0% of each run, Pallas kernels for 0% -> 0%
where the time goes in v2:
time: 35.5 us; the launch traced here: 35.3 us
  waiting for transfers between devices  18.2 us (51%)
  starting transfers between devices  13.2 us (37%)
  Pallas kernels  3.14 us (9%)
  other arithmetic  0.66 us (2%)
    ppermute x4, starting transfers between devices, turn(): lax.ppermute(x, 'mu', [(i, i ^ (2 if (i % 2 == 0) == first else 4)) for i...  7.53 us
    ppermute x4, waiting for transfers between devices, turn(): lax.ppermute(x, 'mu', [(i, i ^ (2 if (i % 2 == 0) == first else 4)) for i...  7.08 us
    ppermute x6, waiting for transfers between devices, swap(): return lax.ppermute(x, 'mu', [(i, i ^ step) for i in range(2 * CHIPS)])  6.39 us
    ppermute x2, waiting for transfers between devices, along(): return lax.ppermute(x, 'aux', [(i, i ^ step) for i in range(4)])  4.74 us
    ppermute x2, starting transfers between devices, along(): return lax.ppermute(x, 'aux', [(i, i ^ step) for i in range(4)])  4.47 us
    pallas_call x1, Pallas kernels, spread(): pl.pallas_call(lambda *refs: main_kernel(group, *refs), out_shape=[chunk,...  1.83 us
    pallas_call x1, Pallas kernels, spread(): pl.pallas_call(lambda *refs: pack_kernel(group, *refs), out_shape=[jax.Sh...  1.32 us
    ppermute x6, starting transfers between devices, swap(): return lax.ppermute(x, 'mu', [(i, i ^ step) for i in range(2 * CHIPS)])  1.22 us
  transfers between devices with their start and end apart: 12, of which 9 were waited for; matrix products, arithmetic and copies ran while one was open for 0% of the time, Pallas kernels for 0%

profile of v2, /device:TPU:0, one launch (start us, length us, event | category | flops | bytes accessed | tf_op | source)
XLA Modules:
  0.0 35.3 jit_solution(5555543002107620657)
XLA Ops:
  0.0 1.3 %pack.1 = (bf16[5,64,512]{2,1,0:T(8,128)(2,1)S(1)}, bf16[14,64,128]{2,1,0:T(8,128)(2,1)S(1)}, bf16[14,64,128]{2,1,0:T(8,128)(2,1)S(1)}, bf16[8,64,128]{2,1,0:T(8,128)(2,1)S(1)}) custom-call(bf16[16,64,512]{2,1,0:T(8,128)(2,1)} %refs_0_.1, bf16[64,512]{1,0:T(8,128)(2,1)} %refs_1_.1, s32[8,8]{1,0:T(8,128)} %refs_2_.1, s32[8,8]{1,0:T(8,128)} %refs_3_.1), custom_call_target="tpu_custom_call" | custom-call | tf_op jit(solution)/shard_map/pack/pallas_call | solution.py:159
  1.3 3.0 %collective-permute-start.1 = (bf16[14,64,128]{2,1,0:T(8,128)(2,1)S(1)}, bf16[14,64,128]{2,1,0:T(8,128)(2,1)S(1)}, u32[]{:S(2)}, u32[]{:S(2)}) collective-permute-start(bf16[14,64,128]{2,1,0:T(8,128)(2,1)S(1)} %get-tuple-element.14), channel_id=1, source_target_pairs={{0,8},{4,20},{8,0},{12,28},{16,24},{20,4},{24,16},{28,12},{1,9},{5... | collective-permute-start | bytes 688136 | tf_op jit(solution)/shard_map/ppermute | solution.py:150
  4.3 1.5 %collective-permute-start.2 = (bf16[14,64,128]{2,1,0:T(8,128)(2,1)S(1)}, bf16[14,64,128]{2,1,0:T(8,128)(2,1)S(1)}, u32[]{:S(2)}, u32[]{:S(2)}) collective-permute-start(bf16[14,64,128]{2,1,0:T(8,128)(2,1)S(1)} %get-tuple-element.15), channel_id=1, source_target_pairs={{0,16},{4,12},{8,24},{12,4},{16,0},{20,28},{24,8},{28,20},{1,17},{... | collective-permute-start | bytes 688136 | tf_op jit(solution)/shard_map/ppermute | solution.py:150
  5.8 0.0 collective-permute-start
  5.9 0.0 collective-permute-start.3
  5.9 4.3 %collective-permute-done.1.refs_2_ = bf16[14,64,128]{2,1,0:T(8,128)(2,1)S(1)} collective-permute-done((bf16[14,64,128]{2,1,0:T(8,128)(2,1)S(1)}, bf16[14,64,128]{2,1,0:T(8,128)(2,1)S(1)}, u32[]{:S(2)}, u32[]{:S(2)}) %collective-permute-start.1) | collective-permute-done | bytes 229408 | tf_op jit(solution)/shard_map/ppermute | solution.py:150
  10.2 0.0 collective-permute-start.4
  10.2 0.3 collective-permute-done.2.refs_3_
  10.5 0.6 %collective-permute-start.5 = (bf16[14,64,128]{2,1,0:T(8,128)(2,1)S(1)}, bf16[14,64,128]{2,1,0:T(8,128)(2,1)S(1)}, u32[]{:S(2)}, u32[]{:S(2)}) collective-permute-start(bf16[14,64,128]{2,1,0:T(8,128)(2,1)S(1)} %collective-permute-done.2.refs_3_), channel_id=1, source_target_pairs={{0,4},{4,0},{8,12},{12,8},{16,20},{20,16},{24,28},{28,24},{1,5},{5... | collective-permute-start | bytes 688136 | tf_op jit(solution)/shard_map/ppermute | solution.py:147
  11.2 2.8 %collective-permute-done.3.refs_4_ = bf16[8,64,128]{2,1,0:T(8,128)(2,1)S(1)} collective-permute-done((bf16[8,64,128]{2,1,0:T(8,128)(2,1)S(1)}, bf16[8,64,128]{2,1,0:T(8,128)(2,1)S(1)}, u32[]{:S(2)}, u32[]{:S(2)}) %collective-permute-start.3) | collective-permute-done | bytes 131104 | tf_op jit(solution)/shard_map/ppermute | solution.py:147
  14.0 0.0 collective-permute-start.6
  14.0 1.3 %collective-permute-done.6.refs_7_ = bf16[8,64,128]{2,1,0:T(8,128)(2,1)S(1)} collective-permute-done((bf16[8,64,128]{2,1,0:T(8,128)(2,1)S(1)}, bf16[8,64,128]{2,1,0:T(8,128)(2,1)S(1)}, u32[]{:S(2)}, u32[]{:S(2)}) %collective-permute-start.6) | collective-permute-done | bytes 131104 | tf_op jit(solution)/shard_map/ppermute | solution.py:147
  15.4 0.0 collective-permute-done.refs_1_
  15.4 0.0 collective-permute-done.4.refs_5_
  15.4 0.0 collective-permute-done.5.refs_6_
  15.4 1.8 %exchange.1 = (bf16[64,512]{1,0:T(8,128)(2,1)S(1)}, bf16[64,512]{1,0:T(8,128)(2,1)S(1)}, bf16[64,512]{1,0:T(8,128)(2,1)S(1)}, f32[64,512]{1,0:T(8,128)S(1)}) custom-call(bf16[5,64,512]{2,1,0:T(8,128)(2,1)S(1)} %get-tuple-element.13.refs_0_, bf16[5,64,512]{2,1,0:T(8,128)(2,1)S(1)} %collective-permute-done.refs_1_, ...), custom_call_target="tpu_custom_call" | custom-call | tf_op jit(solution)/shard_map/exchange/pallas_call | solution.py:178
  17.2 1.7 %collective-permute-start.7 = (bf16[64,512]{1,0:T(8,128)(2,1)S(1)}, bf16[64,512]{1,0:T(8,128)(2,1)S(1)}, u32[]{:S(2)}, u32[]{:S(2)}) collective-permute-start(bf16[64,512]{1,0:T(8,128)(2,1)S(1)} %get-tuple-element.18), channel_id=1, source_target_pairs={{0,8},{4,20},{8,0},{12,28},{16,24},{20,4},{24,16},{28,12},{1,9},{5... | collective-permute-start | bytes 196616 | tf_op jit(solution)/shard_map/ppermute | solution.py:150
  18.9 1.3 %collective-permute-start.8 = (bf16[64,512]{1,0:T(8,128)(2,1)S(1)}, bf16[64,512]{1,0:T(8,128)(2,1)S(1)}, u32[]{:S(2)}, u32[]{:S(2)}) collective-permute-start(bf16[64,512]{1,0:T(8,128)(2,1)S(1)} %get-tuple-element.19), channel_id=1, source_target_pairs={{0,16},{4,12},{8,24},{12,4},{16,0},{20,28},{24,8},{28,20},{1,17},{... | collective-permute-start | bytes 196616 | tf_op jit(solution)/shard_map/ppermute | solution.py:150
  20.2 0.5 %collective-permute-start.9 = (bf16[64,512]{1,0:T(8,128)(2,1)S(1)}, bf16[64,512]{1,0:T(8,128)(2,1)S(1)}, u32[]{:S(2)}, u32[]{:S(2)}) collective-permute-start(bf16[64,512]{1,0:T(8,128)(2,1)S(1)} %get-tuple-element.20), channel_id=1, source_target_pairs={{0,24},{4,28},{8,16},{12,20},{16,8},{20,12},{24,0},{28,4},{1,25},{... | collective-permute-start | bytes 196616 | tf_op jit(solution)/shard_map/ppermute | solution.py:147
  20.8 1.4 %collective-permute-done.7 = bf16[64,512]{1,0:T(8,128)(2,1)S(1)} collective-permute-done((bf16[64,512]{1,0:T(8,128)(2,1)S(1)}, bf16[64,512]{1,0:T(8,128)(2,1)S(1)}, u32[]{:S(2)}, u32[]{:S(2)}) %collective-permute-start.7) | collective-permute-done | bytes 65568 | tf_op jit(solution)/shard_map/ppermute | solution.py:150
  22.1 1.1 %collective-permute-done.8 = bf16[64,512]{1,0:T(8,128)(2,1)S(1)} collective-permute-done((bf16[64,512]{1,0:T(8,128)(2,1)S(1)}, bf16[64,512]{1,0:T(8,128)(2,1)S(1)}, u32[]{:S(2)}, u32[]{:S(2)}) %collective-permute-start.8) | collective-permute-done | bytes 65568 | tf_op jit(solution)/shard_map/ppermute | solution.py:150
  23.2 2.2 %collective-permute-done.9 = bf16[64,512]{1,0:T(8,128)(2,1)S(1)} collective-permute-done((bf16[64,512]{1,0:T(8,128)(2,1)S(1)}, bf16[64,512]{1,0:T(8,128)(2,1)S(1)}, u32[]{:S(2)}, u32[]{:S(2)}) %collective-permute-start.9) | collective-permute-done | bytes 65568 | tf_op jit(solution)/shard_map/ppermute | solution.py:147
  25.4 1.6 %collective-permute-start.10 = (f32[2,16,512]{2,1,0:T(8,128)S(1)}, f32[2,16,512]{2,1,0:T(8,128)S(1)}, u32[]{:S(2)}, u32[]{:S(2)}) collective-permute-start(f32[2,16,512]{2,1,0:T(8,128)S(1)} %dynamic-slice_bitcast_fusion), channel_id=1, source_target_pairs={{0,1},{1,0},{2,3},{3,2},{4,5},{5,4},{6,7},{7,6},{8,9},{9,8},{10,11... | collective-permute-start | bytes 196616 | tf_op jit(solution)/shard_map/ppermute | solution.py:202
  27.1 2.7 %collective-permute-done.10 = f32[2,16,512]{2,1,0:T(8,128)S(1)} collective-permute-done((f32[2,16,512]{2,1,0:T(8,128)S(1)}, f32[2,16,512]{2,1,0:T(8,128)S(1)}, u32[]{:S(2)}, u32[]{:S(2)}) %collective-permute-start.10) | collective-permute-done | bytes 65568 | tf_op jit(solution)/shard_map/ppermute | solution.py:202
  29.8 2.8 %collective-permute-start.11 = (f32[16,512]{1,0:T(8,128)S(1)}, f32[16,512]{1,0:T(8,128)S(1)}, u32[]{:S(2)}, u32[]{:S(2)}) collective-permute-start(f32[16,512]{1,0:T(8,128)S(1)} %dynamic-slice_bitcast_fusion.1), channel_id=1, source_target_pairs={{0,2},{1,3},{2,0},{3,1},{4,6},{5,7},{6,4},{7,5},{8,10},{9,11},{10,... | collective-permute-start | bytes 98312 | tf_op jit(solution)/shard_map/ppermute | solution.py:202
  32.6 2.0 %collective-permute-done.11 = f32[16,512]{1,0:T(8,128)S(1)} collective-permute-done((f32[16,512]{1,0:T(8,128)S(1)}, f32[16,512]{1,0:T(8,128)S(1)}, u32[]{:S(2)}, u32[]{:S(2)}) %collective-permute-start.11) | collective-permute-done | bytes 32800 | tf_op jit(solution)/shard_map/ppermute | solution.py:202
  34.7 0.6 %bitcast_add_fusion.1 = f32[16,512]{1,0:T(8,128)} fusion(f32[16,512]{1,0:T(8,128)S(1)} %collective-permute-done.11, f32[2,16,512]{2,1,0:T(8,128)S(1)} %bitcast_add_fusion, s32[]{:T(128)S(6)} %select_n.32), kind=kLoop, calls=%fused_computation.3 | loop fusion | flops 8192 | bytes 98308 | tf_op jit(solution)/shard_map/add | solution.py:205
  (4 shorter events, 0.1 us)
Async XLA Ops:
  1.3 8.9 %collective-permute-start.1 = (bf16[14,64,128]{2,1,0:T(8,128)(2,1)S(1)}, bf16[14,64,128]{2,1,0:T(8,128)(2,1)S(1)}, u32[]{:S(2)}, u32[]{:S(2)}) collective-permute-start(bf16[14,64,128]{2,1,0:T(8,128)(2,1)S(1)} %get-tuple-element.14), channel_id=1, source_target_pairs={{0,8},{4,20},{8,0},{12,28},{16,24},{20,4},{24,16},{28,12},{1,9},{5... | collective-permute-start | bytes 688136 | tf_op jit(solution)/shard_map/ppermute | solution.py:150
  4.3 6.2 %collective-permute-start.2 = (bf16[14,64,128]{2,1,0:T(8,128)(2,1)S(1)}, bf16[14,64,128]{2,1,0:T(8,128)(2,1)S(1)}, u32[]{:S(2)}, u32[]{:S(2)}) collective-permute-start(bf16[14,64,128]{2,1,0:T(8,128)(2,1)S(1)} %get-tuple-element.15), channel_id=1, source_target_pairs={{0,16},{4,12},{8,24},{12,4},{16,0},{20,28},{24,8},{28,20},{1,17},{... | collective-permute-start | bytes 688136 | tf_op jit(solution)/shard_map/ppermute | solution.py:150
  5.8 9.5 %collective-permute-start = (bf16[5,64,512]{2,1,0:T(8,128)(2,1)S(1)}, bf16[5,64,512]{2,1,0:T(8,128)(2,1)S(1)}, u32[]{:S(2)}, u32[]{:S(2)}) collective-permute-start(bf16[5,64,512]{2,1,0:T(8,128)(2,1)S(1)} %get-tuple-element.13.refs_0_), channel_id=1, source_target_pairs={{0,4},{4,0},{8,12},{12,8},{16,20},{20,16},{24,28},{28,24},{1,5},{5... | collective-permute-start | bytes 983048 | tf_op jit(solution)/shard_map/ppermute | solution.py:147
  5.9 8.2 %collective-permute-start.3 = (bf16[8,64,128]{2,1,0:T(8,128)(2,1)S(1)}, bf16[8,64,128]{2,1,0:T(8,128)(2,1)S(1)}, u32[]{:S(2)}, u32[]{:S(2)}) collective-permute-start(bf16[8,64,128]{2,1,0:T(8,128)(2,1)S(1)} %get-tuple-element.16), channel_id=1, source_target_pairs={{0,24},{4,28},{8,16},{12,20},{16,8},{20,12},{24,0},{28,4},{1,25},{... | collective-permute-start | bytes 393224 | tf_op jit(solution)/shard_map/ppermute | solution.py:147
  10.2 5.2 %collective-permute-start.4 = (bf16[14,64,128]{2,1,0:T(8,128)(2,1)S(1)}, bf16[14,64,128]{2,1,0:T(8,128)(2,1)S(1)}, u32[]{:S(2)}, u32[]{:S(2)}) collective-permute-start(bf16[14,64,128]{2,1,0:T(8,128)(2,1)S(1)} %collective-permute-done.1.refs_2_), channel_id=1, source_target_pairs={{0,4},{4,0},{8,12},{12,8},{16,20},{20,16},{24,28},{28,24},{1,5},{5... | collective-permute-start | bytes 688136 | tf_op jit(solution)/shard_map/ppermute | solution.py:147
  10.5 4.8 %collective-permute-start.5 = (bf16[14,64,128]{2,1,0:T(8,128)(2,1)S(1)}, bf16[14,64,128]{2,1,0:T(8,128)(2,1)S(1)}, u32[]{:S(2)}, u32[]{:S(2)}) collective-permute-start(bf16[14,64,128]{2,1,0:T(8,128)(2,1)S(1)} %collective-permute-done.2.refs_3_), channel_id=1, source_target_pairs={{0,4},{4,0},{8,12},{12,8},{16,20},{20,16},{24,28},{28,24},{1,5},{5... | collective-permute-start | bytes 688136 | tf_op jit(solution)/shard_map/ppermute | solution.py:147
  14.0 1.3 %collective-permute-start.6 = (bf16[8,64,128]{2,1,0:T(8,128)(2,1)S(1)}, bf16[8,64,128]{2,1,0:T(8,128)(2,1)S(1)}, u32[]{:S(2)}, u32[]{:S(2)}) collective-permute-start(bf16[8,64,128]{2,1,0:T(8,128)(2,1)S(1)} %collective-permute-done.3.refs_4_), channel_id=1, source_target_pairs={{0,4},{4,0},{8,12},{12,8},{16,20},{20,16},{24,28},{28,24},{1,5},{5... | collective-permute-start | bytes 393224 | tf_op jit(solution)/shard_map/ppermute | solution.py:147
  17.2 4.9 %collective-permute-start.7 = (bf16[64,512]{1,0:T(8,128)(2,1)S(1)}, bf16[64,512]{1,0:T(8,128)(2,1)S(1)}, u32[]{:S(2)}, u32[]{:S(2)}) collective-permute-start(bf16[64,512]{1,0:T(8,128)(2,1)S(1)} %get-tuple-element.18), channel_id=1, source_target_pairs={{0,8},{4,20},{8,0},{12,28},{16,24},{20,4},{24,16},{28,12},{1,9},{5... | collective-permute-start | bytes 196616 | tf_op jit(solution)/shard_map/ppermute | solution.py:150
  18.9 4.3 %collective-permute-start.8 = (bf16[64,512]{1,0:T(8,128)(2,1)S(1)}, bf16[64,512]{1,0:T(8,128)(2,1)S(1)}, u32[]{:S(2)}, u32[]{:S(2)}) collective-permute-start(bf16[64,512]{1,0:T(8,128)(2,1)S(1)} %get-tuple-element.19), channel_id=1, source_target_pairs={{0,16},{4,12},{8,24},{12,4},{16,0},{20,28},{24,8},{28,20},{1,17},{... | collective-permute-start | bytes 196616 | tf_op jit(solution)/shard_map/ppermute | solution.py:150
  20.2 5.2 %collective-permute-start.9 = (bf16[64,512]{1,0:T(8,128)(2,1)S(1)}, bf16[64,512]{1,0:T(8,128)(2,1)S(1)}, u32[]{:S(2)}, u32[]{:S(2)}) collective-permute-start(bf16[64,512]{1,0:T(8,128)(2,1)S(1)} %get-tuple-element.20), channel_id=1, source_target_pairs={{0,24},{4,28},{8,16},{12,20},{16,8},{20,12},{24,0},{28,4},{1,25},{... | collective-permute-start | bytes 196616 | tf_op jit(solution)/shard_map/ppermute | solution.py:147
  25.4 4.3 %collective-permute-start.10 = (f32[2,16,512]{2,1,0:T(8,128)S(1)}, f32[2,16,512]{2,1,0:T(8,128)S(1)}, u32[]{:S(2)}, u32[]{:S(2)}) collective-permute-start(f32[2,16,512]{2,1,0:T(8,128)S(1)} %dynamic-slice_bitcast_fusion), channel_id=1, source_target_pairs={{0,1},{1,0},{2,3},{3,2},{4,5},{5,4},{6,7},{7,6},{8,9},{9,8},{10,11... | collective-permute-start | bytes 196616 | tf_op jit(solution)/shard_map/ppermute | solution.py:202
  29.8 4.9 %collective-permute-start.11 = (f32[16,512]{1,0:T(8,128)S(1)}, f32[16,512]{1,0:T(8,128)S(1)}, u32[]{:S(2)}, u32[]{:S(2)}) collective-permute-start(f32[16,512]{1,0:T(8,128)S(1)} %dynamic-slice_bitcast_fusion.1), channel_id=1, source_target_pairs={{0,2},{1,3},{2,0},{3,1},{4,6},{5,7},{6,4},{7,5},{8,10},{9,11},{10,... | collective-permute-start | bytes 98312 | tf_op jit(solution)/shard_map/ppermute | solution.py:202

commit v3 on v2

v3 whole, which is shorter than its diff:
```python
import jax
import jax.numpy as jnp
from jax import lax
from jax.experimental import pallas as pl
from jax.experimental.pallas import tpu as pltpu
from jax.sharding import PartitionSpec as P

BF = jnp.bfloat16
F32 = jnp.float32
BLK = 64
TILE = 2 * BLK
CHIPS = 4
GROUP = 4
NEAR = 13
FAR = 7


def expand_row(mask_ref, row, size):
    block = lax.broadcasted_iota(jnp.int32, (1, size), 1) // BLK
    line = jnp.zeros((1, size), F32)
    for j in range(size // BLK):
        line = jnp.where(block == j, mask_ref[row, j].astype(F32), line)
    return line.astype(BF)


def column(chip):
    return pl.ds(pl.multiple_of(chip * TILE, TILE), TILE)


def pack_kernel(
    b_hbm, d_hbm, pair_hbm, dens_hbm, own_ref, s1, s2, s3, pair_ref, dens_ref, d_ref, half_ref, line_ref, sems
):
    me = lax.axis_index("mu")
    c = me // 2
    k = me % 2
    size = d_ref.shape[1]
    copies = [
        pltpu.make_async_copy(pair_hbm, pair_ref, sems.at[0]),
        pltpu.make_async_copy(dens_hbm, dens_ref, sems.at[1]),
        pltpu.make_async_copy(d_hbm, d_ref, sems.at[2]),
    ]
    pieces = []
    for i, (send, d) in enumerate(((s1, 1 + k), (s2, 2 - k), (s3, 3))):
        first = (c ^ d) * GROUP
        pieces.append((send, 0, 2, first + 2 * k, c))
        pieces.append((half_ref, 2 * i, 2, first + 2 * (1 - k), c))
        if send is not s3:
            pieces.append((send, 3, GROUP, first, c ^ (3 - d)))
            pieces.append((send, 7, 2, first + 2 * (d - 1), c ^ 3))
    for i, (into, slot, count, first, chip) in enumerate(pieces):
        copies.append(
            pltpu.make_async_copy(
                b_hbm.at[pl.ds(first, count), :, column(chip)], into.at[pl.ds(slot, count)], sems.at[3 + i]
            )
        )
    copies.append(
        pltpu.make_async_copy(b_hbm.at[pl.ds(c * GROUP, GROUP)], own_ref.at[pl.ds(0, GROUP)], sems.at[3 + len(pieces)])
    )
    for copy in copies:
        copy.start()
    copies[0].wait()
    pair_line = expand_row(pair_ref, me, size)
    for j in range(CHIPS):
        line_ref[j] = pair_line[:, j * TILE : (j + 1) * TILE].astype(F32)
    copies[1].wait()
    dens_line = expand_row(dens_ref, me, size)
    copies[2].wait()
    dens = d_ref[...] * dens_line
    own_ref[GROUP] = dens
    for j in range(CHIPS):
        for send in (s1, s2, s3):
            send[send.shape[0] - CHIPS + j] = dens[:, j * TILE : (j + 1) * TILE]
    for copy, (into, slot, count, first, chip) in zip(copies[3:], pieces):
        copy.wait()
        line = line_ref[chip].astype(BF)
        for p in range(slot, slot + count):
            into[p] = into[p] * line
    for core in (0, 1):

        @pl.when(k == core)
        def _():
            for i, send in enumerate((s1, s2, s3)):
                left, right = (half_ref[2 * i + j][:, core * BLK : (core + 1) * BLK] for j in (0, 1))
                send[2] = jnp.concatenate([left, right], axis=1)

    copies[-1].wait()
    for p in range(GROUP):
        own_ref[p] = own_ref[p] * pair_line


def row_at(p, chip, core):
    return pl.ds(pl.multiple_of(p * 2 * CHIPS * BLK + chip * TILE + core * BLK, BLK), BLK)


def square(p, b0, b1):
    if p < 2:
        corner = b0[p].T[BLK:]
        return b0[p], jnp.concatenate([corner, b1[2][:, p * BLK : (p + 1) * BLK]], axis=1)
    corner = b1[p - 2].T[:BLK]
    return jnp.concatenate([b0[2][:, (p - 2) * BLK : (p - 1) * BLK], corner], axis=1), b1[p - 2]


def early_kernel(own_ref, mate_ref, r1, r2, q1, q2, t_ref, l_ref, x_ref, d_scr, l_scr):
    me = lax.axis_index("mu")
    c = me // 2
    k = me % 2
    size = t_ref.shape[1]
    cx, cy, cg = c ^ 1, c ^ 2, c ^ 3

    def fill(o0, o1, x0, y0, x1, y1):
        for core, own, x, y in ((0, o0, x0, y0), (1, o1, x1, y1)):
            d_scr[row_at(0, c, core), :] = own[GROUP]
            for r, ref in ((cx, x), (cy, y)):
                for j in range(CHIPS):
                    d_scr[row_at(0, r, core), j * TILE : (j + 1) * TILE] = ref[NEAR - CHIPS + j]
            d_scr[row_at(0, cg, core), :] = jnp.zeros((BLK, size), BF)
            for p in range(GROUP):
                t_ref[row_at(p, c, core), :] = own[p]
                t_ref[row_at(p, cx, core), column(cg)] = x[3 + p]
                t_ref[row_at(p, cy, core), column(cg)] = y[3 + p]
                t_ref[row_at(p, cg, core), column(cg)] = jnp.zeros((BLK, TILE), BF)
                if p < 2:
                    t_ref[row_at(p, cx, core), column(cy)] = x[7 + p]
                else:
                    t_ref[row_at(p, cy, core), column(cx)] = y[5 + p]
        for p in range(GROUP):
            for r, b0, b1 in ((cx, x0, x1), (cy, y0, y1)):
                top, low = square(p, b0, b1)
                t_ref[row_at(p, r, 0), column(r)] = top
                t_ref[row_at(p, r, 1), column(r)] = low
            tasks = [(c, dst, o0[p, :, column(dst)], o1[p, :, column(dst)]) for dst in (cx, cy, cg)]
            tasks.append((cx, cg, x0[3 + p], x1[3 + p]))
            tasks.append((cy, cg, y0[3 + p], y1[3 + p]))
            if p < 2:
                tasks.append((cx, cy, x0[7 + p], x1[7 + p]))
            else:
                tasks.append((cy, cx, y0[5 + p], y1[5 + p]))
            for src, dst, top, low in tasks:
                block = jnp.concatenate([top, low], axis=0).T
                t_ref[row_at(p, dst, 0), column(src)] = block[:BLK]
                t_ref[row_at(p, dst, 1), column(src)] = block[BLK:]

    @pl.when(k == 0)
    def _():
        fill(own_ref, mate_ref, r1, r2, q2, q1)

    @pl.when(k == 1)
    def _():
        fill(mate_ref, own_ref, q1, q2, r2, r1)

    for p in range(GROUP):
        for r in range(CHIPS):
            at = slice((p * CHIPS + r) * BLK, (p * CHIPS + r + 1) * BLK)
            l_scr[at, :] = t_ref[row_at(p, r, k), :]
            l_ref[at, :] = t_ref[row_at(p, r, k), column(cg)]
    x_ref[...] = jnp.dot(l_scr[...], d_scr[...], preferred_element_type=F32)


def late_kernel(t_ref, l_ref, xp_ref, r3, q3, e1, e2, e3, keep_ref, d_scr, l_scr, g_scr, x_scr, xg_scr, k_scr):
    me = lax.axis_index("mu")
    c = me // 2
    k = me % 2
    size = t_ref.shape[1]
    half = size // 2
    cg = c ^ 3

    def fill(g0, g1):
        for core, g in ((0, g0), (1, g1)):
            for j in range(CHIPS):
                d_scr[core * BLK : (core + 1) * BLK, j * TILE : (j + 1) * TILE] = g[FAR - CHIPS + j]
        for p in range(GROUP):
            top, low = square(p, g0, g1)
            g_scr[p * TILE : p * TILE + BLK, :] = top
            g_scr[p * TILE + BLK : (p + 1) * TILE, :] = low

    @pl.when(k == 0)
    def _():
        fill(r3, q3)

    @pl.when(k == 1)
    def _():
        fill(q3, r3)

    l_scr[...] = l_ref[...]
    for p in range(GROUP):
        at = pl.ds(pl.multiple_of((p * CHIPS + cg) * BLK, BLK), BLK)
        l_scr[at, :] = g_scr[pl.ds(pl.multiple_of(p * TILE + k * BLK, BLK), BLK), :]
    for p in range(GROUP):
        rest = jnp.dot(l_scr[p * half : (p + 1) * half, :], d_scr[...], preferred_element_type=F32)
        x_scr[:, p * size : (p + 1) * size] = (xp_ref[p * half : (p + 1) * half, :] + rest).astype(BF)
        xg_scr[:, p * TILE : (p + 1) * TILE] = x_scr[:, pl.ds(pl.multiple_of(p * size + cg * TILE, TILE), TILE)]
    k_scr[...] = jnp.dot(x_scr[...], t_ref[...], preferred_element_type=F32)
    k_scr[:, column(cg)] += jnp.dot(xg_scr[...], g_scr[...], preferred_element_type=F32)
    for out, d in ((e1, 1 + k), (e2, 2 - k), (e3, 3)):
        out[...] = k_scr[pl.ds(pl.multiple_of((c ^ d) * BLK, BLK), BLK), :].astype(BF)
    keep_ref[...] = k_scr[pl.ds(pl.multiple_of(c * BLK, BLK), BLK), :]


def spread(b_tensor, density, pair_mask, dens_mask):
    width, size = density.shape
    vmem = pl.BlockSpec(memory_space=pltpu.VMEM)
    hbm = pl.BlockSpec(memory_space=pl.ANY)

    def swap(x, step):
        return lax.ppermute(x, "mu", [(i, i ^ step) for i in range(2 * CHIPS)])

    def turn(x, first):
        return lax.ppermute(x, "mu", [(i, i ^ (2 if (i % 2 == 0) == first else 4)) for i in range(2 * CHIPS)])

    def around(x1, x2, x3):
        return turn(x1, True), turn(x2, False), swap(x3, 6)

    def slots(count):
        return jax.ShapeDtypeStruct((count, width, TILE), BF)

    own, *sends = pl.pallas_call(
        pack_kernel,
        out_shape=[jax.ShapeDtypeStruct((GROUP + 1, width, size), BF), slots(NEAR), slots(NEAR), slots(FAR)],
        in_specs=[hbm] * 4,
        out_specs=[vmem] * 4,
        scratch_shapes=[
            pltpu.SMEM(pair_mask.shape, jnp.int32),
            pltpu.SMEM(dens_mask.shape, jnp.int32),
            pltpu.VMEM(density.shape, BF),
            pltpu.VMEM((6, width, TILE), BF),
            pltpu.VMEM((CHIPS, 1, TILE), F32),
            pltpu.SemaphoreType.DMA((14,)),
        ],
        compiler_params=pltpu.CompilerParams(vmem_limit_bytes=16 << 20),
        name="pack",
    )(*(pltpu.with_memory_space_constraint(x, pltpu.HBM) for x in (b_tensor, density, pair_mask, dens_mask)))
    r1, r2, r3 = around(*sends)
    mate = swap(own, 1)
    q1, q2, q3 = swap(r1, 1), swap(r2, 1), swap(r3, 1)
    half = size // 2
    early = pl.pallas_call(
        early_kernel,
        out_shape=[
            jax.ShapeDtypeStruct((GROUP * size, size), BF),
            jax.ShapeDtypeStruct((GROUP * half, TILE), BF),
            jax.ShapeDtypeStruct((GROUP * half, size), F32),
        ],
        in_specs=[vmem] * 6,
        out_specs=[vmem] * 3,
        scratch_shapes=[pltpu.VMEM((size, size), BF), pltpu.VMEM((GROUP * half, size), BF)],
        compiler_params=pltpu.CompilerParams(vmem_limit_bytes=32 << 20),
        name="early",
    )(own, mate, r1, r2, q1, q2)
    chunk = jax.ShapeDtypeStruct((width, size), BF)
    *parts, keep = pl.pallas_call(
        late_kernel,
        out_shape=[chunk, chunk, chunk, jax.ShapeDtypeStruct((width, size), F32)],
        in_specs=[vmem] * 5,
        out_specs=[vmem] * 4,
        scratch_shapes=[
            pltpu.VMEM((TILE, size), BF),
            pltpu.VMEM((GROUP * half, TILE), BF),
            pltpu.VMEM((GROUP * TILE, TILE), BF),
            pltpu.VMEM((half, GROUP * size), BF),
            pltpu.VMEM((half, GROUP * TILE), BF),
            pltpu.VMEM((half, size), F32),
        ],
        compiler_params=pltpu.CompilerParams(vmem_limit_bytes=32 << 20),
        name="late",
    )(*early, r3, q3)
    y1, y2, y3 = around(*parts)
    plane = (((keep + y3.astype(F32)) + y1.astype(F32)) + y2.astype(F32))
    a = lax.axis_index("aux")
    strip = width // 4

    def strip_of(index):
        return lax.dynamic_slice_in_dim(plane, index * strip, strip, 0)

    def along(step):
        return lax.ppermute(strip_of(a ^ step), "aux", [(i, i ^ step) for i in range(4)])

    z1, z2, z3 = along(1), along(2), along(3)
    return ((strip_of(a) + z2) + z3) + z1


def gathered(b_tensor, density, pair_mask, dens_mask):
    depth, width, nbas = b_tensor.shape
    owner = lax.axis_index("mu")
    pair_row = lax.dynamic_slice_in_dim(pair_mask, owner, 1, 0)[0]
    dens_row = lax.dynamic_slice_in_dim(dens_mask, owner, 1, 0)[0]
    kept = b_tensor * jnp.repeat(pair_row, width).astype(BF)[None, None, :]
    dens_kept = density * jnp.repeat(dens_row, width).astype(BF)[None, :]
    summed = jnp.dot(
        kept.reshape(depth * width, nbas),
        lax.all_gather(dens_kept, "mu", axis=0, tiled=True),
        preferred_element_type=F32,
    )
    half_x = summed.astype(BF).reshape(depth, width, nbas)
    x_cols = lax.all_to_all(half_x, "mu", split_axis=2, concat_axis=1, tiled=True)
    partner = lax.all_to_all(kept, "mu", split_axis=2, concat_axis=1, tiled=True)
    return lax.psum_scatter(
        jnp.einsum("pms,pns->mn", x_cols, partner, preferred_element_type=F32),
        ("mu", "aux"),
        scatter_dimension=0,
        tiled=True,
    )


def solution(mesh):
    in_specs = (P("aux", "mu", None), P("mu", None), P(), P())
    out_specs = P(("mu", "aux"), None)

    def per_device(b_tensor, density, pair_mask, dens_mask):
        depth, width, size = b_tensor.shape
        fits = mesh.shape["mu"] == 2 * CHIPS and mesh.shape["aux"] == 4
        fits = fits and depth == GROUP * CHIPS and width == BLK and size == 2 * CHIPS * BLK
        step = spread if fits else gathered
        return step(b_tensor, density, pair_mask, dens_mask)

    return jax.shard_map(per_device, mesh=mesh, in_specs=in_specs, out_specs=out_specs, check_vma=False)
```

time: 35.5 us -> 32.7 us (0.921)
  waiting for transfers between devices: 18.2 us -> 14.7 us
  Pallas kernels: 3.14 us -> 4.03 us
    ppermute x4, starting transfers between devices: 7.53 us -> 5.55 us  [turn(): lax.ppermute(x, 'mu', [(i, i ^ (2 if (i % 2 == 0) == first else 4)) for i...]
    ppermute x6, waiting for transfers between devices: 6.39 us -> 4.44 us  [swap(): return lax.ppermute(x, 'mu', [(i, i ^ step) for i in range(2 * CHIPS)])]
    ppermute x6, starting transfers between devices: 1.22 us -> 2.97 us  [swap(): return lax.ppermute(x, 'mu', [(i, i ^ step) for i in range(2 * CHIPS)])]
    ppermute x4, waiting for transfers between devices: 7.08 us -> 6.17 us  [turn(): lax.ppermute(x, 'mu', [(i, i ^ (2 if (i % 2 == 0) == first else 4)) for i...]
    pallas_call x2 -> x3, Pallas kernels: 3.14 us -> 4.03 us  [the longest x1 1.41 us: spread(): pl.pallas_call(early_kernel, out_shape=[jax.ShapeDtypeStruct((GROUP * siz...]
    ppermute x2 -> x3, waiting for transfers between devices: 4.74 us -> 4.14 us  [along(): lax.ppermute(strip_of(a ^ step), 'aux', [(i, i ^ step) for i in range(4)])]
    ppermute x2 -> x3, starting transfers between devices: 4.47 us -> 4.46 us  [along(): lax.ppermute(strip_of(a ^ step), 'aux', [(i, i ^ step) for i in range(4)])]
  transfers between devices with their start and end apart: 12 -> 13, of which waited for: 9 -> 7; matrix products, arithmetic and copies ran while one was open for 0% -> 0% of each run, Pallas kernels for 0% -> 4%
where the time goes in v3:
time: 32.7 us; the launch traced here: 32.5 us
  waiting for transfers between devices  14.7 us (45%)
  starting transfers between devices  13 us (40%)
  Pallas kernels  4.03 us (12%)
  other arithmetic  0.66 us (2%)
    ppermute x4, waiting for transfers between devices, turn(): lax.ppermute(x, 'mu', [(i, i ^ (2 if (i % 2 == 0) == first else 4)) for i...  6.17 us
    ppermute x4, starting transfers between devices, turn(): lax.ppermute(x, 'mu', [(i, i ^ (2 if (i % 2 == 0) == first else 4)) for i...  5.55 us
    ppermute x3, starting transfers between devices, along(): lax.ppermute(strip_of(a ^ step), 'aux', [(i, i ^ step) for i in range(4)])  4.46 us
    ppermute x6, waiting for transfers between devices, swap(): return lax.ppermute(x, 'mu', [(i, i ^ step) for i in range(2 * CHIPS)])  4.44 us
    ppermute x3, waiting for transfers between devices, along(): lax.ppermute(strip_of(a ^ step), 'aux', [(i, i ^ step) for i in range(4)])  4.14 us
    ppermute x6, starting transfers between devices, swap(): return lax.ppermute(x, 'mu', [(i, i ^ step) for i in range(2 * CHIPS)])  2.97 us
    pallas_call x1, Pallas kernels, spread(): pl.pallas_call(early_kernel, out_shape=[jax.ShapeDtypeStruct((GROUP * siz...  1.41 us
    pallas_call x1, Pallas kernels, spread(): pl.pallas_call(pack_kernel, out_shape=[jax.ShapeDtypeStruct((GROUP + 1, w...  1.35 us
  transfers between devices with their start and end apart: 13, of which 7 were waited for; matrix products, arithmetic and copies ran while one was open for 0% of the time, Pallas kernels for 4%

profile of v3, /device:TPU:0, one launch (start us, length us, event | category | flops | bytes accessed | tf_op | source)
XLA Modules:
  0.0 32.5 jit_solution(3977204044662749585)
XLA Ops:
  0.0 1.3 %pack.1 = (bf16[5,64,512]{2,1,0:T(8,128)(2,1)S(1)}, bf16[13,64,128]{2,1,0:T(8,128)(2,1)S(1)}, bf16[13,64,128]{2,1,0:T(8,128)(2,1)S(1)}, bf16[7,64,128]{2,1,0:T(8,128)(2,1)S(1)}) custom-call(bf16[16,64,512]{2,1,0:T(8,128)(2,1)} %b_hbm.1, bf16[64,512]{1,0:T(8,128)(2,1)} %d_hbm.1, s32[8,8]{1,0:T(8,128)} %pair_hbm.1, s32[8,8]{1,0:T(8,128)} %dens_hbm.1), custom_call_target="tpu_custom_call" | custom-call | tf_op jit(solution)/shard_map/pack/pallas_call | solution.py:216
  1.4 3.0 %collective-permute-start.1 = (bf16[13,64,128]{2,1,0:T(8,128)(2,1)S(1)}, bf16[13,64,128]{2,1,0:T(8,128)(2,1)S(1)}, u32[]{:S(2)}, u32[]{:S(2)}) collective-permute-start(bf16[13,64,128]{2,1,0:T(8,128)(2,1)S(1)} %get-tuple-element.17), channel_id=1, source_target_pairs={{0,8},{4,20},{8,0},{12,28},{16,24},{20,4},{24,16},{28,12},{1,9},{5... | collective-permute-start | bytes 638984 | tf_op jit(solution)/shard_map/ppermute | solution.py:208
  4.4 1.5 %collective-permute-start.2 = (bf16[13,64,128]{2,1,0:T(8,128)(2,1)S(1)}, bf16[13,64,128]{2,1,0:T(8,128)(2,1)S(1)}, u32[]{:S(2)}, u32[]{:S(2)}) collective-permute-start(bf16[13,64,128]{2,1,0:T(8,128)(2,1)S(1)} %get-tuple-element.18), channel_id=1, source_target_pairs={{0,16},{4,12},{8,24},{12,4},{16,0},{20,28},{24,8},{28,20},{1,17},{... | collective-permute-start | bytes 638984 | tf_op jit(solution)/shard_map/ppermute | solution.py:208
  5.9 0.0 collective-permute-start
  5.9 0.0 collective-permute-start.5
  5.9 4.0 %collective-permute-done.1.r1 = bf16[13,64,128]{2,1,0:T(8,128)(2,1)S(1)} collective-permute-done((bf16[13,64,128]{2,1,0:T(8,128)(2,1)S(1)}, bf16[13,64,128]{2,1,0:T(8,128)(2,1)S(1)}, u32[]{:S(2)}, u32[]{:S(2)}) %collective-permute-start.1) | collective-permute-done | bytes 213024 | tf_op jit(solution)/shard_map/ppermute | solution.py:208
  9.9 0.0 collective-permute-start.3
  9.9 0.6 %collective-permute-done.2.r2 = bf16[13,64,128]{2,1,0:T(8,128)(2,1)S(1)} collective-permute-done((bf16[13,64,128]{2,1,0:T(8,128)(2,1)S(1)}, bf16[13,64,128]{2,1,0:T(8,128)(2,1)S(1)}, u32[]{:S(2)}, u32[]{:S(2)}) %collective-permute-start.2) | collective-permute-done | bytes 213024 | tf_op jit(solution)/shard_map/ppermute | solution.py:208
  10.5 0.4 %collective-permute-start.4 = (bf16[13,64,128]{2,1,0:T(8,128)(2,1)S(1)}, bf16[13,64,128]{2,1,0:T(8,128)(2,1)S(1)}, u32[]{:S(2)}, u32[]{:S(2)}) collective-permute-start(bf16[13,64,128]{2,1,0:T(8,128)(2,1)S(1)} %collective-permute-done.2.r2), channel_id=1, source_target_pairs={{0,4},{4,0},{8,12},{12,8},{16,20},{20,16},{24,28},{28,24},{1,5},{5... | collective-permute-start | bytes 638984 | tf_op jit(solution)/shard_map/ppermute | solution.py:205
  10.9 2.5 %collective-permute-done.5.r3 = bf16[7,64,128]{2,1,0:T(8,128)(2,1)S(1)} collective-permute-done((bf16[7,64,128]{2,1,0:T(8,128)(2,1)S(1)}, bf16[7,64,128]{2,1,0:T(8,128)(2,1)S(1)}, u32[]{:S(2)}, u32[]{:S(2)}) %collective-permute-start.5) | collective-permute-done | bytes 114720 | tf_op jit(solution)/shard_map/ppermute | solution.py:205
  13.4 0.0 collective-permute-start.6
  13.4 0.0 collective-permute-done.mate_ref
  13.4 0.0 collective-permute-done.3.q1
  13.4 0.0 collective-permute-done.4.q2
  13.4 1.4 %early.1 = (bf16[2048,512]{1,0:T(8,128)(2,1)S(1)}, bf16[1024,128]{1,0:T(8,128)(2,1)S(1)}, f32[1024,512]{1,0:T(8,128)S(1)}) custom-call(bf16[5,64,512]{2,1,0:T(8,128)(2,1)S(1)} %get-tuple-element.16.own_ref, bf16[5,64,512]{2,1,0:T(8,128)(2,1)S(1)} %collective-permute-done.mate_ref, bf16[13,64,128]{2,1,0:T(8,128)(2,1)S(1)} %collective-permute-done.1.r1, ...), custom_call_target="tpu_custom_call" | custom-call | tf_op jit(solution)/shard_map/early/pallas_call | solution.py:236
  14.8 0.0 collective-permute-done.6.q3
  14.8 1.3 %late.1 = (bf16[64,512]{1,0:T(8,128)(2,1)S(1)}, bf16[64,512]{1,0:T(8,128)(2,1)S(1)}, bf16[64,512]{1,0:T(8,128)(2,1)S(1)}, f32[64,512]{1,0:T(8,128)S(1)}) custom-call(bf16[2048,512]{1,0:T(8,128)(2,1)S(1)} %get-tuple-element.19.t_ref, bf16[1024,128]{1,0:T(8,128)(2,1)S(1)} %get-tuple-element.20.l_ref, f32[1024,512]{1,0:T(8,128)S(1)} %get-tuple-element.21.xp_ref, ...), custom_call_target="tpu_custom_call" | custom-call | tf_op jit(solution)/shard_map/late/pallas_call | solution.py:250
  16.1 2.5 %collective-permute-start.7 = (bf16[64,512]{1,0:T(8,128)(2,1)S(1)}, bf16[64,512]{1,0:T(8,128)(2,1)S(1)}, u32[]{:S(2)}, u32[]{:S(2)}) collective-permute-start(bf16[64,512]{1,0:T(8,128)(2,1)S(1)} %get-tuple-element.24), channel_id=1, source_target_pairs={{0,24},{4,28},{8,16},{12,20},{16,8},{20,12},{24,0},{28,4},{1,25},{... | collective-permute-start | bytes 196616 | tf_op jit(solution)/shard_map/ppermute | solution.py:205
  18.6 0.0 collective-permute-start.8
  18.6 1.0 %collective-permute-start.9 = (bf16[64,512]{1,0:T(8,128)(2,1)S(1)}, bf16[64,512]{1,0:T(8,128)(2,1)S(1)}, u32[]{:S(2)}, u32[]{:S(2)}) collective-permute-start(bf16[64,512]{1,0:T(8,128)(2,1)S(1)} %get-tuple-element.26), channel_id=1, source_target_pairs={{0,16},{4,12},{8,24},{12,4},{16,0},{20,28},{24,8},{28,20},{1,17},{... | collective-permute-start | bytes 196616 | tf_op jit(solution)/shard_map/ppermute | solution.py:208
  19.6 1.9 %collective-permute-done.7 = bf16[64,512]{1,0:T(8,128)(2,1)S(1)} collective-permute-done((bf16[64,512]{1,0:T(8,128)(2,1)S(1)}, bf16[64,512]{1,0:T(8,128)(2,1)S(1)}, u32[]{:S(2)}, u32[]{:S(2)}) %collective-permute-start.7) | collective-permute-done | bytes 65568 | tf_op jit(solution)/shard_map/ppermute | solution.py:205
  21.6 1.6 %collective-permute-done.8 = bf16[64,512]{1,0:T(8,128)(2,1)S(1)} collective-permute-done((bf16[64,512]{1,0:T(8,128)(2,1)S(1)}, bf16[64,512]{1,0:T(8,128)(2,1)S(1)}, u32[]{:S(2)}, u32[]{:S(2)}) %collective-permute-start.8) | collective-permute-done | bytes 65568 | tf_op jit(solution)/shard_map/ppermute | solution.py:208
  23.2 0.0 collective-permute-done.9
  23.3 2.9 %collective-permute-start.10 = (f32[16,512]{1,0:T(8,128)S(1)}, f32[16,512]{1,0:T(8,128)S(1)}, u32[]{:S(2)}, u32[]{:S(2)}) collective-permute-start(f32[16,512]{1,0:T(8,128)S(1)} %get-tuple-element.27), channel_id=1, source_target_pairs={{0,2},{1,3},{2,0},{3,1},{4,6},{5,7},{6,4},{7,5},{8,10},{9,11},{10,... | collective-permute-start | bytes 98312 | tf_op jit(solution)/shard_map/ppermute | solution.py:275
  26.1 1.3 %collective-permute-start.11 = (f32[16,512]{1,0:T(8,128)S(1)}, f32[16,512]{1,0:T(8,128)S(1)}, u32[]{:S(2)}, u32[]{:S(2)}) collective-permute-start(f32[16,512]{1,0:T(8,128)S(1)} %get-tuple-element.29), channel_id=1, source_target_pairs={{0,3},{1,2},{2,1},{3,0},{4,7},{5,6},{6,5},{7,4},{8,11},{9,10},{10,... | collective-permute-start | bytes 98312 | tf_op jit(solution)/shard_map/ppermute | solution.py:275
  27.5 0.2 collective-permute-start.12
  27.7 0.6 %collective-permute-done.10 = f32[16,512]{1,0:T(8,128)S(1)} collective-permute-done((f32[16,512]{1,0:T(8,128)S(1)}, f32[16,512]{1,0:T(8,128)S(1)}, u32[]{:S(2)}, u32[]{:S(2)}) %collective-permute-start.10) | collective-permute-done | bytes 32800 | tf_op jit(solution)/shard_map/ppermute | solution.py:275
  28.3 3.5 %collective-permute-done.11 = f32[16,512]{1,0:T(8,128)S(1)} collective-permute-done((f32[16,512]{1,0:T(8,128)S(1)}, f32[16,512]{1,0:T(8,128)S(1)}, u32[]{:S(2)}, u32[]{:S(2)}) %collective-permute-start.11) | collective-permute-done | bytes 32800 | tf_op jit(solution)/shard_map/ppermute | solution.py:275
  31.9 0.0 collective-permute-done.12
  31.9 0.6 %add_add_fusion = f32[16,512]{1,0:T(8,128)} fusion(f32[16,512]{1,0:T(8,128)S(1)} %collective-permute-done.12, f32[16,512]{1,0:T(8,128)S(1)} %collective-permute-done.11, f32[16,512]{1,0:T(8,128)S(1)} %collective-permute-done.10, f32[64,512]{1,0:T(8,128)S(1)} %convert_add_fusion, s32[]{:T(128)S(6)} %select_n.12), kind=kLoop, calls=%fused_computation.1 | loop fusion | flops 24576 | bytes 163844 | tf_op jit(solution)/shard_map/add | solution.py:278
  (2 shorter events, 0.0 us)
Async XLA Ops:
  1.4 8.5 %collective-permute-start.1 = (bf16[13,64,128]{2,1,0:T(8,128)(2,1)S(1)}, bf16[13,64,128]{2,1,0:T(8,128)(2,1)S(1)}, u32[]{:S(2)}, u32[]{:S(2)}) collective-permute-start(bf16[13,64,128]{2,1,0:T(8,128)(2,1)S(1)} %get-tuple-element.17), channel_id=1, source_target_pairs={{0,8},{4,20},{8,0},{12,28},{16,24},{20,4},{24,16},{28,12},{1,9},{5... | collective-permute-start | bytes 638984 | tf_op jit(solution)/shard_map/ppermute | solution.py:208
  4.4 6.1 %collective-permute-start.2 = (bf16[13,64,128]{2,1,0:T(8,128)(2,1)S(1)}, bf16[13,64,128]{2,1,0:T(8,128)(2,1)S(1)}, u32[]{:S(2)}, u32[]{:S(2)}) collective-permute-start(bf16[13,64,128]{2,1,0:T(8,128)(2,1)S(1)} %get-tuple-element.18), channel_id=1, source_target_pairs={{0,16},{4,12},{8,24},{12,4},{16,0},{20,28},{24,8},{28,20},{1,17},{... | collective-permute-start | bytes 638984 | tf_op jit(solution)/shard_map/ppermute | solution.py:208
  5.9 7.5 %collective-permute-start = (bf16[5,64,512]{2,1,0:T(8,128)(2,1)S(1)}, bf16[5,64,512]{2,1,0:T(8,128)(2,1)S(1)}, u32[]{:S(2)}, u32[]{:S(2)}) collective-permute-start(bf16[5,64,512]{2,1,0:T(8,128)(2,1)S(1)} %get-tuple-element.16.own_ref), channel_id=1, source_target_pairs={{0,4},{4,0},{8,12},{12,8},{16,20},{20,16},{24,28},{28,24},{1,5},{5... | collective-permute-start | bytes 983048 | tf_op jit(solution)/shard_map/ppermute | solution.py:205
  5.9 7.5 %collective-permute-start.5 = (bf16[7,64,128]{2,1,0:T(8,128)(2,1)S(1)}, bf16[7,64,128]{2,1,0:T(8,128)(2,1)S(1)}, u32[]{:S(2)}, u32[]{:S(2)}) collective-permute-start(bf16[7,64,128]{2,1,0:T(8,128)(2,1)S(1)} %get-tuple-element.22), channel_id=1, source_target_pairs={{0,24},{4,28},{8,16},{12,20},{16,8},{20,12},{24,0},{28,4},{1,25},{... | collective-permute-start | bytes 344072 | tf_op jit(solution)/shard_map/ppermute | solution.py:205
  9.9 3.5 %collective-permute-start.3 = (bf16[13,64,128]{2,1,0:T(8,128)(2,1)S(1)}, bf16[13,64,128]{2,1,0:T(8,128)(2,1)S(1)}, u32[]{:S(2)}, u32[]{:S(2)}) collective-permute-start(bf16[13,64,128]{2,1,0:T(8,128)(2,1)S(1)} %collective-permute-done.1.r1), channel_id=1, source_target_pairs={{0,4},{4,0},{8,12},{12,8},{16,20},{20,16},{24,28},{28,24},{1,5},{5... | collective-permute-start | bytes 638984 | tf_op jit(solution)/shard_map/ppermute | solution.py:205
  10.5 2.9 %collective-permute-start.4 = (bf16[13,64,128]{2,1,0:T(8,128)(2,1)S(1)}, bf16[13,64,128]{2,1,0:T(8,128)(2,1)S(1)}, u32[]{:S(2)}, u32[]{:S(2)}) collective-permute-start(bf16[13,64,128]{2,1,0:T(8,128)(2,1)S(1)} %collective-permute-done.2.r2), channel_id=1, source_target_pairs={{0,4},{4,0},{8,12},{12,8},{16,20},{20,16},{24,28},{28,24},{1,5},{5... | collective-permute-start | bytes 638984 | tf_op jit(solution)/shard_map/ppermute | solution.py:205
  13.4 1.4 %collective-permute-start.6 = (bf16[7,64,128]{2,1,0:T(8,128)(2,1)S(1)}, bf16[7,64,128]{2,1,0:T(8,128)(2,1)S(1)}, u32[]{:S(2)}, u32[]{:S(2)}) collective-permute-start(bf16[7,64,128]{2,1,0:T(8,128)(2,1)S(1)} %collective-permute-done.5.r3), channel_id=1, source_target_pairs={{0,4},{4,0},{8,12},{12,8},{16,20},{20,16},{24,28},{28,24},{1,5},{5... | collective-permute-start | bytes 344072 | tf_op jit(solution)/shard_map/ppermute | solution.py:205
  16.1 5.5 %collective-permute-start.7 = (bf16[64,512]{1,0:T(8,128)(2,1)S(1)}, bf16[64,512]{1,0:T(8,128)(2,1)S(1)}, u32[]{:S(2)}, u32[]{:S(2)}) collective-permute-start(bf16[64,512]{1,0:T(8,128)(2,1)S(1)} %get-tuple-element.24), channel_id=1, source_target_pairs={{0,24},{4,28},{8,16},{12,20},{16,8},{20,12},{24,0},{28,4},{1,25},{... | collective-permute-start | bytes 196616 | tf_op jit(solution)/shard_map/ppermute | solution.py:205
  18.6 4.6 %collective-permute-start.8 = (bf16[64,512]{1,0:T(8,128)(2,1)S(1)}, bf16[64,512]{1,0:T(8,128)(2,1)S(1)}, u32[]{:S(2)}, u32[]{:S(2)}) collective-permute-start(bf16[64,512]{1,0:T(8,128)(2,1)S(1)} %get-tuple-element.25), channel_id=1, source_target_pairs={{0,8},{4,20},{8,0},{12,28},{16,24},{20,4},{24,16},{28,12},{1,9},{5... | collective-permute-start | bytes 196616 | tf_op jit(solution)/shard_map/ppermute | solution.py:208
  18.6 4.6 %collective-permute-start.9 = (bf16[64,512]{1,0:T(8,128)(2,1)S(1)}, bf16[64,512]{1,0:T(8,128)(2,1)S(1)}, u32[]{:S(2)}, u32[]{:S(2)}) collective-permute-start(bf16[64,512]{1,0:T(8,128)(2,1)S(1)} %get-tuple-element.26), channel_id=1, source_target_pairs={{0,16},{4,12},{8,24},{12,4},{16,0},{20,28},{24,8},{28,20},{1,17},{... | collective-permute-start | bytes 196616 | tf_op jit(solution)/shard_map/ppermute | solution.py:208
  23.3 5.1 %collective-permute-start.10 = (f32[16,512]{1,0:T(8,128)S(1)}, f32[16,512]{1,0:T(8,128)S(1)}, u32[]{:S(2)}, u32[]{:S(2)}) collective-permute-start(f32[16,512]{1,0:T(8,128)S(1)} %get-tuple-element.27), channel_id=1, source_target_pairs={{0,2},{1,3},{2,0},{3,1},{4,6},{5,7},{6,4},{7,5},{8,10},{9,11},{10,... | collective-permute-start | bytes 98312 | tf_op jit(solution)/shard_map/ppermute | solution.py:275
  26.1 5.7 %collective-permute-start.11 = (f32[16,512]{1,0:T(8,128)S(1)}, f32[16,512]{1,0:T(8,128)S(1)}, u32[]{:S(2)}, u32[]{:S(2)}) collective-permute-start(f32[16,512]{1,0:T(8,128)S(1)} %get-tuple-element.29), channel_id=1, source_target_pairs={{0,3},{1,2},{2,1},{3,0},{4,7},{5,6},{6,5},{7,4},{8,11},{9,10},{10,... | collective-permute-start | bytes 98312 | tf_op jit(solution)/shard_map/ppermute | solution.py:275
  27.5 4.4 %collective-permute-start.12 = (f32[16,512]{1,0:T(8,128)S(1)}, f32[16,512]{1,0:T(8,128)S(1)}, u32[]{:S(2)}, u32[]{:S(2)}) collective-permute-start(f32[16,512]{1,0:T(8,128)S(1)} %get-tuple-element.28), channel_id=1, source_target_pairs={{0,1},{1,0},{2,3},{3,2},{4,5},{5,4},{6,7},{7,6},{8,9},{9,8},{10,11... | collective-permute-start | bytes 98312 | tf_op jit(solution)/shard_map/ppermute | solution.py:275

commit v4 on v3

--- a/solution.py
+++ b/solution.py
@@ -11,6 +11,7 @@
 TILE = 2 * BLK
 CHIPS = 4
 GROUP = 4
+STEPS = ((2, 3, 1, 0), (3, 2, 0, 1), (1, 0, 3, 2))
 NEAR = 13
 FAR = 7
 
@@ -271,11 +272,11 @@
     def strip_of(index):
         return lax.dynamic_slice_in_dim(plane, index * strip, strip, 0)
 
-    def along(step):
-        return lax.ppermute(strip_of(a ^ step), "aux", [(i, i ^ step) for i in range(4)])
-
-    z1, z2, z3 = along(1), along(2), along(3)
-    return ((strip_of(a) + z2) + z3) + z1
+    total = strip_of(a)
+    for step in STEPS:
+        to = sum(jnp.where(a == i, j, 0) for i, j in enumerate(step))
+        total = total + lax.ppermute(strip_of(to), "aux", list(enumerate(step)))
+    return total
 
 
 def gathered(b_tensor, density, pair_mask, dens_mask):

time: 32.7 us -> 32.1 us (0.982)
  waiting for transfers between devices: 14.7 us -> 14.2 us
    ppermute x3, waiting for transfers between devices: 4.14 us -> 3.59 us  [spread(): total = total + lax.ppermute(strip_of(to), 'aux', list(enumerate(step)))]
  transfers between devices with their start and end apart: 13 -> 13, of which waited for: 7 -> 8; matrix products, arithmetic and copies ran while one was open for 0% -> 0% of each run, Pallas kernels for 4% -> 4%
where the time goes in v4:
time: 32.1 us; the launch traced here: 31.9 us
  waiting for transfers between devices  14.2 us (44%)
  starting transfers between devices  13 us (40%)
  Pallas kernels  4.03 us (13%)
  other arithmetic  0.65 us (2%)
    ppermute x4, waiting for transfers between devices, turn(): lax.ppermute(x, 'mu', [(i, i ^ (2 if (i % 2 == 0) == first else 4)) for i...  6.17 us
    ppermute x4, starting transfers between devices, turn(): lax.ppermute(x, 'mu', [(i, i ^ (2 if (i % 2 == 0) == first else 4)) for i...  5.55 us
    ppermute x3, starting transfers between devices, spread(): total = total + lax.ppermute(strip_of(to), 'aux', list(enumerate(step)))  4.45 us
    ppermute x6, waiting for transfers between devices, swap(): return lax.ppermute(x, 'mu', [(i, i ^ step) for i in range(2 * CHIPS)])  4.44 us
    ppermute x3, waiting for transfers between devices, spread(): total = total + lax.ppermute(strip_of(to), 'aux', list(enumerate(step)))  3.59 us
    ppermute x6, starting transfers between devices, swap(): return lax.ppermute(x, 'mu', [(i, i ^ step) for i in range(2 * CHIPS)])  2.97 us
    pallas_call x1, Pallas kernels, spread(): pl.pallas_call(early_kernel, out_shape=[jax.ShapeDtypeStruct((GROUP * siz...  1.41 us
    pallas_call x1, Pallas kernels, spread(): pl.pallas_call(pack_kernel, out_shape=[jax.ShapeDtypeStruct((GROUP + 1, w...  1.35 us
  transfers between devices with their start and end apart: 13, of which 8 were waited for; matrix products, arithmetic and copies ran while one was open for 0% of the time, Pallas kernels for 4%

profile of v4, /device:TPU:0, one launch (start us, length us, event | category | flops | bytes accessed | tf_op | source)
XLA Modules:
  0.0 31.9 jit_solution(3678592908041715777)
XLA Ops:
  0.0 1.3 %pack.1 = (bf16[5,64,512]{2,1,0:T(8,128)(2,1)S(1)}, bf16[13,64,128]{2,1,0:T(8,128)(2,1)S(1)}, bf16[13,64,128]{2,1,0:T(8,128)(2,1)S(1)}, bf16[7,64,128]{2,1,0:T(8,128)(2,1)S(1)}) custom-call(bf16[16,64,512]{2,1,0:T(8,128)(2,1)} %b_hbm.1, bf16[64,512]{1,0:T(8,128)(2,1)} %d_hbm.1, s32[8,8]{1,0:T(8,128)} %pair_hbm.1, s32[8,8]{1,0:T(8,128)} %dens_hbm.1), custom_call_target="tpu_custom_call" | custom-call | tf_op jit(solution)/shard_map/pack/pallas_call | solution.py:217
  1.4 3.0 %collective-permute-start.1 = (bf16[13,64,128]{2,1,0:T(8,128)(2,1)S(1)}, bf16[13,64,128]{2,1,0:T(8,128)(2,1)S(1)}, u32[]{:S(2)}, u32[]{:S(2)}) collective-permute-start(bf16[13,64,128]{2,1,0:T(8,128)(2,1)S(1)} %get-tuple-element.17), channel_id=1, source_target_pairs={{0,8},{4,20},{8,0},{12,28},{16,24},{20,4},{24,16},{28,12},{1,9},{5... | collective-permute-start | bytes 638984 | tf_op jit(solution)/shard_map/ppermute | solution.py:209
  4.4 1.5 %collective-permute-start.2 = (bf16[13,64,128]{2,1,0:T(8,128)(2,1)S(1)}, bf16[13,64,128]{2,1,0:T(8,128)(2,1)S(1)}, u32[]{:S(2)}, u32[]{:S(2)}) collective-permute-start(bf16[13,64,128]{2,1,0:T(8,128)(2,1)S(1)} %get-tuple-element.18), channel_id=1, source_target_pairs={{0,16},{4,12},{8,24},{12,4},{16,0},{20,28},{24,8},{28,20},{1,17},{... | collective-permute-start | bytes 638984 | tf_op jit(solution)/shard_map/ppermute | solution.py:209
  5.9 0.0 collective-permute-start
  5.9 0.0 collective-permute-start.5
  5.9 4.0 %collective-permute-done.1.r1 = bf16[13,64,128]{2,1,0:T(8,128)(2,1)S(1)} collective-permute-done((bf16[13,64,128]{2,1,0:T(8,128)(2,1)S(1)}, bf16[13,64,128]{2,1,0:T(8,128)(2,1)S(1)}, u32[]{:S(2)}, u32[]{:S(2)}) %collective-permute-start.1) | collective-permute-done | bytes 213024 | tf_op jit(solution)/shard_map/ppermute | solution.py:209
  9.9 0.0 collective-permute-start.3
  9.9 0.6 %collective-permute-done.2.r2 = bf16[13,64,128]{2,1,0:T(8,128)(2,1)S(1)} collective-permute-done((bf16[13,64,128]{2,1,0:T(8,128)(2,1)S(1)}, bf16[13,64,128]{2,1,0:T(8,128)(2,1)S(1)}, u32[]{:S(2)}, u32[]{:S(2)}) %collective-permute-start.2) | collective-permute-done | bytes 213024 | tf_op jit(solution)/shard_map/ppermute | solution.py:209
  10.5 0.4 %collective-permute-start.4 = (bf16[13,64,128]{2,1,0:T(8,128)(2,1)S(1)}, bf16[13,64,128]{2,1,0:T(8,128)(2,1)S(1)}, u32[]{:S(2)}, u32[]{:S(2)}) collective-permute-start(bf16[13,64,128]{2,1,0:T(8,128)(2,1)S(1)} %collective-permute-done.2.r2), channel_id=1, source_target_pairs={{0,4},{4,0},{8,12},{12,8},{16,20},{20,16},{24,28},{28,24},{1,5},{5... | collective-permute-start | bytes 638984 | tf_op jit(solution)/shard_map/ppermute | solution.py:206
  10.9 2.5 %collective-permute-done.5.r3 = bf16[7,64,128]{2,1,0:T(8,128)(2,1)S(1)} collective-permute-done((bf16[7,64,128]{2,1,0:T(8,128)(2,1)S(1)}, bf16[7,64,128]{2,1,0:T(8,128)(2,1)S(1)}, u32[]{:S(2)}, u32[]{:S(2)}) %collective-permute-start.5) | collective-permute-done | bytes 114720 | tf_op jit(solution)/shard_map/ppermute | solution.py:206
  13.4 0.0 collective-permute-start.6
  13.4 0.0 collective-permute-done.mate_ref
  13.4 0.0 collective-permute-done.3.q1
  13.4 0.0 collective-permute-done.4.q2
  13.4 1.4 %early.1 = (bf16[2048,512]{1,0:T(8,128)(2,1)S(1)}, bf16[1024,128]{1,0:T(8,128)(2,1)S(1)}, f32[1024,512]{1,0:T(8,128)S(1)}) custom-call(bf16[5,64,512]{2,1,0:T(8,128)(2,1)S(1)} %get-tuple-element.16.own_ref, bf16[5,64,512]{2,1,0:T(8,128)(2,1)S(1)} %collective-permute-done.mate_ref, bf16[13,64,128]{2,1,0:T(8,128)(2,1)S(1)} %collective-permute-done.1.r1, ...), custom_call_target="tpu_custom_call" | custom-call | tf_op jit(solution)/shard_map/early/pallas_call | solution.py:237
  14.8 0.0 collective-permute-done.6.q3
  14.8 1.3 %late.1 = (bf16[64,512]{1,0:T(8,128)(2,1)S(1)}, bf16[64,512]{1,0:T(8,128)(2,1)S(1)}, bf16[64,512]{1,0:T(8,128)(2,1)S(1)}, f32[64,512]{1,0:T(8,128)S(1)}) custom-call(bf16[2048,512]{1,0:T(8,128)(2,1)S(1)} %get-tuple-element.19.t_ref, bf16[1024,128]{1,0:T(8,128)(2,1)S(1)} %get-tuple-element.20.l_ref, f32[1024,512]{1,0:T(8,128)S(1)} %get-tuple-element.21.xp_ref, ...), custom_call_target="tpu_custom_call" | custom-call | tf_op jit(solution)/shard_map/late/pallas_call | solution.py:251
  16.1 2.5 %collective-permute-start.7 = (bf16[64,512]{1,0:T(8,128)(2,1)S(1)}, bf16[64,512]{1,0:T(8,128)(2,1)S(1)}, u32[]{:S(2)}, u32[]{:S(2)}) collective-permute-start(bf16[64,512]{1,0:T(8,128)(2,1)S(1)} %get-tuple-element.24), channel_id=1, source_target_pairs={{0,24},{4,28},{8,16},{12,20},{16,8},{20,12},{24,0},{28,4},{1,25},{... | collective-permute-start | bytes 196616 | tf_op jit(solution)/shard_map/ppermute | solution.py:206
  18.6 0.0 collective-permute-start.8
  18.6 1.0 %collective-permute-start.9 = (bf16[64,512]{1,0:T(8,128)(2,1)S(1)}, bf16[64,512]{1,0:T(8,128)(2,1)S(1)}, u32[]{:S(2)}, u32[]{:S(2)}) collective-permute-start(bf16[64,512]{1,0:T(8,128)(2,1)S(1)} %get-tuple-element.26), channel_id=1, source_target_pairs={{0,16},{4,12},{8,24},{12,4},{16,0},{20,28},{24,8},{28,20},{1,17},{... | collective-permute-start | bytes 196616 | tf_op jit(solution)/shard_map/ppermute | solution.py:209
  19.6 1.9 %collective-permute-done.7 = bf16[64,512]{1,0:T(8,128)(2,1)S(1)} collective-permute-done((bf16[64,512]{1,0:T(8,128)(2,1)S(1)}, bf16[64,512]{1,0:T(8,128)(2,1)S(1)}, u32[]{:S(2)}, u32[]{:S(2)}) %collective-permute-start.7) | collective-permute-done | bytes 65568 | tf_op jit(solution)/shard_map/ppermute | solution.py:206
  21.6 1.6 %collective-permute-done.8 = bf16[64,512]{1,0:T(8,128)(2,1)S(1)} collective-permute-done((bf16[64,512]{1,0:T(8,128)(2,1)S(1)}, bf16[64,512]{1,0:T(8,128)(2,1)S(1)}, u32[]{:S(2)}, u32[]{:S(2)}) %collective-permute-start.8) | collective-permute-done | bytes 65568 | tf_op jit(solution)/shard_map/ppermute | solution.py:209
  23.2 0.0 collective-permute-done.9
  23.3 2.9 %collective-permute-start.10 = (f32[16,512]{1,0:T(8,128)S(1)}, f32[16,512]{1,0:T(8,128)S(1)}, u32[]{:S(2)}, u32[]{:S(2)}) collective-permute-start(f32[16,512]{1,0:T(8,128)S(1)} %get-tuple-element.27), channel_id=1, source_target_pairs={{0,2},{1,3},{2,1},{3,0},{4,6},{5,7},{6,5},{7,4},{8,10},{9,11},{10,... | collective-permute-start | bytes 98312 | tf_op jit(solution)/shard_map/ppermute | solution.py:278
  26.1 1.1 %collective-permute-start.11 = (f32[16,512]{1,0:T(8,128)S(1)}, f32[16,512]{1,0:T(8,128)S(1)}, u32[]{:S(2)}, u32[]{:S(2)}) collective-permute-start(f32[16,512]{1,0:T(8,128)S(1)} %get-tuple-element.29), channel_id=1, source_target_pairs={{0,3},{1,2},{2,0},{3,1},{4,7},{5,6},{6,4},{7,5},{8,11},{9,10},{10,... | collective-permute-start | bytes 98312 | tf_op jit(solution)/shard_map/ppermute | solution.py:278
  27.2 0.5 %collective-permute-start.12 = (f32[16,512]{1,0:T(8,128)S(1)}, f32[16,512]{1,0:T(8,128)S(1)}, u32[]{:S(2)}, u32[]{:S(2)}) collective-permute-start(f32[16,512]{1,0:T(8,128)S(1)} %get-tuple-element.28), channel_id=1, source_target_pairs={{0,1},{1,0},{2,3},{3,2},{4,5},{5,4},{6,7},{7,6},{8,9},{9,8},{10,11... | collective-permute-start | bytes 98312 | tf_op jit(solution)/shard_map/ppermute | solution.py:278
  27.7 1.3 %collective-permute-done.10 = f32[16,512]{1,0:T(8,128)S(1)} collective-permute-done((f32[16,512]{1,0:T(8,128)S(1)}, f32[16,512]{1,0:T(8,128)S(1)}, u32[]{:S(2)}, u32[]{:S(2)}) %collective-permute-start.10) | collective-permute-done | bytes 32800 | tf_op jit(solution)/shard_map/ppermute | solution.py:278
  29.0 1.9 %collective-permute-done.11 = f32[16,512]{1,0:T(8,128)S(1)} collective-permute-done((f32[16,512]{1,0:T(8,128)S(1)}, f32[16,512]{1,0:T(8,128)S(1)}, u32[]{:S(2)}, u32[]{:S(2)}) %collective-permute-start.11) | collective-permute-done | bytes 32800 | tf_op jit(solution)/shard_map/ppermute | solution.py:278
  31.0 0.3 %collective-permute-done.12 = f32[16,512]{1,0:T(8,128)S(1)} collective-permute-done((f32[16,512]{1,0:T(8,128)S(1)}, f32[16,512]{1,0:T(8,128)S(1)}, u32[]{:S(2)}, u32[]{:S(2)}) %collective-permute-start.12) | collective-permute-done | bytes 32800 | tf_op jit(solution)/shard_map/ppermute | solution.py:278
  31.3 0.6 %add_add_fusion = f32[16,512]{1,0:T(8,128)} fusion(f32[16,512]{1,0:T(8,128)S(1)} %collective-permute-done.12, f32[16,512]{1,0:T(8,128)S(1)} %collective-permute-done.11, f32[16,512]{1,0:T(8,128)S(1)} %collective-permute-done.10, f32[64,512]{1,0:T(8,128)S(1)} %convert_add_fusion, s32[]{:T(128)S(6)} %select_n.43), kind=kLoop, calls=%fused_computation.1 | loop fusion | flops 24576 | bytes 163844 | tf_op jit(solution)/shard_map/add | solution.py:278
  (2 shorter events, 0.0 us)
Async XLA Ops:
  1.4 8.5 %collective-permute-start.1 = (bf16[13,64,128]{2,1,0:T(8,128)(2,1)S(1)}, bf16[13,64,128]{2,1,0:T(8,128)(2,1)S(1)}, u32[]{:S(2)}, u32[]{:S(2)}) collective-permute-start(bf16[13,64,128]{2,1,0:T(8,128)(2,1)S(1)} %get-tuple-element.17), channel_id=1, source_target_pairs={{0,8},{4,20},{8,0},{12,28},{16,24},{20,4},{24,16},{28,12},{1,9},{5... | collective-permute-start | bytes 638984 | tf_op jit(solution)/shard_map/ppermute | solution.py:209
  4.4 6.1 %collective-permute-start.2 = (bf16[13,64,128]{2,1,0:T(8,128)(2,1)S(1)}, bf16[13,64,128]{2,1,0:T(8,128)(2,1)S(1)}, u32[]{:S(2)}, u32[]{:S(2)}) collective-permute-start(bf16[13,64,128]{2,1,0:T(8,128)(2,1)S(1)} %get-tuple-element.18), channel_id=1, source_target_pairs={{0,16},{4,12},{8,24},{12,4},{16,0},{20,28},{24,8},{28,20},{1,17},{... | collective-permute-start | bytes 638984 | tf_op jit(solution)/shard_map/ppermute | solution.py:209
  5.9 7.5 %collective-permute-start = (bf16[5,64,512]{2,1,0:T(8,128)(2,1)S(1)}, bf16[5,64,512]{2,1,0:T(8,128)(2,1)S(1)}, u32[]{:S(2)}, u32[]{:S(2)}) collective-permute-start(bf16[5,64,512]{2,1,0:T(8,128)(2,1)S(1)} %get-tuple-element.16.own_ref), channel_id=1, source_target_pairs={{0,4},{4,0},{8,12},{12,8},{16,20},{20,16},{24,28},{28,24},{1,5},{5... | collective-permute-start | bytes 983048 | tf_op jit(solution)/shard_map/ppermute | solution.py:206
  5.9 7.5 %collective-permute-start.5 = (bf16[7,64,128]{2,1,0:T(8,128)(2,1)S(1)}, bf16[7,64,128]{2,1,0:T(8,128)(2,1)S(1)}, u32[]{:S(2)}, u32[]{:S(2)}) collective-permute-start(bf16[7,64,128]{2,1,0:T(8,128)(2,1)S(1)} %get-tuple-element.22), channel_id=1, source_target_pairs={{0,24},{4,28},{8,16},{12,20},{16,8},{20,12},{24,0},{28,4},{1,25},{... | collective-permute-start | bytes 344072 | tf_op jit(solution)/shard_map/ppermute | solution.py:206
  9.9 3.5 %collective-permute-start.3 = (bf16[13,64,128]{2,1,0:T(8,128)(2,1)S(1)}, bf16[13,64,128]{2,1,0:T(8,128)(2,1)S(1)}, u32[]{:S(2)}, u32[]{:S(2)}) collective-permute-start(bf16[13,64,128]{2,1,0:T(8,128)(2,1)S(1)} %collective-permute-done.1.r1), channel_id=1, source_target_pairs={{0,4},{4,0},{8,12},{12,8},{16,20},{20,16},{24,28},{28,24},{1,5},{5... | collective-permute-start | bytes 638984 | tf_op jit(solution)/shard_map/ppermute | solution.py:206
  10.5 2.9 %collective-permute-start.4 = (bf16[13,64,128]{2,1,0:T(8,128)(2,1)S(1)}, bf16[13,64,128]{2,1,0:T(8,128)(2,1)S(1)}, u32[]{:S(2)}, u32[]{:S(2)}) collective-permute-start(bf16[13,64,128]{2,1,0:T(8,128)(2,1)S(1)} %collective-permute-done.2.r2), channel_id=1, source_target_pairs={{0,4},{4,0},{8,12},{12,8},{16,20},{20,16},{24,28},{28,24},{1,5},{5... | collective-permute-start | bytes 638984 | tf_op jit(solution)/shard_map/ppermute | solution.py:206
  13.4 1.4 %collective-permute-start.6 = (bf16[7,64,128]{2,1,0:T(8,128)(2,1)S(1)}, bf16[7,64,128]{2,1,0:T(8,128)(2,1)S(1)}, u32[]{:S(2)}, u32[]{:S(2)}) collective-permute-start(bf16[7,64,128]{2,1,0:T(8,128)(2,1)S(1)} %collective-permute-done.5.r3), channel_id=1, source_target_pairs={{0,4},{4,0},{8,12},{12,8},{16,20},{20,16},{24,28},{28,24},{1,5},{5... | collective-permute-start | bytes 344072 | tf_op jit(solution)/shard_map/ppermute | solution.py:206
  16.1 5.5 %collective-permute-start.7 = (bf16[64,512]{1,0:T(8,128)(2,1)S(1)}, bf16[64,512]{1,0:T(8,128)(2,1)S(1)}, u32[]{:S(2)}, u32[]{:S(2)}) collective-permute-start(bf16[64,512]{1,0:T(8,128)(2,1)S(1)} %get-tuple-element.24), channel_id=1, source_target_pairs={{0,24},{4,28},{8,16},{12,20},{16,8},{20,12},{24,0},{28,4},{1,25},{... | collective-permute-start | bytes 196616 | tf_op jit(solution)/shard_map/ppermute | solution.py:206
  18.6 4.6 %collective-permute-start.8 = (bf16[64,512]{1,0:T(8,128)(2,1)S(1)}, bf16[64,512]{1,0:T(8,128)(2,1)S(1)}, u32[]{:S(2)}, u32[]{:S(2)}) collective-permute-start(bf16[64,512]{1,0:T(8,128)(2,1)S(1)} %get-tuple-element.25), channel_id=1, source_target_pairs={{0,8},{4,20},{8,0},{12,28},{16,24},{20,4},{24,16},{28,12},{1,9},{5... | collective-permute-start | bytes 196616 | tf_op jit(solution)/shard_map/ppermute | solution.py:209
  18.6 4.6 %collective-permute-start.9 = (bf16[64,512]{1,0:T(8,128)(2,1)S(1)}, bf16[64,512]{1,0:T(8,128)(2,1)S(1)}, u32[]{:S(2)}, u32[]{:S(2)}) collective-permute-start(bf16[64,512]{1,0:T(8,128)(2,1)S(1)} %get-tuple-element.26), channel_id=1, source_target_pairs={{0,16},{4,12},{8,24},{12,4},{16,0},{20,28},{24,8},{28,20},{1,17},{... | collective-permute-start | bytes 196616 | tf_op jit(solution)/shard_map/ppermute | solution.py:209
  23.3 5.8 %collective-permute-start.10 = (f32[16,512]{1,0:T(8,128)S(1)}, f32[16,512]{1,0:T(8,128)S(1)}, u32[]{:S(2)}, u32[]{:S(2)}) collective-permute-start(f32[16,512]{1,0:T(8,128)S(1)} %get-tuple-element.27), channel_id=1, source_target_pairs={{0,2},{1,3},{2,1},{3,0},{4,6},{5,7},{6,5},{7,4},{8,10},{9,11},{10,... | collective-permute-start | bytes 98312 | tf_op jit(solution)/shard_map/ppermute | solution.py:278
  26.1 4.8 %collective-permute-start.11 = (f32[16,512]{1,0:T(8,128)S(1)}, f32[16,512]{1,0:T(8,128)S(1)}, u32[]{:S(2)}, u32[]{:S(2)}) collective-permute-start(f32[16,512]{1,0:T(8,128)S(1)} %get-tuple-element.29), channel_id=1, source_target_pairs={{0,3},{1,2},{2,0},{3,1},{4,7},{5,6},{6,4},{7,5},{8,11},{9,10},{10,... | collective-permute-start | bytes 98312 | tf_op jit(solution)/shard_map/ppermute | solution.py:278
  27.2 4.1 %collective-permute-start.12 = (f32[16,512]{1,0:T(8,128)S(1)}, f32[16,512]{1,0:T(8,128)S(1)}, u32[]{:S(2)}, u32[]{:S(2)}) collective-permute-start(f32[16,512]{1,0:T(8,128)S(1)} %get-tuple-element.28), channel_id=1, source_target_pairs={{0,1},{1,0},{2,3},{3,2},{4,5},{5,4},{6,7},{7,6},{8,9},{9,8},{10,11... | collective-permute-start | bytes 98312 | tf_op jit(solution)/shard_map/ppermute | solution.py:278

commit v5 on v4

--- a/solution.py
+++ b/solution.py
@@ -11,6 +11,7 @@
 TILE = 2 * BLK
 CHIPS = 4
 GROUP = 4
+PLANE = ((1, 3, 0, 2), (3, 2, 1, 0), (2, 0, 3, 1))
 STEPS = ((2, 3, 1, 0), (3, 2, 0, 1), (1, 0, 3, 2))
 NEAR = 13
 FAR = 7
@@ -29,7 +30,7 @@
 
 
 def pack_kernel(
-    b_hbm, d_hbm, pair_hbm, dens_hbm, own_ref, s1, s2, s3, pair_ref, dens_ref, d_ref, half_ref, line_ref, sems
+    b_hbm, d_hbm, pair_hbm, dens_hbm, s1, s2, s3, mine_ref, line_ref, pair_ref, dens_ref, d_ref, half_ref, sems
 ):
     me = lax.axis_index("mu")
     c = me // 2
@@ -54,9 +55,6 @@
                 b_hbm.at[pl.ds(first, count), :, column(chip)], into.at[pl.ds(slot, count)], sems.at[3 + i]
             )
         )
-    copies.append(
-        pltpu.make_async_copy(b_hbm.at[pl.ds(c * GROUP, GROUP)], own_ref.at[pl.ds(0, GROUP)], sems.at[3 + len(pieces)])
-    )
     for copy in copies:
         copy.start()
     copies[0].wait()
@@ -67,7 +65,7 @@
     dens_line = expand_row(dens_ref, me, size)
     copies[2].wait()
     dens = d_ref[...] * dens_line
-    own_ref[GROUP] = dens
+    mine_ref[...] = dens
     for j in range(CHIPS):
         for send in (s1, s2, s3):
             send[send.shape[0] - CHIPS + j] = dens[:, j * TILE : (j + 1) * TILE]
@@ -84,9 +82,17 @@
                 left, right = (half_ref[2 * i + j][:, core * BLK : (core + 1) * BLK] for j in (0, 1))
                 send[2] = jnp.concatenate([left, right], axis=1)
 
-    copies[-1].wait()
+
+def own_kernel(b_hbm, mine_ref, line_ref, own_ref, sem):
+    c = lax.axis_index("mu") // 2
+    copy = pltpu.make_async_copy(b_hbm.at[pl.ds(c * GROUP, GROUP)], own_ref.at[pl.ds(0, GROUP)], sem)
+    copy.start()
+    own_ref[GROUP] = mine_ref[...]
+    copy.wait()
     for p in range(GROUP):
-        own_ref[p] = own_ref[p] * pair_line
+        for j in range(CHIPS):
+            at = slice(j * TILE, (j + 1) * TILE)
+            own_ref[p, :, at] = own_ref[p, :, at] * line_ref[j].astype(BF)
 
 
 def row_at(p, chip, core):
@@ -192,8 +198,9 @@
         xg_scr[:, p * TILE : (p + 1) * TILE] = x_scr[:, pl.ds(pl.multiple_of(p * size + cg * TILE, TILE), TILE)]
     k_scr[...] = jnp.dot(x_scr[...], t_ref[...], preferred_element_type=F32)
     k_scr[:, column(cg)] += jnp.dot(xg_scr[...], g_scr[...], preferred_element_type=F32)
-    for out, d in ((e1, 1 + k), (e2, 2 - k), (e3, 3)):
-        out[...] = k_scr[pl.ds(pl.multiple_of((c ^ d) * BLK, BLK), BLK), :].astype(BF)
+    for out, step in zip((e1, e2, e3), PLANE):
+        to = sum(jnp.where(c == i, j, 0) for i, j in enumerate(step))
+        out[...] = k_scr[pl.ds(pl.multiple_of(to * BLK, BLK), BLK), :].astype(BF)
     keep_ref[...] = k_scr[pl.ds(pl.multiple_of(c * BLK, BLK), BLK), :]
 
 
@@ -214,22 +221,39 @@
     def slots(count):
         return jax.ShapeDtypeStruct((count, width, TILE), BF)
 
-    own, *sends = pl.pallas_call(
+    b_tensor, density, pair_mask, dens_mask = (
+        pltpu.with_memory_space_constraint(x, pltpu.HBM) for x in (b_tensor, density, pair_mask, dens_mask)
+    )
+    *sends, mine, line = pl.pallas_call(
         pack_kernel,
-        out_shape=[jax.ShapeDtypeStruct((GROUP + 1, width, size), BF), slots(NEAR), slots(NEAR), slots(FAR)],
+        out_shape=[
+            slots(NEAR),
+            slots(NEAR),
+            slots(FAR),
+            jax.ShapeDtypeStruct((width, size), BF),
+            jax.ShapeDtypeStruct((CHIPS, 1, TILE), F32),
+        ],
         in_specs=[hbm] * 4,
-        out_specs=[vmem] * 4,
+        out_specs=[vmem] * 5,
         scratch_shapes=[
             pltpu.SMEM(pair_mask.shape, jnp.int32),
             pltpu.SMEM(dens_mask.shape, jnp.int32),
             pltpu.VMEM(density.shape, BF),
             pltpu.VMEM((6, width, TILE), BF),
-            pltpu.VMEM((CHIPS, 1, TILE), F32),
-            pltpu.SemaphoreType.DMA((14,)),
+            pltpu.SemaphoreType.DMA((13,)),
         ],
         compiler_params=pltpu.CompilerParams(vmem_limit_bytes=16 << 20),
         name="pack",
-    )(*(pltpu.with_memory_space_constraint(x, pltpu.HBM) for x in (b_tensor, density, pair_mask, dens_mask)))
+    )(b_tensor, density, pair_mask, dens_mask)
+    own = pl.pallas_call(
+        own_kernel,
+        out_shape=jax.ShapeDtypeStruct((GROUP + 1, width, size), BF),
+        in_specs=[hbm, vmem, vmem],
+        out_specs=vmem,
+        scratch_shapes=[pltpu.SemaphoreType.DMA],
+        compiler_params=pltpu.CompilerParams(vmem_limit_bytes=16 << 20),
+        name="own",
+    )(b_tensor, mine, line)
     r1, r2, r3 = around(*sends)
     mate = swap(own, 1)
     q1, q2, q3 = swap(r1, 1), swap(r2, 1), swap(r3, 1)
@@ -264,8 +288,10 @@
         compiler_params=pltpu.CompilerParams(vmem_limit_bytes=32 << 20),
         name="late",
     )(*early, r3, q3)
-    y1, y2, y3 = around(*parts)
-    plane = (((keep + y3.astype(F32)) + y1.astype(F32)) + y2.astype(F32))
+    plane = keep
+    for part, step in zip(parts, PLANE):
+        pairs = [(2 * i + core, 2 * j + core) for i, j in enumerate(step) for core in (0, 1)]
+        plane = plane + lax.ppermute(part, "mu", pairs).astype(F32)
     a = lax.axis_index("aux")
     strip = width // 4
 

time: 32.1 us -> 32 us (level)
  waiting for transfers between devices: 14.2 us -> 12.5 us
  Pallas kernels: 4.03 us -> 4.93 us
  starting transfers between devices: 13 us -> 13.7 us
    ppermute x0 -> x3, starting transfers between devices: none -> 4.48 us  [spread(): plane = plane + lax.ppermute(part, 'mu', pairs).astype(F32)]
    ppermute x4 -> x2, waiting for transfers between devices: 6.17 us -> 3.14 us  [turn(): lax.ppermute(x, 'mu', [(i, i ^ (2 if (i % 2 == 0) == first else 4)) for i...]
    ppermute x0 -> x3, waiting for transfers between devices: none -> 2.71 us  [spread(): plane = plane + lax.ppermute(part, 'mu', pairs).astype(F32)]
    ppermute x6 -> x5, starting transfers between devices: 2.97 us -> 0.37 us  [swap(): return lax.ppermute(x, 'mu', [(i, i ^ step) for i in range(2 * CHIPS)])]
    ppermute x6 -> x5, waiting for transfers between devices: 4.44 us -> 3.03 us  [swap(): return lax.ppermute(x, 'mu', [(i, i ^ step) for i in range(2 * CHIPS)])]
    ppermute x4 -> x2, starting transfers between devices: 5.55 us -> 4.52 us  [turn(): lax.ppermute(x, 'mu', [(i, i ^ (2 if (i % 2 == 0) == first else 4)) for i...]
    pallas_call x1 -> x2, Pallas kernels: 1.35 us -> 2.25 us  [the longest x1 1.24 us: spread(): pl.pallas_call(pack_kernel, out_shape=[slots(NEAR), slots(NEAR), slots(FA...]
  transfers between devices with their start and end apart: 13 -> 13, of which waited for: 8 -> 9; matrix products, arithmetic and copies ran while one was open for 0% -> 0% of each run, Pallas kernels for 4% -> 8%
where the time goes in v5:
time: 32 us; the launch traced here: 31.8 us
  starting transfers between devices  13.7 us (43%)
  waiting for transfers between devices  12.5 us (39%)
  Pallas kernels  4.93 us (15%)
  other arithmetic  0.65 us (2%)
    ppermute x2, starting transfers between devices, turn(): lax.ppermute(x, 'mu', [(i, i ^ (2 if (i % 2 == 0) == first else 4)) for i...  4.52 us
    ppermute x3, starting transfers between devices, spread(): plane = plane + lax.ppermute(part, 'mu', pairs).astype(F32)  4.48 us
    ppermute x3, starting transfers between devices, spread(): total = total + lax.ppermute(strip_of(to), 'aux', list(enumerate(step)))  4.29 us
    ppermute x3, waiting for transfers between devices, spread(): total = total + lax.ppermute(strip_of(to), 'aux', list(enumerate(step)))  3.59 us
    ppermute x2, waiting for transfers between devices, turn(): lax.ppermute(x, 'mu', [(i, i ^ (2 if (i % 2 == 0) == first else 4)) for i...  3.14 us
    ppermute x5, waiting for transfers between devices, swap(): return lax.ppermute(x, 'mu', [(i, i ^ step) for i in range(2 * CHIPS)])  3.03 us
    ppermute x3, waiting for transfers between devices, spread(): plane = plane + lax.ppermute(part, 'mu', pairs).astype(F32)  2.71 us
    pallas_call x1, Pallas kernels, spread(): pl.pallas_call(early_kernel, out_shape=[jax.ShapeDtypeStruct((GROUP * siz...  1.41 us
  transfers between devices with their start and end apart: 13, of which 9 were waited for; matrix products, arithmetic and copies ran while one was open for 0% of the time, Pallas kernels for 8%

profile of v5, /device:TPU:0, one launch (start us, length us, event | category | flops | bytes accessed | tf_op | source)
XLA Modules:
  0.0 31.8 jit_solution(13090302235113745892)
XLA Ops:
  0.0 1.2 %pack.1 = (bf16[13,64,128]{2,1,0:T(8,128)(2,1)S(1)}, bf16[13,64,128]{2,1,0:T(8,128)(2,1)S(1)}, bf16[7,64,128]{2,1,0:T(8,128)(2,1)S(1)}, bf16[64,512]{1,0:T(8,128)(2,1)S(1)}, f32[4,1,128]{2,1,0:T(1,128)S(1)}) custom-call(bf16[16,64,512]{2,1,0:T(8,128)(2,1)} %b_hbm.3, bf16[64,512]{1,0:T(8,128)(2,1)} %d_hbm.1, s32[8,8]{1,0:T(8,128)} %pair_hbm.1, s32[8,8]{1,0:T(8,128)} %dens_hbm.1), custom_call_target="tpu_custom_call" | custom-call | tf_op jit(solution)/shard_map/pack/pallas_call | solution.py:227
  1.2 3.0 %collective-permute-start.1 = (bf16[13,64,128]{2,1,0:T(8,128)(2,1)S(1)}, bf16[13,64,128]{2,1,0:T(8,128)(2,1)S(1)}, u32[]{:S(2)}, u32[]{:S(2)}) collective-permute-start(bf16[13,64,128]{2,1,0:T(8,128)(2,1)S(1)} %get-tuple-element.19), channel_id=1, source_target_pairs={{0,8},{4,20},{8,0},{12,28},{16,24},{20,4},{24,16},{28,12},{1,9},{5... | collective-permute-start | bytes 638984 | tf_op jit(solution)/shard_map/ppermute | solution.py:216
  4.3 1.5 %collective-permute-start.2 = (bf16[13,64,128]{2,1,0:T(8,128)(2,1)S(1)}, bf16[13,64,128]{2,1,0:T(8,128)(2,1)S(1)}, u32[]{:S(2)}, u32[]{:S(2)}) collective-permute-start(bf16[13,64,128]{2,1,0:T(8,128)(2,1)S(1)} %get-tuple-element.20), channel_id=1, source_target_pairs={{0,16},{4,12},{8,24},{12,4},{16,0},{20,28},{24,8},{28,20},{1,17},{... | collective-permute-start | bytes 638984 | tf_op jit(solution)/shard_map/ppermute | solution.py:216
  5.8 1.0 %own.1.own_ref = bf16[5,64,512]{2,1,0:T(8,128)(2,1)S(1)} custom-call(bf16[16,64,512]{2,1,0:T(8,128)(2,1)} %b_hbm.3, bf16[64,512]{1,0:T(8,128)(2,1)S(1)} %get-tuple-element.17.mine_ref, f32[4,1,128]{2,1,0:T(1,128)S(1)} %get-tuple-element.18.line_ref), custom_call_target="tpu_custom_call" | custom-call | tf_op jit(solution)/shard_map/own/pallas_call | solution.py:248
  6.8 0.1 collective-permute-start
  6.9 0.1 collective-permute-start.5
  7.0 2.8 %collective-permute-done.1.r1 = bf16[13,64,128]{2,1,0:T(8,128)(2,1)S(1)} collective-permute-done((bf16[13,64,128]{2,1,0:T(8,128)(2,1)S(1)}, bf16[13,64,128]{2,1,0:T(8,128)(2,1)S(1)}, u32[]{:S(2)}, u32[]{:S(2)}) %collective-permute-start.1) | collective-permute-done | bytes 213024 | tf_op jit(solution)/shard_map/ppermute | solution.py:216
  9.8 0.0 collective-permute-start.3
  9.8 0.3 collective-permute-done.2.r2
  10.1 0.2 collective-permute-start.4
  10.3 3.0 %collective-permute-done.5.r3 = bf16[7,64,128]{2,1,0:T(8,128)(2,1)S(1)} collective-permute-done((bf16[7,64,128]{2,1,0:T(8,128)(2,1)S(1)}, bf16[7,64,128]{2,1,0:T(8,128)(2,1)S(1)}, u32[]{:S(2)}, u32[]{:S(2)}) %collective-permute-start.5) | collective-permute-done | bytes 114720 | tf_op jit(solution)/shard_map/ppermute | solution.py:213
  13.3 0.0 collective-permute-start.6
  13.3 0.0 collective-permute-done.mate_ref
  13.3 0.0 collective-permute-done.3.q1
  13.3 0.0 collective-permute-done.4.q2
  13.4 1.4 %early.1 = (bf16[2048,512]{1,0:T(8,128)(2,1)S(1)}, bf16[1024,128]{1,0:T(8,128)(2,1)S(1)}, f32[1024,512]{1,0:T(8,128)S(1)}) custom-call(bf16[5,64,512]{2,1,0:T(8,128)(2,1)S(1)} %own.1.own_ref, bf16[5,64,512]{2,1,0:T(8,128)(2,1)S(1)} %collective-permute-done.mate_ref, bf16[13,64,128]{2,1,0:T(8,128)(2,1)S(1)} %collective-permute-done.1.r1, ...), custom_call_target="tpu_custom_call" | custom-call | tf_op jit(solution)/shard_map/early/pallas_call | solution.py:261
  14.8 0.0 collective-permute-done.6.q3
  14.8 1.3 %late.1 = (bf16[64,512]{1,0:T(8,128)(2,1)S(1)}, bf16[64,512]{1,0:T(8,128)(2,1)S(1)}, bf16[64,512]{1,0:T(8,128)(2,1)S(1)}, f32[64,512]{1,0:T(8,128)S(1)}) custom-call(bf16[2048,512]{1,0:T(8,128)(2,1)S(1)} %get-tuple-element.21.t_ref, bf16[1024,128]{1,0:T(8,128)(2,1)S(1)} %get-tuple-element.22.l_ref, f32[1024,512]{1,0:T(8,128)S(1)} %get-tuple-element.23.xp_ref, ...), custom_call_target="tpu_custom_call" | custom-call | tf_op jit(solution)/shard_map/late/pallas_call | solution.py:275
  16.1 1.6 %collective-permute-start.7 = (bf16[64,512]{1,0:T(8,128)(2,1)S(1)}, bf16[64,512]{1,0:T(8,128)(2,1)S(1)}, u32[]{:S(2)}, u32[]{:S(2)}) collective-permute-start(bf16[64,512]{1,0:T(8,128)(2,1)S(1)} %get-tuple-element.26), channel_id=1, source_target_pairs={{0,8},{4,12},{8,24},{12,28},{16,0},{20,4},{24,16},{28,20},{1,9},{5... | collective-permute-start | bytes 196616 | tf_op jit(solution)/shard_map/ppermute | solution.py:294
  17.7 0.9 %collective-permute-start.8 = (bf16[64,512]{1,0:T(8,128)(2,1)S(1)}, bf16[64,512]{1,0:T(8,128)(2,1)S(1)}, u32[]{:S(2)}, u32[]{:S(2)}) collective-permute-start(bf16[64,512]{1,0:T(8,128)(2,1)S(1)} %get-tuple-element.27), channel_id=1, source_target_pairs={{0,24},{4,28},{8,16},{12,20},{16,8},{20,12},{24,0},{28,4},{1,25},{... | collective-permute-start | bytes 196616 | tf_op jit(solution)/shard_map/ppermute | solution.py:294
  18.6 1.9 %collective-permute-start.9 = (bf16[64,512]{1,0:T(8,128)(2,1)S(1)}, bf16[64,512]{1,0:T(8,128)(2,1)S(1)}, u32[]{:S(2)}, u32[]{:S(2)}) collective-permute-start(bf16[64,512]{1,0:T(8,128)(2,1)S(1)} %get-tuple-element.28), channel_id=1, source_target_pairs={{0,16},{4,20},{8,0},{12,4},{16,24},{20,28},{24,8},{28,12},{1,17},{... | collective-permute-start | bytes 196616 | tf_op jit(solution)/shard_map/ppermute | solution.py:294
  20.5 0.1 collective-permute-done.7
  20.6 2.2 %collective-permute-done.8 = bf16[64,512]{1,0:T(8,128)(2,1)S(1)} collective-permute-done((bf16[64,512]{1,0:T(8,128)(2,1)S(1)}, bf16[64,512]{1,0:T(8,128)(2,1)S(1)}, u32[]{:S(2)}, u32[]{:S(2)}) %collective-permute-start.8) | collective-permute-done | bytes 65568 | tf_op jit(solution)/shard_map/ppermute | solution.py:294
  22.8 0.4 %collective-permute-done.9 = bf16[64,512]{1,0:T(8,128)(2,1)S(1)} collective-permute-done((bf16[64,512]{1,0:T(8,128)(2,1)S(1)}, bf16[64,512]{1,0:T(8,128)(2,1)S(1)}, u32[]{:S(2)}, u32[]{:S(2)}) %collective-permute-start.9) | collective-permute-done | bytes 65568 | tf_op jit(solution)/shard_map/ppermute | solution.py:294
  23.3 2.7 %collective-permute-start.10 = (f32[16,512]{1,0:T(8,128)S(1)}, f32[16,512]{1,0:T(8,128)S(1)}, u32[]{:S(2)}, u32[]{:S(2)}) collective-permute-start(f32[16,512]{1,0:T(8,128)S(1)} %get-tuple-element.29), channel_id=1, source_target_pairs={{0,2},{1,3},{2,1},{3,0},{4,6},{5,7},{6,5},{7,4},{8,10},{9,11},{10,... | collective-permute-start | bytes 98312 | tf_op jit(solution)/shard_map/ppermute | solution.py:304
  26.0 1.2 %collective-permute-start.11 = (f32[16,512]{1,0:T(8,128)S(1)}, f32[16,512]{1,0:T(8,128)S(1)}, u32[]{:S(2)}, u32[]{:S(2)}) collective-permute-start(f32[16,512]{1,0:T(8,128)S(1)} %get-tuple-element.31), channel_id=1, source_target_pairs={{0,3},{1,2},{2,0},{3,1},{4,7},{5,6},{6,4},{7,5},{8,11},{9,10},{10,... | collective-permute-start | bytes 98312 | tf_op jit(solution)/shard_map/ppermute | solution.py:304
  27.2 0.4 %collective-permute-start.12 = (f32[16,512]{1,0:T(8,128)S(1)}, f32[16,512]{1,0:T(8,128)S(1)}, u32[]{:S(2)}, u32[]{:S(2)}) collective-permute-start(f32[16,512]{1,0:T(8,128)S(1)} %get-tuple-element.30), channel_id=1, source_target_pairs={{0,1},{1,0},{2,3},{3,2},{4,5},{5,4},{6,7},{7,6},{8,9},{9,8},{10,11... | collective-permute-start | bytes 98312 | tf_op jit(solution)/shard_map/ppermute | solution.py:304
  27.6 1.6 %collective-permute-done.10 = f32[16,512]{1,0:T(8,128)S(1)} collective-permute-done((f32[16,512]{1,0:T(8,128)S(1)}, f32[16,512]{1,0:T(8,128)S(1)}, u32[]{:S(2)}, u32[]{:S(2)}) %collective-permute-start.10) | collective-permute-done | bytes 32800 | tf_op jit(solution)/shard_map/ppermute | solution.py:304
  29.2 1.6 %collective-permute-done.11 = f32[16,512]{1,0:T(8,128)S(1)} collective-permute-done((f32[16,512]{1,0:T(8,128)S(1)}, f32[16,512]{1,0:T(8,128)S(1)}, u32[]{:S(2)}, u32[]{:S(2)}) %collective-permute-start.11) | collective-permute-done | bytes 32800 | tf_op jit(solution)/shard_map/ppermute | solution.py:304
  30.8 0.3 %collective-permute-done.12 = f32[16,512]{1,0:T(8,128)S(1)} collective-permute-done((f32[16,512]{1,0:T(8,128)S(1)}, f32[16,512]{1,0:T(8,128)S(1)}, u32[]{:S(2)}, u32[]{:S(2)}) %collective-permute-start.12) | collective-permute-done | bytes 32800 | tf_op jit(solution)/shard_map/ppermute | solution.py:304
  31.2 0.6 %add_add_fusion = f32[16,512]{1,0:T(8,128)} fusion(f32[16,512]{1,0:T(8,128)S(1)} %collective-permute-done.12, f32[16,512]{1,0:T(8,128)S(1)} %collective-permute-done.11, f32[16,512]{1,0:T(8,128)S(1)} %collective-permute-done.10, f32[64,512]{1,0:T(8,128)S(1)} %convert_add_fusion, s32[]{:T(128)S(6)} %select_n.43), kind=kLoop, calls=%fused_computation.1 | loop fusion | flops 24576 | bytes 163844 | tf_op jit(solution)/shard_map/add | solution.py:304
  (2 shorter events, 0.0 us)
Async XLA Ops:
  1.2 8.5 %collective-permute-start.1 = (bf16[13,64,128]{2,1,0:T(8,128)(2,1)S(1)}, bf16[13,64,128]{2,1,0:T(8,128)(2,1)S(1)}, u32[]{:S(2)}, u32[]{:S(2)}) collective-permute-start(bf16[13,64,128]{2,1,0:T(8,128)(2,1)S(1)} %get-tuple-element.19), channel_id=1, source_target_pairs={{0,8},{4,20},{8,0},{12,28},{16,24},{20,4},{24,16},{28,12},{1,9},{5... | collective-permute-start | bytes 638984 | tf_op jit(solution)/shard_map/ppermute | solution.py:216
  4.3 5.8 %collective-permute-start.2 = (bf16[13,64,128]{2,1,0:T(8,128)(2,1)S(1)}, bf16[13,64,128]{2,1,0:T(8,128)(2,1)S(1)}, u32[]{:S(2)}, u32[]{:S(2)}) collective-permute-start(bf16[13,64,128]{2,1,0:T(8,128)(2,1)S(1)} %get-tuple-element.20), channel_id=1, source_target_pairs={{0,16},{4,12},{8,24},{12,4},{16,0},{20,28},{24,8},{28,20},{1,17},{... | collective-permute-start | bytes 638984 | tf_op jit(solution)/shard_map/ppermute | solution.py:216
  6.8 6.5 %collective-permute-start = (bf16[5,64,512]{2,1,0:T(8,128)(2,1)S(1)}, bf16[5,64,512]{2,1,0:T(8,128)(2,1)S(1)}, u32[]{:S(2)}, u32[]{:S(2)}) collective-permute-start(bf16[5,64,512]{2,1,0:T(8,128)(2,1)S(1)} %own.1.own_ref), channel_id=1, source_target_pairs={{0,4},{4,0},{8,12},{12,8},{16,20},{20,16},{24,28},{28,24},{1,5},{5... | collective-permute-start | bytes 983048 | tf_op jit(solution)/shard_map/ppermute | solution.py:213
  6.9 6.5 %collective-permute-start.5 = (bf16[7,64,128]{2,1,0:T(8,128)(2,1)S(1)}, bf16[7,64,128]{2,1,0:T(8,128)(2,1)S(1)}, u32[]{:S(2)}, u32[]{:S(2)}) collective-permute-start(bf16[7,64,128]{2,1,0:T(8,128)(2,1)S(1)} %get-tuple-element.24), channel_id=1, source_target_pairs={{0,24},{4,28},{8,16},{12,20},{16,8},{20,12},{24,0},{28,4},{1,25},{... | collective-permute-start | bytes 344072 | tf_op jit(solution)/shard_map/ppermute | solution.py:213
  9.8 3.5 %collective-permute-start.3 = (bf16[13,64,128]{2,1,0:T(8,128)(2,1)S(1)}, bf16[13,64,128]{2,1,0:T(8,128)(2,1)S(1)}, u32[]{:S(2)}, u32[]{:S(2)}) collective-permute-start(bf16[13,64,128]{2,1,0:T(8,128)(2,1)S(1)} %collective-permute-done.1.r1), channel_id=1, source_target_pairs={{0,4},{4,0},{8,12},{12,8},{16,20},{20,16},{24,28},{28,24},{1,5},{5... | collective-permute-start | bytes 638984 | tf_op jit(solution)/shard_map/ppermute | solution.py:213
  10.1 3.2 %collective-permute-start.4 = (bf16[13,64,128]{2,1,0:T(8,128)(2,1)S(1)}, bf16[13,64,128]{2,1,0:T(8,128)(2,1)S(1)}, u32[]{:S(2)}, u32[]{:S(2)}) collective-permute-start(bf16[13,64,128]{2,1,0:T(8,128)(2,1)S(1)} %collective-permute-done.2.r2), channel_id=1, source_target_pairs={{0,4},{4,0},{8,12},{12,8},{16,20},{20,16},{24,28},{28,24},{1,5},{5... | collective-permute-start | bytes 638984 | tf_op jit(solution)/shard_map/ppermute | solution.py:213
  13.3 1.4 %collective-permute-start.6 = (bf16[7,64,128]{2,1,0:T(8,128)(2,1)S(1)}, bf16[7,64,128]{2,1,0:T(8,128)(2,1)S(1)}, u32[]{:S(2)}, u32[]{:S(2)}) collective-permute-start(bf16[7,64,128]{2,1,0:T(8,128)(2,1)S(1)} %collective-permute-done.5.r3), channel_id=1, source_target_pairs={{0,4},{4,0},{8,12},{12,8},{16,20},{20,16},{24,28},{28,24},{1,5},{5... | collective-permute-start | bytes 344072 | tf_op jit(solution)/shard_map/ppermute | solution.py:213
  16.1 4.6 %collective-permute-start.7 = (bf16[64,512]{1,0:T(8,128)(2,1)S(1)}, bf16[64,512]{1,0:T(8,128)(2,1)S(1)}, u32[]{:S(2)}, u32[]{:S(2)}) collective-permute-start(bf16[64,512]{1,0:T(8,128)(2,1)S(1)} %get-tuple-element.26), channel_id=1, source_target_pairs={{0,8},{4,12},{8,24},{12,28},{16,0},{20,4},{24,16},{28,20},{1,9},{5... | collective-permute-start | bytes 196616 | tf_op jit(solution)/shard_map/ppermute | solution.py:294
  17.7 5.2 %collective-permute-start.8 = (bf16[64,512]{1,0:T(8,128)(2,1)S(1)}, bf16[64,512]{1,0:T(8,128)(2,1)S(1)}, u32[]{:S(2)}, u32[]{:S(2)}) collective-permute-start(bf16[64,512]{1,0:T(8,128)(2,1)S(1)} %get-tuple-element.27), channel_id=1, source_target_pairs={{0,24},{4,28},{8,16},{12,20},{16,8},{20,12},{24,0},{28,4},{1,25},{... | collective-permute-start | bytes 196616 | tf_op jit(solution)/shard_map/ppermute | solution.py:294
  18.6 4.7 %collective-permute-start.9 = (bf16[64,512]{1,0:T(8,128)(2,1)S(1)}, bf16[64,512]{1,0:T(8,128)(2,1)S(1)}, u32[]{:S(2)}, u32[]{:S(2)}) collective-permute-start(bf16[64,512]{1,0:T(8,128)(2,1)S(1)} %get-tuple-element.28), channel_id=1, source_target_pairs={{0,16},{4,20},{8,0},{12,4},{16,24},{20,28},{24,8},{28,12},{1,17},{... | collective-permute-start | bytes 196616 | tf_op jit(solution)/shard_map/ppermute | solution.py:294
  23.3 5.9 %collective-permute-start.10 = (f32[16,512]{1,0:T(8,128)S(1)}, f32[16,512]{1,0:T(8,128)S(1)}, u32[]{:S(2)}, u32[]{:S(2)}) collective-permute-start(f32[16,512]{1,0:T(8,128)S(1)} %get-tuple-element.29), channel_id=1, source_target_pairs={{0,2},{1,3},{2,1},{3,0},{4,6},{5,7},{6,5},{7,4},{8,10},{9,11},{10,... | collective-permute-start | bytes 98312 | tf_op jit(solution)/shard_map/ppermute | solution.py:304
  26.0 4.8 %collective-permute-start.11 = (f32[16,512]{1,0:T(8,128)S(1)}, f32[16,512]{1,0:T(8,128)S(1)}, u32[]{:S(2)}, u32[]{:S(2)}) collective-permute-start(f32[16,512]{1,0:T(8,128)S(1)} %get-tuple-element.31), channel_id=1, source_target_pairs={{0,3},{1,2},{2,0},{3,1},{4,7},{5,6},{6,4},{7,5},{8,11},{9,10},{10,... | collective-permute-start | bytes 98312 | tf_op jit(solution)/shard_map/ppermute | solution.py:304
  27.2 4.0 %collective-permute-start.12 = (f32[16,512]{1,0:T(8,128)S(1)}, f32[16,512]{1,0:T(8,128)S(1)}, u32[]{:S(2)}, u32[]{:S(2)}) collective-permute-start(f32[16,512]{1,0:T(8,128)S(1)} %get-tuple-element.30), channel_id=1, source_target_pairs={{0,1},{1,0},{2,3},{3,2},{4,5},{5,4},{6,7},{7,6},{8,9},{9,8},{10,11... | collective-permute-start | bytes 98312 | tf_op jit(solution)/shard_map/ppermute | solution.py:304

commit v6 on v4

--- a/solution.py
+++ b/solution.py
@@ -157,7 +157,7 @@
     x_ref[...] = jnp.dot(l_scr[...], d_scr[...], preferred_element_type=F32)
 
 
-def late_kernel(t_ref, l_ref, xp_ref, r3, q3, e1, e2, e3, keep_ref, d_scr, l_scr, g_scr, x_scr, xg_scr, k_scr):
+def late_kernel(t_in, l_ref, xp_ref, r3, q3, e1, e2, e3, keep_ref, t_ref, d_scr, l_scr, x_scr, k_scr):
     me = lax.axis_index("mu")
     c = me // 2
     k = me % 2
@@ -171,8 +171,8 @@
                 d_scr[core * BLK : (core + 1) * BLK, j * TILE : (j + 1) * TILE] = g[FAR - CHIPS + j]
         for p in range(GROUP):
             top, low = square(p, g0, g1)
-            g_scr[p * TILE : p * TILE + BLK, :] = top
-            g_scr[p * TILE + BLK : (p + 1) * TILE, :] = low
+            t_ref[row_at(p, cg, 0), column(cg)] = top
+            t_ref[row_at(p, cg, 1), column(cg)] = low
 
     @pl.when(k == 0)
     def _():
@@ -185,13 +185,11 @@
     l_scr[...] = l_ref[...]
     for p in range(GROUP):
         at = pl.ds(pl.multiple_of((p * CHIPS + cg) * BLK, BLK), BLK)
-        l_scr[at, :] = g_scr[pl.ds(pl.multiple_of(p * TILE + k * BLK, BLK), BLK), :]
+        l_scr[at, :] = t_ref[row_at(p, cg, k), column(cg)]
     for p in range(GROUP):
         rest = jnp.dot(l_scr[p * half : (p + 1) * half, :], d_scr[...], preferred_element_type=F32)
         x_scr[:, p * size : (p + 1) * size] = (xp_ref[p * half : (p + 1) * half, :] + rest).astype(BF)
-        xg_scr[:, p * TILE : (p + 1) * TILE] = x_scr[:, pl.ds(pl.multiple_of(p * size + cg * TILE, TILE), TILE)]
     k_scr[...] = jnp.dot(x_scr[...], t_ref[...], preferred_element_type=F32)
-    k_scr[:, column(cg)] += jnp.dot(xg_scr[...], g_scr[...], preferred_element_type=F32)
     for out, d in ((e1, 1 + k), (e2, 2 - k), (e3, 3)):
         out[...] = k_scr[pl.ds(pl.multiple_of((c ^ d) * BLK, BLK), BLK), :].astype(BF)
     keep_ref[...] = k_scr[pl.ds(pl.multiple_of(c * BLK, BLK), BLK), :]
@@ -248,17 +246,16 @@
         name="early",
     )(own, mate, r1, r2, q1, q2)
     chunk = jax.ShapeDtypeStruct((width, size), BF)
-    *parts, keep = pl.pallas_call(
+    *parts, keep, unused = pl.pallas_call(
         late_kernel,
-        out_shape=[chunk, chunk, chunk, jax.ShapeDtypeStruct((width, size), F32)],
+        out_shape=[chunk, chunk, chunk, jax.ShapeDtypeStruct((width, size), F32), jax.ShapeDtypeStruct(early[0].shape, BF)],
         in_specs=[vmem] * 5,
-        out_specs=[vmem] * 4,
+        out_specs=[vmem] * 5,
+        input_output_aliases={0: 4},
         scratch_shapes=[
             pltpu.VMEM((TILE, size), BF),
             pltpu.VMEM((GROUP * half, TILE), BF),
-            pltpu.VMEM((GROUP * TILE, TILE), BF),
             pltpu.VMEM((half, GROUP * size), BF),
-            pltpu.VMEM((half, GROUP * TILE), BF),
             pltpu.VMEM((half, size), F32),
         ],
         compiler_params=pltpu.CompilerParams(vmem_limit_bytes=32 << 20),

time: 32.1 us -> 32 us (level)
  no operation moved by 1% of the time
where the time goes in v6:
time: 32 us; the launch traced here: 31.8 us
  waiting for transfers between devices  14.2 us (44%)
  starting transfers between devices  13 us (41%)
  Pallas kernels  3.93 us (12%)
  other arithmetic  0.65 us (2%)
    ppermute x4, waiting for transfers between devices, turn(): lax.ppermute(x, 'mu', [(i, i ^ (2 if (i % 2 == 0) == first else 4)) for i...  6.17 us
    ppermute x4, starting transfers between devices, turn(): lax.ppermute(x, 'mu', [(i, i ^ (2 if (i % 2 == 0) == first else 4)) for i...  5.54 us
    ppermute x3, starting transfers between devices, spread(): total = total + lax.ppermute(strip_of(to), 'aux', list(enumerate(step)))  4.45 us
    ppermute x6, waiting for transfers between devices, swap(): return lax.ppermute(x, 'mu', [(i, i ^ step) for i in range(2 * CHIPS)])  4.44 us
    ppermute x3, waiting for transfers between devices, spread(): total = total + lax.ppermute(strip_of(to), 'aux', list(enumerate(step)))  3.58 us
    ppermute x6, starting transfers between devices, swap(): return lax.ppermute(x, 'mu', [(i, i ^ step) for i in range(2 * CHIPS)])  2.98 us
    pallas_call x1, Pallas kernels, spread(): pl.pallas_call(early_kernel, out_shape=[jax.ShapeDtypeStruct((GROUP * siz...  1.41 us
    pallas_call x1, Pallas kernels, spread(): pl.pallas_call(pack_kernel, out_shape=[jax.ShapeDtypeStruct((GROUP + 1, w...  1.35 us
  transfers between devices with their start and end apart: 13, of which 8 were waited for; matrix products, arithmetic and copies ran while one was open for 0% of the time, Pallas kernels for 4%

profile of v6, /device:TPU:0, one launch (start us, length us, event | category | flops | bytes accessed | tf_op | source)
XLA Modules:
  0.0 31.8 jit_solution(12239824726013961137)
XLA Ops:
  0.0 1.3 %pack.1 = (bf16[5,64,512]{2,1,0:T(8,128)(2,1)S(1)}, bf16[13,64,128]{2,1,0:T(8,128)(2,1)S(1)}, bf16[13,64,128]{2,1,0:T(8,128)(2,1)S(1)}, bf16[7,64,128]{2,1,0:T(8,128)(2,1)S(1)}) custom-call(bf16[16,64,512]{2,1,0:T(8,128)(2,1)} %b_hbm.1, bf16[64,512]{1,0:T(8,128)(2,1)} %d_hbm.1, s32[8,8]{1,0:T(8,128)} %pair_hbm.1, s32[8,8]{1,0:T(8,128)} %dens_hbm.1), custom_call_target="tpu_custom_call" | custom-call | tf_op jit(solution)/shard_map/pack/pallas_call | solution.py:215
  1.4 3.0 %collective-permute-start.1 = (bf16[13,64,128]{2,1,0:T(8,128)(2,1)S(1)}, bf16[13,64,128]{2,1,0:T(8,128)(2,1)S(1)}, u32[]{:S(2)}, u32[]{:S(2)}) collective-permute-start(bf16[13,64,128]{2,1,0:T(8,128)(2,1)S(1)} %get-tuple-element.17), channel_id=1, source_target_pairs={{0,8},{4,20},{8,0},{12,28},{16,24},{20,4},{24,16},{28,12},{1,9},{5... | collective-permute-start | bytes 638984 | tf_op jit(solution)/shard_map/ppermute | solution.py:207
  4.4 1.5 %collective-permute-start.2 = (bf16[13,64,128]{2,1,0:T(8,128)(2,1)S(1)}, bf16[13,64,128]{2,1,0:T(8,128)(2,1)S(1)}, u32[]{:S(2)}, u32[]{:S(2)}) collective-permute-start(bf16[13,64,128]{2,1,0:T(8,128)(2,1)S(1)} %get-tuple-element.18), channel_id=1, source_target_pairs={{0,16},{4,12},{8,24},{12,4},{16,0},{20,28},{24,8},{28,20},{1,17},{... | collective-permute-start | bytes 638984 | tf_op jit(solution)/shard_map/ppermute | solution.py:207
  5.9 0.0 collective-permute-start
  5.9 0.0 collective-permute-start.5
  5.9 4.0 %collective-permute-done.1.r1 = bf16[13,64,128]{2,1,0:T(8,128)(2,1)S(1)} collective-permute-done((bf16[13,64,128]{2,1,0:T(8,128)(2,1)S(1)}, bf16[13,64,128]{2,1,0:T(8,128)(2,1)S(1)}, u32[]{:S(2)}, u32[]{:S(2)}) %collective-permute-start.1) | collective-permute-done | bytes 213024 | tf_op jit(solution)/shard_map/ppermute | solution.py:207
  9.9 0.0 collective-permute-start.3
  9.9 0.6 %collective-permute-done.2.r2 = bf16[13,64,128]{2,1,0:T(8,128)(2,1)S(1)} collective-permute-done((bf16[13,64,128]{2,1,0:T(8,128)(2,1)S(1)}, bf16[13,64,128]{2,1,0:T(8,128)(2,1)S(1)}, u32[]{:S(2)}, u32[]{:S(2)}) %collective-permute-start.2) | collective-permute-done | bytes 213024 | tf_op jit(solution)/shard_map/ppermute | solution.py:207
  10.5 0.4 %collective-permute-start.4 = (bf16[13,64,128]{2,1,0:T(8,128)(2,1)S(1)}, bf16[13,64,128]{2,1,0:T(8,128)(2,1)S(1)}, u32[]{:S(2)}, u32[]{:S(2)}) collective-permute-start(bf16[13,64,128]{2,1,0:T(8,128)(2,1)S(1)} %collective-permute-done.2.r2), channel_id=1, source_target_pairs={{0,4},{4,0},{8,12},{12,8},{16,20},{20,16},{24,28},{28,24},{1,5},{5... | collective-permute-start | bytes 638984 | tf_op jit(solution)/shard_map/ppermute | solution.py:204
  10.9 2.5 %collective-permute-done.5.r3 = bf16[7,64,128]{2,1,0:T(8,128)(2,1)S(1)} collective-permute-done((bf16[7,64,128]{2,1,0:T(8,128)(2,1)S(1)}, bf16[7,64,128]{2,1,0:T(8,128)(2,1)S(1)}, u32[]{:S(2)}, u32[]{:S(2)}) %collective-permute-start.5) | collective-permute-done | bytes 114720 | tf_op jit(solution)/shard_map/ppermute | solution.py:204
  13.4 0.0 collective-permute-start.6
  13.4 0.0 collective-permute-done.mate_ref
  13.4 0.0 collective-permute-done.3.q1
  13.4 0.0 collective-permute-done.4.q2
  13.4 1.4 %early.1 = (bf16[2048,512]{1,0:T(8,128)(2,1)S(1)}, bf16[1024,128]{1,0:T(8,128)(2,1)S(1)}, f32[1024,512]{1,0:T(8,128)S(1)}) custom-call(bf16[5,64,512]{2,1,0:T(8,128)(2,1)S(1)} %get-tuple-element.16.own_ref, bf16[5,64,512]{2,1,0:T(8,128)(2,1)S(1)} %collective-permute-done.mate_ref, bf16[13,64,128]{2,1,0:T(8,128)(2,1)S(1)} %collective-permute-done.1.r1, ...), custom_call_target="tpu_custom_call" | custom-call | tf_op jit(solution)/shard_map/early/pallas_call | solution.py:235
  14.8 0.0 collective-permute-done.6.q3
  14.8 1.2 %late.1 = (bf16[64,512]{1,0:T(8,128)(2,1)S(1)}, bf16[64,512]{1,0:T(8,128)(2,1)S(1)}, bf16[64,512]{1,0:T(8,128)(2,1)S(1)}, f32[64,512]{1,0:T(8,128)S(1)}, bf16[2048,512]{1,0:T(8,128)(2,1)S(1)}) custom-call(bf16[2048,512]{1,0:T(8,128)(2,1)S(1)} %get-tuple-element.19.t_in, ...), custom_call_target="tpu_custom_call", output_to_operand_aliasing={{4}: (0, {})} | custom-call | tf_op jit(solution)/shard_map/late/pallas_call | solution.py:249
  16.0 2.5 %collective-permute-start.7 = (bf16[64,512]{1,0:T(8,128)(2,1)S(1)}, bf16[64,512]{1,0:T(8,128)(2,1)S(1)}, u32[]{:S(2)}, u32[]{:S(2)}) collective-permute-start(bf16[64,512]{1,0:T(8,128)(2,1)S(1)} %get-tuple-element.24), channel_id=1, source_target_pairs={{0,24},{4,28},{8,16},{12,20},{16,8},{20,12},{24,0},{28,4},{1,25},{... | collective-permute-start | bytes 196616 | tf_op jit(solution)/shard_map/ppermute | solution.py:204
  18.5 0.0 collective-permute-start.8
  18.5 1.0 %collective-permute-start.9 = (bf16[64,512]{1,0:T(8,128)(2,1)S(1)}, bf16[64,512]{1,0:T(8,128)(2,1)S(1)}, u32[]{:S(2)}, u32[]{:S(2)}) collective-permute-start(bf16[64,512]{1,0:T(8,128)(2,1)S(1)} %get-tuple-element.26), channel_id=1, source_target_pairs={{0,16},{4,12},{8,24},{12,4},{16,0},{20,28},{24,8},{28,20},{1,17},{... | collective-permute-start | bytes 196616 | tf_op jit(solution)/shard_map/ppermute | solution.py:207
  19.5 1.9 %collective-permute-done.7 = bf16[64,512]{1,0:T(8,128)(2,1)S(1)} collective-permute-done((bf16[64,512]{1,0:T(8,128)(2,1)S(1)}, bf16[64,512]{1,0:T(8,128)(2,1)S(1)}, u32[]{:S(2)}, u32[]{:S(2)}) %collective-permute-start.7) | collective-permute-done | bytes 65568 | tf_op jit(solution)/shard_map/ppermute | solution.py:204
  21.5 1.6 %collective-permute-done.8 = bf16[64,512]{1,0:T(8,128)(2,1)S(1)} collective-permute-done((bf16[64,512]{1,0:T(8,128)(2,1)S(1)}, bf16[64,512]{1,0:T(8,128)(2,1)S(1)}, u32[]{:S(2)}, u32[]{:S(2)}) %collective-permute-start.8) | collective-permute-done | bytes 65568 | tf_op jit(solution)/shard_map/ppermute | solution.py:207
  23.1 0.0 collective-permute-done.9
  23.2 2.9 %collective-permute-start.10 = (f32[16,512]{1,0:T(8,128)S(1)}, f32[16,512]{1,0:T(8,128)S(1)}, u32[]{:S(2)}, u32[]{:S(2)}) collective-permute-start(f32[16,512]{1,0:T(8,128)S(1)} %get-tuple-element.27), channel_id=1, source_target_pairs={{0,2},{1,3},{2,1},{3,0},{4,6},{5,7},{6,5},{7,4},{8,10},{9,11},{10,... | collective-permute-start | bytes 98312 | tf_op jit(solution)/shard_map/ppermute | solution.py:275
  26.0 1.1 %collective-permute-start.11 = (f32[16,512]{1,0:T(8,128)S(1)}, f32[16,512]{1,0:T(8,128)S(1)}, u32[]{:S(2)}, u32[]{:S(2)}) collective-permute-start(f32[16,512]{1,0:T(8,128)S(1)} %get-tuple-element.29), channel_id=1, source_target_pairs={{0,3},{1,2},{2,0},{3,1},{4,7},{5,6},{6,4},{7,5},{8,11},{9,10},{10,... | collective-permute-start | bytes 98312 | tf_op jit(solution)/shard_map/ppermute | solution.py:275
  27.1 0.5 %collective-permute-start.12 = (f32[16,512]{1,0:T(8,128)S(1)}, f32[16,512]{1,0:T(8,128)S(1)}, u32[]{:S(2)}, u32[]{:S(2)}) collective-permute-start(f32[16,512]{1,0:T(8,128)S(1)} %get-tuple-element.28), channel_id=1, source_target_pairs={{0,1},{1,0},{2,3},{3,2},{4,5},{5,4},{6,7},{7,6},{8,9},{9,8},{10,11... | collective-permute-start | bytes 98312 | tf_op jit(solution)/shard_map/ppermute | solution.py:275
  27.6 1.3 %collective-permute-done.10 = f32[16,512]{1,0:T(8,128)S(1)} collective-permute-done((f32[16,512]{1,0:T(8,128)S(1)}, f32[16,512]{1,0:T(8,128)S(1)}, u32[]{:S(2)}, u32[]{:S(2)}) %collective-permute-start.10) | collective-permute-done | bytes 32800 | tf_op jit(solution)/shard_map/ppermute | solution.py:275
  29.0 1.9 %collective-permute-done.11 = f32[16,512]{1,0:T(8,128)S(1)} collective-permute-done((f32[16,512]{1,0:T(8,128)S(1)}, f32[16,512]{1,0:T(8,128)S(1)}, u32[]{:S(2)}, u32[]{:S(2)}) %collective-permute-start.11) | collective-permute-done | bytes 32800 | tf_op jit(solution)/shard_map/ppermute | solution.py:275
  30.9 0.3 %collective-permute-done.12 = f32[16,512]{1,0:T(8,128)S(1)} collective-permute-done((f32[16,512]{1,0:T(8,128)S(1)}, f32[16,512]{1,0:T(8,128)S(1)}, u32[]{:S(2)}, u32[]{:S(2)}) %collective-permute-start.12) | collective-permute-done | bytes 32800 | tf_op jit(solution)/shard_map/ppermute | solution.py:275
  31.2 0.6 %add_add_fusion = f32[16,512]{1,0:T(8,128)} fusion(f32[16,512]{1,0:T(8,128)S(1)} %collective-permute-done.12, f32[16,512]{1,0:T(8,128)S(1)} %collective-permute-done.11, f32[16,512]{1,0:T(8,128)S(1)} %collective-permute-done.10, f32[64,512]{1,0:T(8,128)S(1)} %convert_add_fusion, s32[]{:T(128)S(6)} %select_n.43), kind=kLoop, calls=%fused_computation.1 | loop fusion | flops 24576 | bytes 163844 | tf_op jit(solution)/shard_map/add | solution.py:275
  (2 shorter events, 0.0 us)
Async XLA Ops:
  1.4 8.5 %collective-permute-start.1 = (bf16[13,64,128]{2,1,0:T(8,128)(2,1)S(1)}, bf16[13,64,128]{2,1,0:T(8,128)(2,1)S(1)}, u32[]{:S(2)}, u32[]{:S(2)}) collective-permute-start(bf16[13,64,128]{2,1,0:T(8,128)(2,1)S(1)} %get-tuple-element.17), channel_id=1, source_target_pairs={{0,8},{4,20},{8,0},{12,28},{16,24},{20,4},{24,16},{28,12},{1,9},{5... | collective-permute-start | bytes 638984 | tf_op jit(solution)/shard_map/ppermute | solution.py:207
  4.4 6.1 %collective-permute-start.2 = (bf16[13,64,128]{2,1,0:T(8,128)(2,1)S(1)}, bf16[13,64,128]{2,1,0:T(8,128)(2,1)S(1)}, u32[]{:S(2)}, u32[]{:S(2)}) collective-permute-start(bf16[13,64,128]{2,1,0:T(8,128)(2,1)S(1)} %get-tuple-element.18), channel_id=1, source_target_pairs={{0,16},{4,12},{8,24},{12,4},{16,0},{20,28},{24,8},{28,20},{1,17},{... | collective-permute-start | bytes 638984 | tf_op jit(solution)/shard_map/ppermute | solution.py:207
  5.9 7.5 %collective-permute-start = (bf16[5,64,512]{2,1,0:T(8,128)(2,1)S(1)}, bf16[5,64,512]{2,1,0:T(8,128)(2,1)S(1)}, u32[]{:S(2)}, u32[]{:S(2)}) collective-permute-start(bf16[5,64,512]{2,1,0:T(8,128)(2,1)S(1)} %get-tuple-element.16.own_ref), channel_id=1, source_target_pairs={{0,4},{4,0},{8,12},{12,8},{16,20},{20,16},{24,28},{28,24},{1,5},{5... | collective-permute-start | bytes 983048 | tf_op jit(solution)/shard_map/ppermute | solution.py:204
  5.9 7.5 %collective-permute-start.5 = (bf16[7,64,128]{2,1,0:T(8,128)(2,1)S(1)}, bf16[7,64,128]{2,1,0:T(8,128)(2,1)S(1)}, u32[]{:S(2)}, u32[]{:S(2)}) collective-permute-start(bf16[7,64,128]{2,1,0:T(8,128)(2,1)S(1)} %get-tuple-element.22), channel_id=1, source_target_pairs={{0,24},{4,28},{8,16},{12,20},{16,8},{20,12},{24,0},{28,4},{1,25},{... | collective-permute-start | bytes 344072 | tf_op jit(solution)/shard_map/ppermute | solution.py:204
  9.9 3.5 %collective-permute-start.3 = (bf16[13,64,128]{2,1,0:T(8,128)(2,1)S(1)}, bf16[13,64,128]{2,1,0:T(8,128)(2,1)S(1)}, u32[]{:S(2)}, u32[]{:S(2)}) collective-permute-start(bf16[13,64,128]{2,1,0:T(8,128)(2,1)S(1)} %collective-permute-done.1.r1), channel_id=1, source_target_pairs={{0,4},{4,0},{8,12},{12,8},{16,20},{20,16},{24,28},{28,24},{1,5},{5... | collective-permute-start | bytes 638984 | tf_op jit(solution)/shard_map/ppermute | solution.py:204
  10.5 2.9 %collective-permute-start.4 = (bf16[13,64,128]{2,1,0:T(8,128)(2,1)S(1)}, bf16[13,64,128]{2,1,0:T(8,128)(2,1)S(1)}, u32[]{:S(2)}, u32[]{:S(2)}) collective-permute-start(bf16[13,64,128]{2,1,0:T(8,128)(2,1)S(1)} %collective-permute-done.2.r2), channel_id=1, source_target_pairs={{0,4},{4,0},{8,12},{12,8},{16,20},{20,16},{24,28},{28,24},{1,5},{5... | collective-permute-start | bytes 638984 | tf_op jit(solution)/shard_map/ppermute | solution.py:204
  13.4 1.4 %collective-permute-start.6 = (bf16[7,64,128]{2,1,0:T(8,128)(2,1)S(1)}, bf16[7,64,128]{2,1,0:T(8,128)(2,1)S(1)}, u32[]{:S(2)}, u32[]{:S(2)}) collective-permute-start(bf16[7,64,128]{2,1,0:T(8,128)(2,1)S(1)} %collective-permute-done.5.r3), channel_id=1, source_target_pairs={{0,4},{4,0},{8,12},{12,8},{16,20},{20,16},{24,28},{28,24},{1,5},{5... | collective-permute-start | bytes 344072 | tf_op jit(solution)/shard_map/ppermute | solution.py:204
  16.0 5.5 %collective-permute-start.7 = (bf16[64,512]{1,0:T(8,128)(2,1)S(1)}, bf16[64,512]{1,0:T(8,128)(2,1)S(1)}, u32[]{:S(2)}, u32[]{:S(2)}) collective-permute-start(bf16[64,512]{1,0:T(8,128)(2,1)S(1)} %get-tuple-element.24), channel_id=1, source_target_pairs={{0,24},{4,28},{8,16},{12,20},{16,8},{20,12},{24,0},{28,4},{1,25},{... | collective-permute-start | bytes 196616 | tf_op jit(solution)/shard_map/ppermute | solution.py:204
  18.5 4.6 %collective-permute-start.8 = (bf16[64,512]{1,0:T(8,128)(2,1)S(1)}, bf16[64,512]{1,0:T(8,128)(2,1)S(1)}, u32[]{:S(2)}, u32[]{:S(2)}) collective-permute-start(bf16[64,512]{1,0:T(8,128)(2,1)S(1)} %get-tuple-element.25), channel_id=1, source_target_pairs={{0,8},{4,20},{8,0},{12,28},{16,24},{20,4},{24,16},{28,12},{1,9},{5... | collective-permute-start | bytes 196616 | tf_op jit(solution)/shard_map/ppermute | solution.py:207
  18.5 4.6 %collective-permute-start.9 = (bf16[64,512]{1,0:T(8,128)(2,1)S(1)}, bf16[64,512]{1,0:T(8,128)(2,1)S(1)}, u32[]{:S(2)}, u32[]{:S(2)}) collective-permute-start(bf16[64,512]{1,0:T(8,128)(2,1)S(1)} %get-tuple-element.26), channel_id=1, source_target_pairs={{0,16},{4,12},{8,24},{12,4},{16,0},{20,28},{24,8},{28,20},{1,17},{... | collective-permute-start | bytes 196616 | tf_op jit(solution)/shard_map/ppermute | solution.py:207
  23.2 5.8 %collective-permute-start.10 = (f32[16,512]{1,0:T(8,128)S(1)}, f32[16,512]{1,0:T(8,128)S(1)}, u32[]{:S(2)}, u32[]{:S(2)}) collective-permute-start(f32[16,512]{1,0:T(8,128)S(1)} %get-tuple-element.27), channel_id=1, source_target_pairs={{0,2},{1,3},{2,1},{3,0},{4,6},{5,7},{6,5},{7,4},{8,10},{9,11},{10,... | collective-permute-start | bytes 98312 | tf_op jit(solution)/shard_map/ppermute | solution.py:275
  26.0 4.8 %collective-permute-start.11 = (f32[16,512]{1,0:T(8,128)S(1)}, f32[16,512]{1,0:T(8,128)S(1)}, u32[]{:S(2)}, u32[]{:S(2)}) collective-permute-start(f32[16,512]{1,0:T(8,128)S(1)} %get-tuple-element.29), channel_id=1, source_target_pairs={{0,3},{1,2},{2,0},{3,1},{4,7},{5,6},{6,4},{7,5},{8,11},{9,10},{10,... | collective-permute-start | bytes 98312 | tf_op jit(solution)/shard_map/ppermute | solution.py:275
  27.1 4.1 %collective-permute-start.12 = (f32[16,512]{1,0:T(8,128)S(1)}, f32[16,512]{1,0:T(8,128)S(1)}, u32[]{:S(2)}, u32[]{:S(2)}) collective-permute-start(f32[16,512]{1,0:T(8,128)S(1)} %get-tuple-element.28), channel_id=1, source_target_pairs={{0,1},{1,0},{2,3},{3,2},{4,5},{5,4},{6,7},{7,6},{8,9},{9,8},{10,11... | collective-permute-start | bytes 98312 | tf_op jit(solution)/shard_map/ppermute | solution.py:275

commit v7 on v5

--- a/solution.py
+++ b/solution.py
@@ -10,9 +10,14 @@
 BLK = 64
 TILE = 2 * BLK
 CHIPS = 4
+LAYERS = 4
+STRIP = BLK // LAYERS
+Z_FIRST = 1
+ALONG_ONE = ((3, 2, 1, 0), (1, 0, 3, 2), (2, 3, 0, 1))
+PLANE_TWO = ((3, 2, 1, 0), (1, 0, 3, 2), (2, 3, 0, 1))
+PLANE_ONE = ((1, 3, 0, 2), (3, 2, 1, 0), (2, 0, 3, 1))
+ALONG_TWO = ((2, 3, 1, 0), (3, 2, 0, 1), (1, 0, 3, 2))
 GROUP = 4
-PLANE = ((1, 3, 0, 2), (3, 2, 1, 0), (2, 0, 3, 1))
-STEPS = ((2, 3, 1, 0), (3, 2, 0, 1), (1, 0, 3, 2))
 NEAR = 13
 FAR = 7
 
@@ -198,10 +203,26 @@
         xg_scr[:, p * TILE : (p + 1) * TILE] = x_scr[:, pl.ds(pl.multiple_of(p * size + cg * TILE, TILE), TILE)]
     k_scr[...] = jnp.dot(x_scr[...], t_ref[...], preferred_element_type=F32)
     k_scr[:, column(cg)] += jnp.dot(xg_scr[...], g_scr[...], preferred_element_type=F32)
-    for out, step in zip((e1, e2, e3), PLANE):
-        to = sum(jnp.where(c == i, j, 0) for i, j in enumerate(step))
-        out[...] = k_scr[pl.ds(pl.multiple_of(to * BLK, BLK), BLK), :].astype(BF)
-    keep_ref[...] = k_scr[pl.ds(pl.multiple_of(c * BLK, BLK), BLK), :]
+
+    @pl.when(k != Z_FIRST)
+    def _():
+        for out, step in zip((e1, e2, e3), PLANE_ONE):
+            out[...] = k_scr[pl.ds(pl.multiple_of(goal(step, c) * BLK, BLK), BLK), :].astype(BF)
+        keep_ref[...] = k_scr[pl.ds(pl.multiple_of(c * BLK, BLK), BLK), :]
+
+    @pl.when(k == Z_FIRST)
+    def _():
+        a = lax.axis_index("aux")
+        for r in range(CHIPS):
+            into = slice(r * STRIP, (r + 1) * STRIP)
+            for out, step in zip((e1, e2, e3), ALONG_ONE):
+                at = pl.ds(pl.multiple_of(r * BLK + goal(step, a) * STRIP, STRIP), STRIP)
+                out[into, :] = k_scr[at, :].astype(BF)
+            keep_ref[into, :] = k_scr[pl.ds(pl.multiple_of(r * BLK + a * STRIP, STRIP), STRIP), :]
+
+
+def goal(step, place):
+    return sum(jnp.where(place == i, j, 0) for i, j in enumerate(step))
 
 
 def spread(b_tensor, density, pair_mask, dens_mask):
@@ -288,20 +309,33 @@
         compiler_params=pltpu.CompilerParams(vmem_limit_bytes=32 << 20),
         name="late",
     )(*early, r3, q3)
-    plane = keep
-    for part, step in zip(parts, PLANE):
-        pairs = [(2 * i + core, 2 * j + core) for i, j in enumerate(step) for core in (0, 1)]
-        plane = plane + lax.ppermute(part, "mu", pairs).astype(F32)
-    a = lax.axis_index("aux")
-    strip = width // 4
+
+    def cross(x, plane, along, z_core):
+        pairs = []
+        for i in range(2 * CHIPS * LAYERS):
+            mu, a = divmod(i, LAYERS)
+            c, k = divmod(mu, 2)
+            if k == z_core:
+                pairs.append((i, mu * LAYERS + along[a]))
+            else:
+                pairs.append((i, (2 * plane[c] + k) * LAYERS + a))
+        return lax.ppermute(x, ("mu", "aux"), pairs)
+
+    once = keep
+    for part, plane, along in zip(parts, PLANE_ONE, ALONG_ONE):
+        once = once + cross(part, plane, along, Z_FIRST).astype(F32)
+    once = once.reshape(CHIPS, STRIP, size)
+    me = lax.axis_index("mu")
+    z_now = me % 2 != Z_FIRST
+    c, a = me // 2, lax.axis_index("aux")
 
     def strip_of(index):
-        return lax.dynamic_slice_in_dim(plane, index * strip, strip, 0)
-
-    total = strip_of(a)
-    for step in STEPS:
-        to = sum(jnp.where(a == i, j, 0) for i, j in enumerate(step))
-        total = total + lax.ppermute(strip_of(to), "aux", list(enumerate(step)))
+        return lax.dynamic_index_in_dim(once, index, 0, keepdims=False)
+
+    total = strip_of(jnp.where(z_now, a, c))
+    for plane, along in zip(PLANE_TWO, ALONG_TWO):
+        to = jnp.where(z_now, goal(along, a), goal(plane, c))
+        total = total + cross(strip_of(to), plane, along, 1 - Z_FIRST)
     return total
 
 
@@ -334,7 +368,7 @@
 
     def per_device(b_tensor, density, pair_mask, dens_mask):
         depth, width, size = b_tensor.shape
-        fits = mesh.shape["mu"] == 2 * CHIPS and mesh.shape["aux"] == 4
+        fits = mesh.shape["mu"] == 2 * CHIPS and mesh.shape["aux"] == LAYERS
         fits = fits and depth == GROUP * CHIPS and width == BLK and size == 2 * CHIPS * BLK
         step = spread if fits else gathered
         return step(b_tensor, density, pair_mask, dens_mask)

time: 32 us -> 32 us (level)
  waiting for transfers between devices: 12.5 us -> 12.1 us
    ppermute x6, waiting for transfers between devices: 6.3 us -> 5.91 us  [cross(): return lax.ppermute(x, ('mu', 'aux'), pairs)]
    ppermute x6, starting transfers between devices: 8.77 us -> 9.16 us  [cross(): return lax.ppermute(x, ('mu', 'aux'), pairs)]
  transfers between devices with their start and end apart: 13 -> 13, of which waited for: 9 -> 7; matrix products, arithmetic and copies ran while one was open for 0% -> 0% of each run, Pallas kernels for 8% -> 8%
where the time goes in v7:
time: 32 us; the launch traced here: 31.8 us
  starting transfers between devices  14 us (44%)
  waiting for transfers between devices  12.1 us (38%)
  Pallas kernels  4.94 us (15%)
  other arithmetic  0.65 us (2%)
    ppermute x6, starting transfers between devices, cross(): return lax.ppermute(x, ('mu', 'aux'), pairs)  9.16 us
    ppermute x6, waiting for transfers between devices, cross(): return lax.ppermute(x, ('mu', 'aux'), pairs)  5.91 us
    ppermute x2, starting transfers between devices, turn(): lax.ppermute(x, 'mu', [(i, i ^ (2 if (i % 2 == 0) == first else 4)) for i...  4.52 us
    ppermute x2, waiting for transfers between devices, turn(): lax.ppermute(x, 'mu', [(i, i ^ (2 if (i % 2 == 0) == first else 4)) for i...  3.14 us
    ppermute x5, waiting for transfers between devices, swap(): return lax.ppermute(x, 'mu', [(i, i ^ step) for i in range(2 * CHIPS)])  3.03 us
    pallas_call x1, Pallas kernels, spread(): pl.pallas_call(early_kernel, out_shape=[jax.ShapeDtypeStruct((GROUP * siz...  1.41 us
    pallas_call x1, Pallas kernels, spread(): pl.pallas_call(late_kernel, out_shape=[chunk, chunk, chunk, jax.ShapeDtyp...  1.28 us
    pallas_call x1, Pallas kernels, spread(): pl.pallas_call(pack_kernel, out_shape=[slots(NEAR), slots(NEAR), slots(FA...  1.24 us
  transfers between devices with their start and end apart: 13, of which 7 were waited for; matrix products, arithmetic and copies ran while one was open for 0% of the time, Pallas kernels for 8%

profile of v7, /device:TPU:0, one launch (start us, length us, event | category | flops | bytes accessed | tf_op | source)
XLA Modules:
  0.0 31.8 jit_solution(10580865449324764755)
XLA Ops:
  0.0 1.2 %pack.1 = (bf16[13,64,128]{2,1,0:T(8,128)(2,1)S(1)}, bf16[13,64,128]{2,1,0:T(8,128)(2,1)S(1)}, bf16[7,64,128]{2,1,0:T(8,128)(2,1)S(1)}, bf16[64,512]{1,0:T(8,128)(2,1)S(1)}, f32[4,1,128]{2,1,0:T(1,128)S(1)}) custom-call(bf16[16,64,512]{2,1,0:T(8,128)(2,1)} %b_hbm.3, bf16[64,512]{1,0:T(8,128)(2,1)} %d_hbm.1, s32[8,8]{1,0:T(8,128)} %pair_hbm.1, s32[8,8]{1,0:T(8,128)} %dens_hbm.1), custom_call_target="tpu_custom_call" | custom-call | tf_op jit(solution)/shard_map/pack/pallas_call | solution.py:248
  1.2 3.0 %collective-permute-start.1 = (bf16[13,64,128]{2,1,0:T(8,128)(2,1)S(1)}, bf16[13,64,128]{2,1,0:T(8,128)(2,1)S(1)}, u32[]{:S(2)}, u32[]{:S(2)}) collective-permute-start(bf16[13,64,128]{2,1,0:T(8,128)(2,1)S(1)} %get-tuple-element.19), channel_id=1, source_target_pairs={{0,8},{4,20},{8,0},{12,28},{16,24},{20,4},{24,16},{28,12},{1,9},{5... | collective-permute-start | bytes 638984 | tf_op jit(solution)/shard_map/ppermute | solution.py:237
  4.3 1.5 %collective-permute-start.2 = (bf16[13,64,128]{2,1,0:T(8,128)(2,1)S(1)}, bf16[13,64,128]{2,1,0:T(8,128)(2,1)S(1)}, u32[]{:S(2)}, u32[]{:S(2)}) collective-permute-start(bf16[13,64,128]{2,1,0:T(8,128)(2,1)S(1)} %get-tuple-element.20), channel_id=1, source_target_pairs={{0,16},{4,12},{8,24},{12,4},{16,0},{20,28},{24,8},{28,20},{1,17},{... | collective-permute-start | bytes 638984 | tf_op jit(solution)/shard_map/ppermute | solution.py:237
  5.8 1.0 %own.1.own_ref = bf16[5,64,512]{2,1,0:T(8,128)(2,1)S(1)} custom-call(bf16[16,64,512]{2,1,0:T(8,128)(2,1)} %b_hbm.3, bf16[64,512]{1,0:T(8,128)(2,1)S(1)} %get-tuple-element.17.mine_ref, f32[4,1,128]{2,1,0:T(1,128)S(1)} %get-tuple-element.18.line_ref), custom_call_target="tpu_custom_call" | custom-call | tf_op jit(solution)/shard_map/own/pallas_call | solution.py:269
  6.8 0.1 collective-permute-start
  6.9 0.1 collective-permute-start.5
  7.0 2.8 %collective-permute-done.1.r1 = bf16[13,64,128]{2,1,0:T(8,128)(2,1)S(1)} collective-permute-done((bf16[13,64,128]{2,1,0:T(8,128)(2,1)S(1)}, bf16[13,64,128]{2,1,0:T(8,128)(2,1)S(1)}, u32[]{:S(2)}, u32[]{:S(2)}) %collective-permute-start.1) | collective-permute-done | bytes 213024 | tf_op jit(solution)/shard_map/ppermute | solution.py:237
  9.8 0.0 collective-permute-start.3
  9.8 0.3 collective-permute-done.2.r2
  10.1 0.2 collective-permute-start.4
  10.3 3.0 %collective-permute-done.5.r3 = bf16[7,64,128]{2,1,0:T(8,128)(2,1)S(1)} collective-permute-done((bf16[7,64,128]{2,1,0:T(8,128)(2,1)S(1)}, bf16[7,64,128]{2,1,0:T(8,128)(2,1)S(1)}, u32[]{:S(2)}, u32[]{:S(2)}) %collective-permute-start.5) | collective-permute-done | bytes 114720 | tf_op jit(solution)/shard_map/ppermute | solution.py:234
  13.3 0.0 collective-permute-start.6
  13.3 0.0 collective-permute-done.mate_ref
  13.3 0.0 collective-permute-done.3.q1
  13.3 0.0 collective-permute-done.4.q2
  13.4 1.4 %early.1 = (bf16[2048,512]{1,0:T(8,128)(2,1)S(1)}, bf16[1024,128]{1,0:T(8,128)(2,1)S(1)}, f32[1024,512]{1,0:T(8,128)S(1)}) custom-call(bf16[5,64,512]{2,1,0:T(8,128)(2,1)S(1)} %own.1.own_ref, bf16[5,64,512]{2,1,0:T(8,128)(2,1)S(1)} %collective-permute-done.mate_ref, bf16[13,64,128]{2,1,0:T(8,128)(2,1)S(1)} %collective-permute-done.1.r1, ...), custom_call_target="tpu_custom_call" | custom-call | tf_op jit(solution)/shard_map/early/pallas_call | solution.py:282
  14.8 0.0 collective-permute-done.6.q3
  14.8 1.3 %late.1 = (bf16[64,512]{1,0:T(8,128)(2,1)S(1)}, bf16[64,512]{1,0:T(8,128)(2,1)S(1)}, bf16[64,512]{1,0:T(8,128)(2,1)S(1)}, f32[64,512]{1,0:T(8,128)S(1)}) custom-call(bf16[2048,512]{1,0:T(8,128)(2,1)S(1)} %get-tuple-element.21.t_ref, bf16[1024,128]{1,0:T(8,128)(2,1)S(1)} %get-tuple-element.22.l_ref, f32[1024,512]{1,0:T(8,128)S(1)} %get-tuple-element.23.xp_ref, ...), custom_call_target="tpu_custom_call" | custom-call | tf_op jit(solution)/shard_map/late/pallas_call | solution.py:296
  16.1 1.6 %collective-permute-start.7 = (bf16[64,512]{1,0:T(8,128)(2,1)S(1)}, bf16[64,512]{1,0:T(8,128)(2,1)S(1)}, u32[]{:S(2)}, u32[]{:S(2)}) collective-permute-start(bf16[64,512]{1,0:T(8,128)(2,1)S(1)} %get-tuple-element.26), channel_id=1, source_target_pairs={{0,8},{1,9},{2,10},{3,11},{4,7},{5,6},{6,5},{7,4},{8,24},{9,25},{1... | collective-permute-start | bytes 196616 | tf_op jit(solution)/shard_map/ppermute | solution.py:322
  17.7 0.9 %collective-permute-start.8 = (bf16[64,512]{1,0:T(8,128)(2,1)S(1)}, bf16[64,512]{1,0:T(8,128)(2,1)S(1)}, u32[]{:S(2)}, u32[]{:S(2)}) collective-permute-start(bf16[64,512]{1,0:T(8,128)(2,1)S(1)} %get-tuple-element.27), channel_id=1, source_target_pairs={{0,24},{1,25},{2,26},{3,27},{4,5},{5,4},{6,7},{7,6},{8,16},{9,17},... | collective-permute-start | bytes 196616 | tf_op jit(solution)/shard_map/ppermute | solution.py:322
  18.6 1.9 %collective-permute-start.9 = (bf16[64,512]{1,0:T(8,128)(2,1)S(1)}, bf16[64,512]{1,0:T(8,128)(2,1)S(1)}, u32[]{:S(2)}, u32[]{:S(2)}) collective-permute-start(bf16[64,512]{1,0:T(8,128)(2,1)S(1)} %get-tuple-element.28), channel_id=1, source_target_pairs={{0,16},{1,17},{2,18},{3,19},{4,6},{5,7},{6,4},{7,5},{8,0},{9,1},{1... | collective-permute-start | bytes 196616 | tf_op jit(solution)/shard_map/ppermute | solution.py:322
  20.5 0.0 collective-permute-done.7
  20.5 2.3 %collective-permute-done.8 = bf16[64,512]{1,0:T(8,128)(2,1)S(1)} collective-permute-done((bf16[64,512]{1,0:T(8,128)(2,1)S(1)}, bf16[64,512]{1,0:T(8,128)(2,1)S(1)}, u32[]{:S(2)}, u32[]{:S(2)}) %collective-permute-start.8) | collective-permute-done | bytes 65568 | tf_op jit(solution)/shard_map/ppermute | solution.py:322
  22.8 0.0 collective-permute-done.9
  22.9 3.1 %collective-permute-start.10 = (f32[16,512]{1,0:T(8,128)S(1)}, f32[16,512]{1,0:T(8,128)S(1)}, u32[]{:S(2)}, u32[]{:S(2)}) collective-permute-start(f32[16,512]{1,0:T(8,128)S(1)} %get-tuple-element.29), channel_id=1, source_target_pairs={{0,2},{1,3},{2,1},{3,0},{4,28},{5,29},{6,30},{7,31},{8,10},{9,11},... | collective-permute-start | bytes 98312 | tf_op jit(solution)/shard_map/ppermute | solution.py:322
  26.0 1.1 %collective-permute-start.11 = (f32[16,512]{1,0:T(8,128)S(1)}, f32[16,512]{1,0:T(8,128)S(1)}, u32[]{:S(2)}, u32[]{:S(2)}) collective-permute-start(f32[16,512]{1,0:T(8,128)S(1)} %get-tuple-element.31), channel_id=1, source_target_pairs={{0,3},{1,2},{2,0},{3,1},{4,12},{5,13},{6,14},{7,15},{8,11},{9,10},... | collective-permute-start | bytes 98312 | tf_op jit(solution)/shard_map/ppermute | solution.py:322
  27.1 0.5 %collective-permute-start.12 = (f32[16,512]{1,0:T(8,128)S(1)}, f32[16,512]{1,0:T(8,128)S(1)}, u32[]{:S(2)}, u32[]{:S(2)}) collective-permute-start(f32[16,512]{1,0:T(8,128)S(1)} %get-tuple-element.30), channel_id=1, source_target_pairs={{0,1},{1,0},{2,3},{3,2},{4,20},{5,21},{6,22},{7,23},{8,9},{9,8},{1... | collective-permute-start | bytes 98312 | tf_op jit(solution)/shard_map/ppermute | solution.py:322
  27.6 1.3 %collective-permute-done.10 = f32[16,512]{1,0:T(8,128)S(1)} collective-permute-done((f32[16,512]{1,0:T(8,128)S(1)}, f32[16,512]{1,0:T(8,128)S(1)}, u32[]{:S(2)}, u32[]{:S(2)}) %collective-permute-start.10) | collective-permute-done | bytes 32800 | tf_op jit(solution)/shard_map/ppermute | solution.py:322
  28.9 1.9 %collective-permute-done.11 = f32[16,512]{1,0:T(8,128)S(1)} collective-permute-done((f32[16,512]{1,0:T(8,128)S(1)}, f32[16,512]{1,0:T(8,128)S(1)}, u32[]{:S(2)}, u32[]{:S(2)}) %collective-permute-start.11) | collective-permute-done | bytes 32800 | tf_op jit(solution)/shard_map/ppermute | solution.py:322
  30.9 0.3 %collective-permute-done.12 = f32[16,512]{1,0:T(8,128)S(1)} collective-permute-done((f32[16,512]{1,0:T(8,128)S(1)}, f32[16,512]{1,0:T(8,128)S(1)}, u32[]{:S(2)}, u32[]{:S(2)}) %collective-permute-start.12) | collective-permute-done | bytes 32800 | tf_op jit(solution)/shard_map/ppermute | solution.py:322
  31.2 0.6 %fusion.1 = f32[16,512]{1,0:T(8,128)} fusion(f32[16,512]{1,0:T(8,128)S(1)} %collective-permute-done.12, f32[16,512]{1,0:T(8,128)S(1)} %collective-permute-done.11, f32[16,512]{1,0:T(8,128)S(1)} %collective-permute-done.10, f32[4,16,512]{2,1,0:T(8,128)S(1)} %bitcast.14, s32[]{:T(128)S(6)} %select_n.102), kind=kLoop, calls=%fused_computation.3 | loop fusion | flops 24576 | bytes 163844 | tf_op jit(solution)/shard_map/add | solution.py:338
  (2 shorter events, 0.1 us)
Async XLA Ops:
  1.2 8.5 %collective-permute-start.1 = (bf16[13,64,128]{2,1,0:T(8,128)(2,1)S(1)}, bf16[13,64,128]{2,1,0:T(8,128)(2,1)S(1)}, u32[]{:S(2)}, u32[]{:S(2)}) collective-permute-start(bf16[13,64,128]{2,1,0:T(8,128)(2,1)S(1)} %get-tuple-element.19), channel_id=1, source_target_pairs={{0,8},{4,20},{8,0},{12,28},{16,24},{20,4},{24,16},{28,12},{1,9},{5... | collective-permute-start | bytes 638984 | tf_op jit(solution)/shard_map/ppermute | solution.py:237
  4.3 5.8 %collective-permute-start.2 = (bf16[13,64,128]{2,1,0:T(8,128)(2,1)S(1)}, bf16[13,64,128]{2,1,0:T(8,128)(2,1)S(1)}, u32[]{:S(2)}, u32[]{:S(2)}) collective-permute-start(bf16[13,64,128]{2,1,0:T(8,128)(2,1)S(1)} %get-tuple-element.20), channel_id=1, source_target_pairs={{0,16},{4,12},{8,24},{12,4},{16,0},{20,28},{24,8},{28,20},{1,17},{... | collective-permute-start | bytes 638984 | tf_op jit(solution)/shard_map/ppermute | solution.py:237
  6.8 6.5 %collective-permute-start = (bf16[5,64,512]{2,1,0:T(8,128)(2,1)S(1)}, bf16[5,64,512]{2,1,0:T(8,128)(2,1)S(1)}, u32[]{:S(2)}, u32[]{:S(2)}) collective-permute-start(bf16[5,64,512]{2,1,0:T(8,128)(2,1)S(1)} %own.1.own_ref), channel_id=1, source_target_pairs={{0,4},{4,0},{8,12},{12,8},{16,20},{20,16},{24,28},{28,24},{1,5},{5... | collective-permute-start | bytes 983048 | tf_op jit(solution)/shard_map/ppermute | solution.py:234
  6.9 6.5 %collective-permute-start.5 = (bf16[7,64,128]{2,1,0:T(8,128)(2,1)S(1)}, bf16[7,64,128]{2,1,0:T(8,128)(2,1)S(1)}, u32[]{:S(2)}, u32[]{:S(2)}) collective-permute-start(bf16[7,64,128]{2,1,0:T(8,128)(2,1)S(1)} %get-tuple-element.24), channel_id=1, source_target_pairs={{0,24},{4,28},{8,16},{12,20},{16,8},{20,12},{24,0},{28,4},{1,25},{... | collective-permute-start | bytes 344072 | tf_op jit(solution)/shard_map/ppermute | solution.py:234
  9.8 3.5 %collective-permute-start.3 = (bf16[13,64,128]{2,1,0:T(8,128)(2,1)S(1)}, bf16[13,64,128]{2,1,0:T(8,128)(2,1)S(1)}, u32[]{:S(2)}, u32[]{:S(2)}) collective-permute-start(bf16[13,64,128]{2,1,0:T(8,128)(2,1)S(1)} %collective-permute-done.1.r1), channel_id=1, source_target_pairs={{0,4},{4,0},{8,12},{12,8},{16,20},{20,16},{24,28},{28,24},{1,5},{5... | collective-permute-start | bytes 638984 | tf_op jit(solution)/shard_map/ppermute | solution.py:234
  10.1 3.2 %collective-permute-start.4 = (bf16[13,64,128]{2,1,0:T(8,128)(2,1)S(1)}, bf16[13,64,128]{2,1,0:T(8,128)(2,1)S(1)}, u32[]{:S(2)}, u32[]{:S(2)}) collective-permute-start(bf16[13,64,128]{2,1,0:T(8,128)(2,1)S(1)} %collective-permute-done.2.r2), channel_id=1, source_target_pairs={{0,4},{4,0},{8,12},{12,8},{16,20},{20,16},{24,28},{28,24},{1,5},{5... | collective-permute-start | bytes 638984 | tf_op jit(solution)/shard_map/ppermute | solution.py:234
  13.3 1.4 %collective-permute-start.6 = (bf16[7,64,128]{2,1,0:T(8,128)(2,1)S(1)}, bf16[7,64,128]{2,1,0:T(8,128)(2,1)S(1)}, u32[]{:S(2)}, u32[]{:S(2)}) collective-permute-start(bf16[7,64,128]{2,1,0:T(8,128)(2,1)S(1)} %collective-permute-done.5.r3), channel_id=1, source_target_pairs={{0,4},{4,0},{8,12},{12,8},{16,20},{20,16},{24,28},{28,24},{1,5},{5... | collective-permute-start | bytes 344072 | tf_op jit(solution)/shard_map/ppermute | solution.py:234
  16.1 4.5 %collective-permute-start.7 = (bf16[64,512]{1,0:T(8,128)(2,1)S(1)}, bf16[64,512]{1,0:T(8,128)(2,1)S(1)}, u32[]{:S(2)}, u32[]{:S(2)}) collective-permute-start(bf16[64,512]{1,0:T(8,128)(2,1)S(1)} %get-tuple-element.26), channel_id=1, source_target_pairs={{0,8},{1,9},{2,10},{3,11},{4,7},{5,6},{6,5},{7,4},{8,24},{9,25},{1... | collective-permute-start | bytes 196616 | tf_op jit(solution)/shard_map/ppermute | solution.py:322
  17.7 5.2 %collective-permute-start.8 = (bf16[64,512]{1,0:T(8,128)(2,1)S(1)}, bf16[64,512]{1,0:T(8,128)(2,1)S(1)}, u32[]{:S(2)}, u32[]{:S(2)}) collective-permute-start(bf16[64,512]{1,0:T(8,128)(2,1)S(1)} %get-tuple-element.27), channel_id=1, source_target_pairs={{0,24},{1,25},{2,26},{3,27},{4,5},{5,4},{6,7},{7,6},{8,16},{9,17},... | collective-permute-start | bytes 196616 | tf_op jit(solution)/shard_map/ppermute | solution.py:322
  18.6 4.3 %collective-permute-start.9 = (bf16[64,512]{1,0:T(8,128)(2,1)S(1)}, bf16[64,512]{1,0:T(8,128)(2,1)S(1)}, u32[]{:S(2)}, u32[]{:S(2)}) collective-permute-start(bf16[64,512]{1,0:T(8,128)(2,1)S(1)} %get-tuple-element.28), channel_id=1, source_target_pairs={{0,16},{1,17},{2,18},{3,19},{4,6},{5,7},{6,4},{7,5},{8,0},{9,1},{1... | collective-permute-start | bytes 196616 | tf_op jit(solution)/shard_map/ppermute | solution.py:322
  22.9 6.0 %collective-permute-start.10 = (f32[16,512]{1,0:T(8,128)S(1)}, f32[16,512]{1,0:T(8,128)S(1)}, u32[]{:S(2)}, u32[]{:S(2)}) collective-permute-start(f32[16,512]{1,0:T(8,128)S(1)} %get-tuple-element.29), channel_id=1, source_target_pairs={{0,2},{1,3},{2,1},{3,0},{4,28},{5,29},{6,30},{7,31},{8,10},{9,11},... | collective-permute-start | bytes 98312 | tf_op jit(solution)/shard_map/ppermute | solution.py:322
  26.0 4.8 %collective-permute-start.11 = (f32[16,512]{1,0:T(8,128)S(1)}, f32[16,512]{1,0:T(8,128)S(1)}, u32[]{:S(2)}, u32[]{:S(2)}) collective-permute-start(f32[16,512]{1,0:T(8,128)S(1)} %get-tuple-element.31), channel_id=1, source_target_pairs={{0,3},{1,2},{2,0},{3,1},{4,12},{5,13},{6,14},{7,15},{8,11},{9,10},... | collective-permute-start | bytes 98312 | tf_op jit(solution)/shard_map/ppermute | solution.py:322
  27.1 4.1 %collective-permute-start.12 = (f32[16,512]{1,0:T(8,128)S(1)}, f32[16,512]{1,0:T(8,128)S(1)}, u32[]{:S(2)}, u32[]{:S(2)}) collective-permute-start(f32[16,512]{1,0:T(8,128)S(1)} %get-tuple-element.30), channel_id=1, source_target_pairs={{0,1},{1,0},{2,3},{3,2},{4,20},{5,21},{6,22},{7,23},{8,9},{9,8},{1... | collective-permute-start | bytes 98312 | tf_op jit(solution)/shard_map/ppermute | solution.py:322

commit v8 on v4

--- a/solution.py
+++ b/solution.py
@@ -190,8 +190,9 @@
         rest = jnp.dot(l_scr[p * half : (p + 1) * half, :], d_scr[...], preferred_element_type=F32)
         x_scr[:, p * size : (p + 1) * size] = (xp_ref[p * half : (p + 1) * half, :] + rest).astype(BF)
         xg_scr[:, p * TILE : (p + 1) * TILE] = x_scr[:, pl.ds(pl.multiple_of(p * size + cg * TILE, TILE), TILE)]
+    corner = jnp.dot(xg_scr[...], g_scr[...], preferred_element_type=F32)
     k_scr[...] = jnp.dot(x_scr[...], t_ref[...], preferred_element_type=F32)
-    k_scr[:, column(cg)] += jnp.dot(xg_scr[...], g_scr[...], preferred_element_type=F32)
+    k_scr[:, column(cg)] += corner
     for out, d in ((e1, 1 + k), (e2, 2 - k), (e3, 3)):
         out[...] = k_scr[pl.ds(pl.multiple_of((c ^ d) * BLK, BLK), BLK), :].astype(BF)
     keep_ref[...] = k_scr[pl.ds(pl.multiple_of(c * BLK, BLK), BLK), :]

time: 32.1 us -> 32.2 us (level)
  no operation moved by 1% of the time
where the time goes in v8:
time: 32.2 us; the launch traced here: 32.1 us
  waiting for transfers between devices  14.2 us (44%)
  starting transfers between devices  13 us (40%)
  Pallas kernels  4.16 us (13%)
  other arithmetic  0.65 us (2%)
    ppermute x4, waiting for transfers between devices, turn(): lax.ppermute(x, 'mu', [(i, i ^ (2 if (i % 2 == 0) == first else 4)) for i...  6.17 us
    ppermute x4, starting transfers between devices, turn(): lax.ppermute(x, 'mu', [(i, i ^ (2 if (i % 2 == 0) == first else 4)) for i...  5.54 us
    ppermute x3, starting transfers between devices, spread(): total = total + lax.ppermute(strip_of(to), 'aux', list(enumerate(step)))  4.44 us
    ppermute x6, waiting for transfers between devices, swap(): return lax.ppermute(x, 'mu', [(i, i ^ step) for i in range(2 * CHIPS)])  4.44 us
    ppermute x3, waiting for transfers between devices, spread(): total = total + lax.ppermute(strip_of(to), 'aux', list(enumerate(step)))  3.59 us
    ppermute x6, starting transfers between devices, swap(): return lax.ppermute(x, 'mu', [(i, i ^ step) for i in range(2 * CHIPS)])  2.97 us
    pallas_call x1, Pallas kernels, spread(): pl.pallas_call(early_kernel, out_shape=[jax.ShapeDtypeStruct((GROUP * siz...  1.41 us
    pallas_call x1, Pallas kernels, spread(): pl.pallas_call(late_kernel, out_shape=[chunk, chunk, chunk, jax.ShapeDtyp...  1.4 us
  transfers between devices with their start and end apart: 13, of which 8 were waited for; matrix products, arithmetic and copies ran while one was open for 0% of the time, Pallas kernels for 4%

profile of v8, /device:TPU:0, one launch (start us, length us, event | category | flops | bytes accessed | tf_op | source)
XLA Modules:
  0.0 32.1 jit_solution(1315426255757435219)
XLA Ops:
  0.0 1.3 %pack.1 = (bf16[5,64,512]{2,1,0:T(8,128)(2,1)S(1)}, bf16[13,64,128]{2,1,0:T(8,128)(2,1)S(1)}, bf16[13,64,128]{2,1,0:T(8,128)(2,1)S(1)}, bf16[7,64,128]{2,1,0:T(8,128)(2,1)S(1)}) custom-call(bf16[16,64,512]{2,1,0:T(8,128)(2,1)} %b_hbm.1, bf16[64,512]{1,0:T(8,128)(2,1)} %d_hbm.1, s32[8,8]{1,0:T(8,128)} %pair_hbm.1, s32[8,8]{1,0:T(8,128)} %dens_hbm.1), custom_call_target="tpu_custom_call" | custom-call | tf_op jit(solution)/shard_map/pack/pallas_call | solution.py:218
  1.4 3.0 %collective-permute-start.1 = (bf16[13,64,128]{2,1,0:T(8,128)(2,1)S(1)}, bf16[13,64,128]{2,1,0:T(8,128)(2,1)S(1)}, u32[]{:S(2)}, u32[]{:S(2)}) collective-permute-start(bf16[13,64,128]{2,1,0:T(8,128)(2,1)S(1)} %get-tuple-element.17), channel_id=1, source_target_pairs={{0,8},{4,20},{8,0},{12,28},{16,24},{20,4},{24,16},{28,12},{1,9},{5... | collective-permute-start | bytes 638984 | tf_op jit(solution)/shard_map/ppermute | solution.py:210
  4.4 1.5 %collective-permute-start.2 = (bf16[13,64,128]{2,1,0:T(8,128)(2,1)S(1)}, bf16[13,64,128]{2,1,0:T(8,128)(2,1)S(1)}, u32[]{:S(2)}, u32[]{:S(2)}) collective-permute-start(bf16[13,64,128]{2,1,0:T(8,128)(2,1)S(1)} %get-tuple-element.18), channel_id=1, source_target_pairs={{0,16},{4,12},{8,24},{12,4},{16,0},{20,28},{24,8},{28,20},{1,17},{... | collective-permute-start | bytes 638984 | tf_op jit(solution)/shard_map/ppermute | solution.py:210
  5.9 0.0 collective-permute-start
  5.9 0.0 collective-permute-start.5
  5.9 4.0 %collective-permute-done.1.r1 = bf16[13,64,128]{2,1,0:T(8,128)(2,1)S(1)} collective-permute-done((bf16[13,64,128]{2,1,0:T(8,128)(2,1)S(1)}, bf16[13,64,128]{2,1,0:T(8,128)(2,1)S(1)}, u32[]{:S(2)}, u32[]{:S(2)}) %collective-permute-start.1) | collective-permute-done | bytes 213024 | tf_op jit(solution)/shard_map/ppermute | solution.py:210
  9.9 0.0 collective-permute-start.3
  9.9 0.6 %collective-permute-done.2.r2 = bf16[13,64,128]{2,1,0:T(8,128)(2,1)S(1)} collective-permute-done((bf16[13,64,128]{2,1,0:T(8,128)(2,1)S(1)}, bf16[13,64,128]{2,1,0:T(8,128)(2,1)S(1)}, u32[]{:S(2)}, u32[]{:S(2)}) %collective-permute-start.2) | collective-permute-done | bytes 213024 | tf_op jit(solution)/shard_map/ppermute | solution.py:210
  10.5 0.4 %collective-permute-start.4 = (bf16[13,64,128]{2,1,0:T(8,128)(2,1)S(1)}, bf16[13,64,128]{2,1,0:T(8,128)(2,1)S(1)}, u32[]{:S(2)}, u32[]{:S(2)}) collective-permute-start(bf16[13,64,128]{2,1,0:T(8,128)(2,1)S(1)} %collective-permute-done.2.r2), channel_id=1, source_target_pairs={{0,4},{4,0},{8,12},{12,8},{16,20},{20,16},{24,28},{28,24},{1,5},{5... | collective-permute-start | bytes 638984 | tf_op jit(solution)/shard_map/ppermute | solution.py:207
  10.9 2.5 %collective-permute-done.5.r3 = bf16[7,64,128]{2,1,0:T(8,128)(2,1)S(1)} collective-permute-done((bf16[7,64,128]{2,1,0:T(8,128)(2,1)S(1)}, bf16[7,64,128]{2,1,0:T(8,128)(2,1)S(1)}, u32[]{:S(2)}, u32[]{:S(2)}) %collective-permute-start.5) | collective-permute-done | bytes 114720 | tf_op jit(solution)/shard_map/ppermute | solution.py:207
  13.4 0.0 collective-permute-start.6
  13.4 0.0 collective-permute-done.mate_ref
  13.4 0.0 collective-permute-done.3.q1
  13.4 0.0 collective-permute-done.4.q2
  13.4 1.4 %early.1 = (bf16[2048,512]{1,0:T(8,128)(2,1)S(1)}, bf16[1024,128]{1,0:T(8,128)(2,1)S(1)}, f32[1024,512]{1,0:T(8,128)S(1)}) custom-call(bf16[5,64,512]{2,1,0:T(8,128)(2,1)S(1)} %get-tuple-element.16.own_ref, bf16[5,64,512]{2,1,0:T(8,128)(2,1)S(1)} %collective-permute-done.mate_ref, bf16[13,64,128]{2,1,0:T(8,128)(2,1)S(1)} %collective-permute-done.1.r1, ...), custom_call_target="tpu_custom_call" | custom-call | tf_op jit(solution)/shard_map/early/pallas_call | solution.py:238
  14.8 0.0 collective-permute-done.6.q3
  14.8 1.4 %late.1 = (bf16[64,512]{1,0:T(8,128)(2,1)S(1)}, bf16[64,512]{1,0:T(8,128)(2,1)S(1)}, bf16[64,512]{1,0:T(8,128)(2,1)S(1)}, f32[64,512]{1,0:T(8,128)S(1)}) custom-call(bf16[2048,512]{1,0:T(8,128)(2,1)S(1)} %get-tuple-element.19.t_ref, bf16[1024,128]{1,0:T(8,128)(2,1)S(1)} %get-tuple-element.20.l_ref, f32[1024,512]{1,0:T(8,128)S(1)} %get-tuple-element.21.xp_ref, ...), custom_call_target="tpu_custom_call" | custom-call | tf_op jit(solution)/shard_map/late/pallas_call | solution.py:252
  16.2 2.5 %collective-permute-start.7 = (bf16[64,512]{1,0:T(8,128)(2,1)S(1)}, bf16[64,512]{1,0:T(8,128)(2,1)S(1)}, u32[]{:S(2)}, u32[]{:S(2)}) collective-permute-start(bf16[64,512]{1,0:T(8,128)(2,1)S(1)} %get-tuple-element.24), channel_id=1, source_target_pairs={{0,24},{4,28},{8,16},{12,20},{16,8},{20,12},{24,0},{28,4},{1,25},{... | collective-permute-start | bytes 196616 | tf_op jit(solution)/shard_map/ppermute | solution.py:207
  18.7 0.0 collective-permute-start.8
  18.7 1.0 %collective-permute-start.9 = (bf16[64,512]{1,0:T(8,128)(2,1)S(1)}, bf16[64,512]{1,0:T(8,128)(2,1)S(1)}, u32[]{:S(2)}, u32[]{:S(2)}) collective-permute-start(bf16[64,512]{1,0:T(8,128)(2,1)S(1)} %get-tuple-element.26), channel_id=1, source_target_pairs={{0,16},{4,12},{8,24},{12,4},{16,0},{20,28},{24,8},{28,20},{1,17},{... | collective-permute-start | bytes 196616 | tf_op jit(solution)/shard_map/ppermute | solution.py:210
  19.8 1.9 %collective-permute-done.7 = bf16[64,512]{1,0:T(8,128)(2,1)S(1)} collective-permute-done((bf16[64,512]{1,0:T(8,128)(2,1)S(1)}, bf16[64,512]{1,0:T(8,128)(2,1)S(1)}, u32[]{:S(2)}, u32[]{:S(2)}) %collective-permute-start.7) | collective-permute-done | bytes 65568 | tf_op jit(solution)/shard_map/ppermute | solution.py:207
  21.7 1.6 %collective-permute-done.8 = bf16[64,512]{1,0:T(8,128)(2,1)S(1)} collective-permute-done((bf16[64,512]{1,0:T(8,128)(2,1)S(1)}, bf16[64,512]{1,0:T(8,128)(2,1)S(1)}, u32[]{:S(2)}, u32[]{:S(2)}) %collective-permute-start.8) | collective-permute-done | bytes 65568 | tf_op jit(solution)/shard_map/ppermute | solution.py:210
  23.3 0.0 collective-permute-done.9
  23.4 2.9 %collective-permute-start.10 = (f32[16,512]{1,0:T(8,128)S(1)}, f32[16,512]{1,0:T(8,128)S(1)}, u32[]{:S(2)}, u32[]{:S(2)}) collective-permute-start(f32[16,512]{1,0:T(8,128)S(1)} %get-tuple-element.27), channel_id=1, source_target_pairs={{0,2},{1,3},{2,1},{3,0},{4,6},{5,7},{6,5},{7,4},{8,10},{9,11},{10,... | collective-permute-start | bytes 98312 | tf_op jit(solution)/shard_map/ppermute | solution.py:279
  26.3 1.1 %collective-permute-start.11 = (f32[16,512]{1,0:T(8,128)S(1)}, f32[16,512]{1,0:T(8,128)S(1)}, u32[]{:S(2)}, u32[]{:S(2)}) collective-permute-start(f32[16,512]{1,0:T(8,128)S(1)} %get-tuple-element.29), channel_id=1, source_target_pairs={{0,3},{1,2},{2,0},{3,1},{4,7},{5,6},{6,4},{7,5},{8,11},{9,10},{10,... | collective-permute-start | bytes 98312 | tf_op jit(solution)/shard_map/ppermute | solution.py:279
  27.3 0.5 %collective-permute-start.12 = (f32[16,512]{1,0:T(8,128)S(1)}, f32[16,512]{1,0:T(8,128)S(1)}, u32[]{:S(2)}, u32[]{:S(2)}) collective-permute-start(f32[16,512]{1,0:T(8,128)S(1)} %get-tuple-element.28), channel_id=1, source_target_pairs={{0,1},{1,0},{2,3},{3,2},{4,5},{5,4},{6,7},{7,6},{8,9},{9,8},{10,11... | collective-permute-start | bytes 98312 | tf_op jit(solution)/shard_map/ppermute | solution.py:279
  27.8 1.3 %collective-permute-done.10 = f32[16,512]{1,0:T(8,128)S(1)} collective-permute-done((f32[16,512]{1,0:T(8,128)S(1)}, f32[16,512]{1,0:T(8,128)S(1)}, u32[]{:S(2)}, u32[]{:S(2)}) %collective-permute-start.10) | collective-permute-done | bytes 32800 | tf_op jit(solution)/shard_map/ppermute | solution.py:279
  29.2 1.9 %collective-permute-done.11 = f32[16,512]{1,0:T(8,128)S(1)} collective-permute-done((f32[16,512]{1,0:T(8,128)S(1)}, f32[16,512]{1,0:T(8,128)S(1)}, u32[]{:S(2)}, u32[]{:S(2)}) %collective-permute-start.11) | collective-permute-done | bytes 32800 | tf_op jit(solution)/shard_map/ppermute | solution.py:279
  31.1 0.3 %collective-permute-done.12 = f32[16,512]{1,0:T(8,128)S(1)} collective-permute-done((f32[16,512]{1,0:T(8,128)S(1)}, f32[16,512]{1,0:T(8,128)S(1)}, u32[]{:S(2)}, u32[]{:S(2)}) %collective-permute-start.12) | collective-permute-done | bytes 32800 | tf_op jit(solution)/shard_map/ppermute | solution.py:279
  31.4 0.6 %add_add_fusion = f32[16,512]{1,0:T(8,128)} fusion(f32[16,512]{1,0:T(8,128)S(1)} %collective-permute-done.12, f32[16,512]{1,0:T(8,128)S(1)} %collective-permute-done.11, f32[16,512]{1,0:T(8,128)S(1)} %collective-permute-done.10, f32[64,512]{1,0:T(8,128)S(1)} %convert_add_fusion, s32[]{:T(128)S(6)} %select_n.43), kind=kLoop, calls=%fused_computation.1 | loop fusion | flops 24576 | bytes 163844 | tf_op jit(solution)/shard_map/add | solution.py:279
  (2 shorter events, 0.0 us)
Async XLA Ops:
  1.4 8.5 %collective-permute-start.1 = (bf16[13,64,128]{2,1,0:T(8,128)(2,1)S(1)}, bf16[13,64,128]{2,1,0:T(8,128)(2,1)S(1)}, u32[]{:S(2)}, u32[]{:S(2)}) collective-permute-start(bf16[13,64,128]{2,1,0:T(8,128)(2,1)S(1)} %get-tuple-element.17), channel_id=1, source_target_pairs={{0,8},{4,20},{8,0},{12,28},{16,24},{20,4},{24,16},{28,12},{1,9},{5... | collective-permute-start | bytes 638984 | tf_op jit(solution)/shard_map/ppermute | solution.py:210
  4.4 6.1 %collective-permute-start.2 = (bf16[13,64,128]{2,1,0:T(8,128)(2,1)S(1)}, bf16[13,64,128]{2,1,0:T(8,128)(2,1)S(1)}, u32[]{:S(2)}, u32[]{:S(2)}) collective-permute-start(bf16[13,64,128]{2,1,0:T(8,128)(2,1)S(1)} %get-tuple-element.18), channel_id=1, source_target_pairs={{0,16},{4,12},{8,24},{12,4},{16,0},{20,28},{24,8},{28,20},{1,17},{... | collective-permute-start | bytes 638984 | tf_op jit(solution)/shard_map/ppermute | solution.py:210
  5.9 7.5 %collective-permute-start = (bf16[5,64,512]{2,1,0:T(8,128)(2,1)S(1)}, bf16[5,64,512]{2,1,0:T(8,128)(2,1)S(1)}, u32[]{:S(2)}, u32[]{:S(2)}) collective-permute-start(bf16[5,64,512]{2,1,0:T(8,128)(2,1)S(1)} %get-tuple-element.16.own_ref), channel_id=1, source_target_pairs={{0,4},{4,0},{8,12},{12,8},{16,20},{20,16},{24,28},{28,24},{1,5},{5... | collective-permute-start | bytes 983048 | tf_op jit(solution)/shard_map/ppermute | solution.py:207
  5.9 7.5 %collective-permute-start.5 = (bf16[7,64,128]{2,1,0:T(8,128)(2,1)S(1)}, bf16[7,64,128]{2,1,0:T(8,128)(2,1)S(1)}, u32[]{:S(2)}, u32[]{:S(2)}) collective-permute-start(bf16[7,64,128]{2,1,0:T(8,128)(2,1)S(1)} %get-tuple-element.22), channel_id=1, source_target_pairs={{0,24},{4,28},{8,16},{12,20},{16,8},{20,12},{24,0},{28,4},{1,25},{... | collective-permute-start | bytes 344072 | tf_op jit(solution)/shard_map/ppermute | solution.py:207
  9.9 3.5 %collective-permute-start.3 = (bf16[13,64,128]{2,1,0:T(8,128)(2,1)S(1)}, bf16[13,64,128]{2,1,0:T(8,128)(2,1)S(1)}, u32[]{:S(2)}, u32[]{:S(2)}) collective-permute-start(bf16[13,64,128]{2,1,0:T(8,128)(2,1)S(1)} %collective-permute-done.1.r1), channel_id=1, source_target_pairs={{0,4},{4,0},{8,12},{12,8},{16,20},{20,16},{24,28},{28,24},{1,5},{5... | collective-permute-start | bytes 638984 | tf_op jit(solution)/shard_map/ppermute | solution.py:207
  10.5 2.9 %collective-permute-start.4 = (bf16[13,64,128]{2,1,0:T(8,128)(2,1)S(1)}, bf16[13,64,128]{2,1,0:T(8,128)(2,1)S(1)}, u32[]{:S(2)}, u32[]{:S(2)}) collective-permute-start(bf16[13,64,128]{2,1,0:T(8,128)(2,1)S(1)} %collective-permute-done.2.r2), channel_id=1, source_target_pairs={{0,4},{4,0},{8,12},{12,8},{16,20},{20,16},{24,28},{28,24},{1,5},{5... | collective-permute-start | bytes 638984 | tf_op jit(solution)/shard_map/ppermute | solution.py:207
  13.4 1.4 %collective-permute-start.6 = (bf16[7,64,128]{2,1,0:T(8,128)(2,1)S(1)}, bf16[7,64,128]{2,1,0:T(8,128)(2,1)S(1)}, u32[]{:S(2)}, u32[]{:S(2)}) collective-permute-start(bf16[7,64,128]{2,1,0:T(8,128)(2,1)S(1)} %collective-permute-done.5.r3), channel_id=1, source_target_pairs={{0,4},{4,0},{8,12},{12,8},{16,20},{20,16},{24,28},{28,24},{1,5},{5... | collective-permute-start | bytes 344072 | tf_op jit(solution)/shard_map/ppermute | solution.py:207
  16.2 5.5 %collective-permute-start.7 = (bf16[64,512]{1,0:T(8,128)(2,1)S(1)}, bf16[64,512]{1,0:T(8,128)(2,1)S(1)}, u32[]{:S(2)}, u32[]{:S(2)}) collective-permute-start(bf16[64,512]{1,0:T(8,128)(2,1)S(1)} %get-tuple-element.24), channel_id=1, source_target_pairs={{0,24},{4,28},{8,16},{12,20},{16,8},{20,12},{24,0},{28,4},{1,25},{... | collective-permute-start | bytes 196616 | tf_op jit(solution)/shard_map/ppermute | solution.py:207
  18.7 4.6 %collective-permute-start.8 = (bf16[64,512]{1,0:T(8,128)(2,1)S(1)}, bf16[64,512]{1,0:T(8,128)(2,1)S(1)}, u32[]{:S(2)}, u32[]{:S(2)}) collective-permute-start(bf16[64,512]{1,0:T(8,128)(2,1)S(1)} %get-tuple-element.25), channel_id=1, source_target_pairs={{0,8},{4,20},{8,0},{12,28},{16,24},{20,4},{24,16},{28,12},{1,9},{5... | collective-permute-start | bytes 196616 | tf_op jit(solution)/shard_map/ppermute | solution.py:210
  18.7 4.6 %collective-permute-start.9 = (bf16[64,512]{1,0:T(8,128)(2,1)S(1)}, bf16[64,512]{1,0:T(8,128)(2,1)S(1)}, u32[]{:S(2)}, u32[]{:S(2)}) collective-permute-start(bf16[64,512]{1,0:T(8,128)(2,1)S(1)} %get-tuple-element.26), channel_id=1, source_target_pairs={{0,16},{4,12},{8,24},{12,4},{16,0},{20,28},{24,8},{28,20},{1,17},{... | collective-permute-start | bytes 196616 | tf_op jit(solution)/shard_map/ppermute | solution.py:210
  23.4 5.8 %collective-permute-start.10 = (f32[16,512]{1,0:T(8,128)S(1)}, f32[16,512]{1,0:T(8,128)S(1)}, u32[]{:S(2)}, u32[]{:S(2)}) collective-permute-start(f32[16,512]{1,0:T(8,128)S(1)} %get-tuple-element.27), channel_id=1, source_target_pairs={{0,2},{1,3},{2,1},{3,0},{4,6},{5,7},{6,5},{7,4},{8,10},{9,11},{10,... | collective-permute-start | bytes 98312 | tf_op jit(solution)/shard_map/ppermute | solution.py:279
  26.3 4.8 %collective-permute-start.11 = (f32[16,512]{1,0:T(8,128)S(1)}, f32[16,512]{1,0:T(8,128)S(1)}, u32[]{:S(2)}, u32[]{:S(2)}) collective-permute-start(f32[16,512]{1,0:T(8,128)S(1)} %get-tuple-element.29), channel_id=1, source_target_pairs={{0,3},{1,2},{2,0},{3,1},{4,7},{5,6},{6,4},{7,5},{8,11},{9,10},{10,... | collective-permute-start | bytes 98312 | tf_op jit(solution)/shard_map/ppermute | solution.py:279
  27.3 4.1 %collective-permute-start.12 = (f32[16,512]{1,0:T(8,128)S(1)}, f32[16,512]{1,0:T(8,128)S(1)}, u32[]{:S(2)}, u32[]{:S(2)}) collective-permute-start(f32[16,512]{1,0:T(8,128)S(1)} %get-tuple-element.28), channel_id=1, source_target_pairs={{0,1},{1,0},{2,3},{3,2},{4,5},{5,4},{6,7},{7,6},{8,9},{9,8},{10,11... | collective-permute-start | bytes 98312 | tf_op jit(solution)/shard_map/ppermute | solution.py:279

commit v9 on v5

--- a/solution.py
+++ b/solution.py
@@ -11,7 +11,7 @@
 TILE = 2 * BLK
 CHIPS = 4
 GROUP = 4
-PLANE = ((1, 3, 0, 2), (3, 2, 1, 0), (2, 0, 3, 1))
+PLANE = ((3, 2, 1, 0), (1, 3, 0, 2), (2, 0, 3, 1))
 STEPS = ((2, 3, 1, 0), (3, 2, 0, 1), (1, 0, 3, 2))
 NEAR = 13
 FAR = 7

time: 32 us -> 32 us (level)
  transfers between devices with their start and end apart: 13 -> 13, of which waited for: 9 -> 8; matrix products, arithmetic and copies ran while one was open for 0% -> 0% of each run, Pallas kernels for 8% -> 8%
where the time goes in v9:
time: 32 us; the launch traced here: 31.8 us
  starting transfers between devices  14 us (44%)
  waiting for transfers between devices  12.2 us (38%)
  Pallas kernels  4.93 us (15%)
  other arithmetic  0.65 us (2%)
    ppermute x3, starting transfers between devices, spread(): total = total + lax.ppermute(strip_of(to), 'aux', list(enumerate(step)))  4.6 us
    ppermute x2, starting transfers between devices, turn(): lax.ppermute(x, 'mu', [(i, i ^ (2 if (i % 2 == 0) == first else 4)) for i...  4.52 us
    ppermute x3, starting transfers between devices, spread(): plane = plane + lax.ppermute(part, 'mu', pairs).astype(F32)  4.49 us
    ppermute x3, waiting for transfers between devices, spread(): total = total + lax.ppermute(strip_of(to), 'aux', list(enumerate(step)))  3.59 us
    ppermute x2, waiting for transfers between devices, turn(): lax.ppermute(x, 'mu', [(i, i ^ (2 if (i % 2 == 0) == first else 4)) for i...  3.14 us
    ppermute x5, waiting for transfers between devices, swap(): return lax.ppermute(x, 'mu', [(i, i ^ step) for i in range(2 * CHIPS)])  3.03 us
    ppermute x3, waiting for transfers between devices, spread(): plane = plane + lax.ppermute(part, 'mu', pairs).astype(F32)  2.39 us
    pallas_call x1, Pallas kernels, spread(): pl.pallas_call(early_kernel, out_shape=[jax.ShapeDtypeStruct((GROUP * siz...  1.41 us
  transfers between devices with their start and end apart: 13, of which 8 were waited for; matrix products, arithmetic and copies ran while one was open for 0% of the time, Pallas kernels for 8%

profile of v9, /device:TPU:0, one launch (start us, length us, event | category | flops | bytes accessed | tf_op | source)
XLA Modules:
  0.0 31.8 jit_solution(16611864233994783953)
XLA Ops:
  0.0 1.2 %pack.1 = (bf16[13,64,128]{2,1,0:T(8,128)(2,1)S(1)}, bf16[13,64,128]{2,1,0:T(8,128)(2,1)S(1)}, bf16[7,64,128]{2,1,0:T(8,128)(2,1)S(1)}, bf16[64,512]{1,0:T(8,128)(2,1)S(1)}, f32[4,1,128]{2,1,0:T(1,128)S(1)}) custom-call(bf16[16,64,512]{2,1,0:T(8,128)(2,1)} %b_hbm.3, bf16[64,512]{1,0:T(8,128)(2,1)} %d_hbm.1, s32[8,8]{1,0:T(8,128)} %pair_hbm.1, s32[8,8]{1,0:T(8,128)} %dens_hbm.1), custom_call_target="tpu_custom_call" | custom-call | tf_op jit(solution)/shard_map/pack/pallas_call | solution.py:227
  1.2 3.0 %collective-permute-start.1 = (bf16[13,64,128]{2,1,0:T(8,128)(2,1)S(1)}, bf16[13,64,128]{2,1,0:T(8,128)(2,1)S(1)}, u32[]{:S(2)}, u32[]{:S(2)}) collective-permute-start(bf16[13,64,128]{2,1,0:T(8,128)(2,1)S(1)} %get-tuple-element.19), channel_id=1, source_target_pairs={{0,8},{4,20},{8,0},{12,28},{16,24},{20,4},{24,16},{28,12},{1,9},{5... | collective-permute-start | bytes 638984 | tf_op jit(solution)/shard_map/ppermute | solution.py:216
  4.3 1.5 %collective-permute-start.2 = (bf16[13,64,128]{2,1,0:T(8,128)(2,1)S(1)}, bf16[13,64,128]{2,1,0:T(8,128)(2,1)S(1)}, u32[]{:S(2)}, u32[]{:S(2)}) collective-permute-start(bf16[13,64,128]{2,1,0:T(8,128)(2,1)S(1)} %get-tuple-element.20), channel_id=1, source_target_pairs={{0,16},{4,12},{8,24},{12,4},{16,0},{20,28},{24,8},{28,20},{1,17},{... | collective-permute-start | bytes 638984 | tf_op jit(solution)/shard_map/ppermute | solution.py:216
  5.8 1.0 %own.1.own_ref = bf16[5,64,512]{2,1,0:T(8,128)(2,1)S(1)} custom-call(bf16[16,64,512]{2,1,0:T(8,128)(2,1)} %b_hbm.3, bf16[64,512]{1,0:T(8,128)(2,1)S(1)} %get-tuple-element.17.mine_ref, f32[4,1,128]{2,1,0:T(1,128)S(1)} %get-tuple-element.18.line_ref), custom_call_target="tpu_custom_call" | custom-call | tf_op jit(solution)/shard_map/own/pallas_call | solution.py:248
  6.8 0.1 collective-permute-start
  6.9 0.1 collective-permute-start.5
  7.0 2.8 %collective-permute-done.1.r1 = bf16[13,64,128]{2,1,0:T(8,128)(2,1)S(1)} collective-permute-done((bf16[13,64,128]{2,1,0:T(8,128)(2,1)S(1)}, bf16[13,64,128]{2,1,0:T(8,128)(2,1)S(1)}, u32[]{:S(2)}, u32[]{:S(2)}) %collective-permute-start.1) | collective-permute-done | bytes 213024 | tf_op jit(solution)/shard_map/ppermute | solution.py:216
  9.8 0.0 collective-permute-start.3
  9.8 0.3 collective-permute-done.2.r2
  10.1 0.2 collective-permute-start.4
  10.3 3.0 %collective-permute-done.5.r3 = bf16[7,64,128]{2,1,0:T(8,128)(2,1)S(1)} collective-permute-done((bf16[7,64,128]{2,1,0:T(8,128)(2,1)S(1)}, bf16[7,64,128]{2,1,0:T(8,128)(2,1)S(1)}, u32[]{:S(2)}, u32[]{:S(2)}) %collective-permute-start.5) | collective-permute-done | bytes 114720 | tf_op jit(solution)/shard_map/ppermute | solution.py:213
  13.3 0.0 collective-permute-start.6
  13.3 0.0 collective-permute-done.mate_ref
  13.3 0.0 collective-permute-done.3.q1
  13.3 0.0 collective-permute-done.4.q2
  13.4 1.4 %early.1 = (bf16[2048,512]{1,0:T(8,128)(2,1)S(1)}, bf16[1024,128]{1,0:T(8,128)(2,1)S(1)}, f32[1024,512]{1,0:T(8,128)S(1)}) custom-call(bf16[5,64,512]{2,1,0:T(8,128)(2,1)S(1)} %own.1.own_ref, bf16[5,64,512]{2,1,0:T(8,128)(2,1)S(1)} %collective-permute-done.mate_ref, bf16[13,64,128]{2,1,0:T(8,128)(2,1)S(1)} %collective-permute-done.1.r1, ...), custom_call_target="tpu_custom_call" | custom-call | tf_op jit(solution)/shard_map/early/pallas_call | solution.py:261
  14.8 0.0 collective-permute-done.6.q3
  14.8 1.3 %late.1 = (bf16[64,512]{1,0:T(8,128)(2,1)S(1)}, bf16[64,512]{1,0:T(8,128)(2,1)S(1)}, bf16[64,512]{1,0:T(8,128)(2,1)S(1)}, f32[64,512]{1,0:T(8,128)S(1)}) custom-call(bf16[2048,512]{1,0:T(8,128)(2,1)S(1)} %get-tuple-element.21.t_ref, bf16[1024,128]{1,0:T(8,128)(2,1)S(1)} %get-tuple-element.22.l_ref, f32[1024,512]{1,0:T(8,128)S(1)} %get-tuple-element.23.xp_ref, ...), custom_call_target="tpu_custom_call" | custom-call | tf_op jit(solution)/shard_map/late/pallas_call | solution.py:275
  16.1 2.5 %collective-permute-start.7 = (bf16[64,512]{1,0:T(8,128)(2,1)S(1)}, bf16[64,512]{1,0:T(8,128)(2,1)S(1)}, u32[]{:S(2)}, u32[]{:S(2)}) collective-permute-start(bf16[64,512]{1,0:T(8,128)(2,1)S(1)} %get-tuple-element.26), channel_id=1, source_target_pairs={{0,24},{4,28},{8,16},{12,20},{16,8},{20,12},{24,0},{28,4},{1,25},{... | collective-permute-start | bytes 196616 | tf_op jit(solution)/shard_map/ppermute | solution.py:294
  18.5 0.0 collective-permute-start.8
  18.5 2.0 %collective-permute-start.9 = (bf16[64,512]{1,0:T(8,128)(2,1)S(1)}, bf16[64,512]{1,0:T(8,128)(2,1)S(1)}, u32[]{:S(2)}, u32[]{:S(2)}) collective-permute-start(bf16[64,512]{1,0:T(8,128)(2,1)S(1)} %get-tuple-element.28), channel_id=1, source_target_pairs={{0,16},{4,20},{8,0},{12,4},{16,24},{20,28},{24,8},{28,12},{1,17},{... | collective-permute-start | bytes 196616 | tf_op jit(solution)/shard_map/ppermute | solution.py:294
  20.5 1.1 %collective-permute-done.7 = bf16[64,512]{1,0:T(8,128)(2,1)S(1)} collective-permute-done((bf16[64,512]{1,0:T(8,128)(2,1)S(1)}, bf16[64,512]{1,0:T(8,128)(2,1)S(1)}, u32[]{:S(2)}, u32[]{:S(2)}) %collective-permute-start.7) | collective-permute-done | bytes 65568 | tf_op jit(solution)/shard_map/ppermute | solution.py:294
  21.7 1.2 %collective-permute-done.8 = bf16[64,512]{1,0:T(8,128)(2,1)S(1)} collective-permute-done((bf16[64,512]{1,0:T(8,128)(2,1)S(1)}, bf16[64,512]{1,0:T(8,128)(2,1)S(1)}, u32[]{:S(2)}, u32[]{:S(2)}) %collective-permute-start.8) | collective-permute-done | bytes 65568 | tf_op jit(solution)/shard_map/ppermute | solution.py:294
  22.9 0.0 collective-permute-done.9
  23.0 3.0 %collective-permute-start.10 = (f32[16,512]{1,0:T(8,128)S(1)}, f32[16,512]{1,0:T(8,128)S(1)}, u32[]{:S(2)}, u32[]{:S(2)}) collective-permute-start(f32[16,512]{1,0:T(8,128)S(1)} %get-tuple-element.29), channel_id=1, source_target_pairs={{0,2},{1,3},{2,1},{3,0},{4,6},{5,7},{6,5},{7,4},{8,10},{9,11},{10,... | collective-permute-start | bytes 98312 | tf_op jit(solution)/shard_map/ppermute | solution.py:304
  26.0 1.1 %collective-permute-start.11 = (f32[16,512]{1,0:T(8,128)S(1)}, f32[16,512]{1,0:T(8,128)S(1)}, u32[]{:S(2)}, u32[]{:S(2)}) collective-permute-start(f32[16,512]{1,0:T(8,128)S(1)} %get-tuple-element.31), channel_id=1, source_target_pairs={{0,3},{1,2},{2,0},{3,1},{4,7},{5,6},{6,4},{7,5},{8,11},{9,10},{10,... | collective-permute-start | bytes 98312 | tf_op jit(solution)/shard_map/ppermute | solution.py:304
  27.1 0.5 %collective-permute-start.12 = (f32[16,512]{1,0:T(8,128)S(1)}, f32[16,512]{1,0:T(8,128)S(1)}, u32[]{:S(2)}, u32[]{:S(2)}) collective-permute-start(f32[16,512]{1,0:T(8,128)S(1)} %get-tuple-element.30), channel_id=1, source_target_pairs={{0,1},{1,0},{2,3},{3,2},{4,5},{5,4},{6,7},{7,6},{8,9},{9,8},{10,11... | collective-permute-start | bytes 98312 | tf_op jit(solution)/shard_map/ppermute | solution.py:304
  27.6 1.5 %collective-permute-done.10 = f32[16,512]{1,0:T(8,128)S(1)} collective-permute-done((f32[16,512]{1,0:T(8,128)S(1)}, f32[16,512]{1,0:T(8,128)S(1)}, u32[]{:S(2)}, u32[]{:S(2)}) %collective-permute-start.10) | collective-permute-done | bytes 32800 | tf_op jit(solution)/shard_map/ppermute | solution.py:304
  29.1 1.8 %collective-permute-done.11 = f32[16,512]{1,0:T(8,128)S(1)} collective-permute-done((f32[16,512]{1,0:T(8,128)S(1)}, f32[16,512]{1,0:T(8,128)S(1)}, u32[]{:S(2)}, u32[]{:S(2)}) %collective-permute-start.11) | collective-permute-done | bytes 32800 | tf_op jit(solution)/shard_map/ppermute | solution.py:304
  30.9 0.3 %collective-permute-done.12 = f32[16,512]{1,0:T(8,128)S(1)} collective-permute-done((f32[16,512]{1,0:T(8,128)S(1)}, f32[16,512]{1,0:T(8,128)S(1)}, u32[]{:S(2)}, u32[]{:S(2)}) %collective-permute-start.12) | collective-permute-done | bytes 32800 | tf_op jit(solution)/shard_map/ppermute | solution.py:304
  31.2 0.6 %add_add_fusion = f32[16,512]{1,0:T(8,128)} fusion(f32[16,512]{1,0:T(8,128)S(1)} %collective-permute-done.12, f32[16,512]{1,0:T(8,128)S(1)} %collective-permute-done.11, f32[16,512]{1,0:T(8,128)S(1)} %collective-permute-done.10, f32[64,512]{1,0:T(8,128)S(1)} %convert_add_fusion, s32[]{:T(128)S(6)} %select_n.43), kind=kLoop, calls=%fused_computation.1 | loop fusion | flops 24576 | bytes 163844 | tf_op jit(solution)/shard_map/add | solution.py:304
  (2 shorter events, 0.0 us)
Async XLA Ops:
  1.2 8.5 %collective-permute-start.1 = (bf16[13,64,128]{2,1,0:T(8,128)(2,1)S(1)}, bf16[13,64,128]{2,1,0:T(8,128)(2,1)S(1)}, u32[]{:S(2)}, u32[]{:S(2)}) collective-permute-start(bf16[13,64,128]{2,1,0:T(8,128)(2,1)S(1)} %get-tuple-element.19), channel_id=1, source_target_pairs={{0,8},{4,20},{8,0},{12,28},{16,24},{20,4},{24,16},{28,12},{1,9},{5... | collective-permute-start | bytes 638984 | tf_op jit(solution)/shard_map/ppermute | solution.py:216
  4.3 5.8 %collective-permute-start.2 = (bf16[13,64,128]{2,1,0:T(8,128)(2,1)S(1)}, bf16[13,64,128]{2,1,0:T(8,128)(2,1)S(1)}, u32[]{:S(2)}, u32[]{:S(2)}) collective-permute-start(bf16[13,64,128]{2,1,0:T(8,128)(2,1)S(1)} %get-tuple-element.20), channel_id=1, source_target_pairs={{0,16},{4,12},{8,24},{12,4},{16,0},{20,28},{24,8},{28,20},{1,17},{... | collective-permute-start | bytes 638984 | tf_op jit(solution)/shard_map/ppermute | solution.py:216
  6.8 6.5 %collective-permute-start = (bf16[5,64,512]{2,1,0:T(8,128)(2,1)S(1)}, bf16[5,64,512]{2,1,0:T(8,128)(2,1)S(1)}, u32[]{:S(2)}, u32[]{:S(2)}) collective-permute-start(bf16[5,64,512]{2,1,0:T(8,128)(2,1)S(1)} %own.1.own_ref), channel_id=1, source_target_pairs={{0,4},{4,0},{8,12},{12,8},{16,20},{20,16},{24,28},{28,24},{1,5},{5... | collective-permute-start | bytes 983048 | tf_op jit(solution)/shard_map/ppermute | solution.py:213
  6.9 6.5 %collective-permute-start.5 = (bf16[7,64,128]{2,1,0:T(8,128)(2,1)S(1)}, bf16[7,64,128]{2,1,0:T(8,128)(2,1)S(1)}, u32[]{:S(2)}, u32[]{:S(2)}) collective-permute-start(bf16[7,64,128]{2,1,0:T(8,128)(2,1)S(1)} %get-tuple-element.24), channel_id=1, source_target_pairs={{0,24},{4,28},{8,16},{12,20},{16,8},{20,12},{24,0},{28,4},{1,25},{... | collective-permute-start | bytes 344072 | tf_op jit(solution)/shard_map/ppermute | solution.py:213
  9.8 3.5 %collective-permute-start.3 = (bf16[13,64,128]{2,1,0:T(8,128)(2,1)S(1)}, bf16[13,64,128]{2,1,0:T(8,128)(2,1)S(1)}, u32[]{:S(2)}, u32[]{:S(2)}) collective-permute-start(bf16[13,64,128]{2,1,0:T(8,128)(2,1)S(1)} %collective-permute-done.1.r1), channel_id=1, source_target_pairs={{0,4},{4,0},{8,12},{12,8},{16,20},{20,16},{24,28},{28,24},{1,5},{5... | collective-permute-start | bytes 638984 | tf_op jit(solution)/shard_map/ppermute | solution.py:213
  10.1 3.2 %collective-permute-start.4 = (bf16[13,64,128]{2,1,0:T(8,128)(2,1)S(1)}, bf16[13,64,128]{2,1,0:T(8,128)(2,1)S(1)}, u32[]{:S(2)}, u32[]{:S(2)}) collective-permute-start(bf16[13,64,128]{2,1,0:T(8,128)(2,1)S(1)} %collective-permute-done.2.r2), channel_id=1, source_target_pairs={{0,4},{4,0},{8,12},{12,8},{16,20},{20,16},{24,28},{28,24},{1,5},{5... | collective-permute-start | bytes 638984 | tf_op jit(solution)/shard_map/ppermute | solution.py:213
  13.3 1.4 %collective-permute-start.6 = (bf16[7,64,128]{2,1,0:T(8,128)(2,1)S(1)}, bf16[7,64,128]{2,1,0:T(8,128)(2,1)S(1)}, u32[]{:S(2)}, u32[]{:S(2)}) collective-permute-start(bf16[7,64,128]{2,1,0:T(8,128)(2,1)S(1)} %collective-permute-done.5.r3), channel_id=1, source_target_pairs={{0,4},{4,0},{8,12},{12,8},{16,20},{20,16},{24,28},{28,24},{1,5},{5... | collective-permute-start | bytes 344072 | tf_op jit(solution)/shard_map/ppermute | solution.py:213
  16.1 5.6 %collective-permute-start.7 = (bf16[64,512]{1,0:T(8,128)(2,1)S(1)}, bf16[64,512]{1,0:T(8,128)(2,1)S(1)}, u32[]{:S(2)}, u32[]{:S(2)}) collective-permute-start(bf16[64,512]{1,0:T(8,128)(2,1)S(1)} %get-tuple-element.26), channel_id=1, source_target_pairs={{0,24},{4,28},{8,16},{12,20},{16,8},{20,12},{24,0},{28,4},{1,25},{... | collective-permute-start | bytes 196616 | tf_op jit(solution)/shard_map/ppermute | solution.py:294
  18.5 4.4 %collective-permute-start.8 = (bf16[64,512]{1,0:T(8,128)(2,1)S(1)}, bf16[64,512]{1,0:T(8,128)(2,1)S(1)}, u32[]{:S(2)}, u32[]{:S(2)}) collective-permute-start(bf16[64,512]{1,0:T(8,128)(2,1)S(1)} %get-tuple-element.27), channel_id=1, source_target_pairs={{0,8},{4,12},{8,24},{12,28},{16,0},{20,4},{24,16},{28,20},{1,9},{5... | collective-permute-start | bytes 196616 | tf_op jit(solution)/shard_map/ppermute | solution.py:294
  18.5 4.4 %collective-permute-start.9 = (bf16[64,512]{1,0:T(8,128)(2,1)S(1)}, bf16[64,512]{1,0:T(8,128)(2,1)S(1)}, u32[]{:S(2)}, u32[]{:S(2)}) collective-permute-start(bf16[64,512]{1,0:T(8,128)(2,1)S(1)} %get-tuple-element.28), channel_id=1, source_target_pairs={{0,16},{4,20},{8,0},{12,4},{16,24},{20,28},{24,8},{28,12},{1,17},{... | collective-permute-start | bytes 196616 | tf_op jit(solution)/shard_map/ppermute | solution.py:294
  23.0 6.1 %collective-permute-start.10 = (f32[16,512]{1,0:T(8,128)S(1)}, f32[16,512]{1,0:T(8,128)S(1)}, u32[]{:S(2)}, u32[]{:S(2)}) collective-permute-start(f32[16,512]{1,0:T(8,128)S(1)} %get-tuple-element.29), channel_id=1, source_target_pairs={{0,2},{1,3},{2,1},{3,0},{4,6},{5,7},{6,5},{7,4},{8,10},{9,11},{10,... | collective-permute-start | bytes 98312 | tf_op jit(solution)/shard_map/ppermute | solution.py:304
  26.0 4.8 %collective-permute-start.11 = (f32[16,512]{1,0:T(8,128)S(1)}, f32[16,512]{1,0:T(8,128)S(1)}, u32[]{:S(2)}, u32[]{:S(2)}) collective-permute-start(f32[16,512]{1,0:T(8,128)S(1)} %get-tuple-element.31), channel_id=1, source_target_pairs={{0,3},{1,2},{2,0},{3,1},{4,7},{5,6},{6,4},{7,5},{8,11},{9,10},{10,... | collective-permute-start | bytes 98312 | tf_op jit(solution)/shard_map/ppermute | solution.py:304
  27.1 4.1 %collective-permute-start.12 = (f32[16,512]{1,0:T(8,128)S(1)}, f32[16,512]{1,0:T(8,128)S(1)}, u32[]{:S(2)}, u32[]{:S(2)}) collective-permute-start(f32[16,512]{1,0:T(8,128)S(1)} %get-tuple-element.30), channel_id=1, source_target_pairs={{0,1},{1,0},{2,3},{3,2},{4,5},{5,4},{6,7},{7,6},{8,9},{9,8},{10,11... | collective-permute-start | bytes 98312 | tf_op jit(solution)/shard_map/ppermute | solution.py:304
